TPU v7x, 32 devices: a whole 2x2x4 slice. The times are simulated.
32 devices in a mesh: fsdp: 2 (over x), ctx: 4 (over y, core), tp: 4 (over z).
Axes of the slice: x: 2, y: 2, z: 4, core: 2. Of those that a mesh axis runs over, the one named last changes fastest.
Arguments:
- block_in: bfloat16 [4, 2048, 2048], P('fsdp', 'ctx'), may hold values from -6 to 6
- segments: int32 [4, 2048], P('fsdp'), may hold values from 0 to 16, as said below
- out_grad: bfloat16 [4, 2048, 2048], P('fsdp', 'ctx'), may hold values from -6 to 6
- ln1_gain: bfloat16 [2048], replicated, may hold values from 0.5 to 1.5
- ln1_bias: bfloat16 [2048], replicated, may hold values from -3 to 3
- w_qkv: bfloat16 [2048, 3, 2048], P('fsdp', None, 'tp'), may hold values from -0.125 to 0.125
- b_qv: bfloat16 [2, 2048], P(None, 'tp'), may hold values from -2 to 2
- w_attn_out: bfloat16 [2048, 2048], P('tp', 'fsdp'), may hold values from -0.375 to 0.375
- b_attn_out: bfloat16 [2048], replicated, may hold values from -2 to 2
- ln2_gain: bfloat16 [2048], replicated, may hold values from 0.5 to 1.5
- ln2_bias: bfloat16 [2048], replicated, may hold values from -3 to 3
- w_up: bfloat16 [2048, 8192], P('fsdp', 'tp'), may hold values from -0.125 to 0.125
- b_up: bfloat16 [8192], P('tp'), may hold values from -3 to 3
- w_down: bfloat16 [8192, 2048], P('tp', 'fsdp'), may hold values from -0.0625 to 0.0625
- b_down: bfloat16 [2048], replicated, may hold values from -2 to 2
Outputs:
- block_out: bfloat16 [4, 2048, 2048], P('fsdp', 'ctx')
- in_grad: bfloat16 [4, 2048, 2048], P('fsdp', 'ctx')
- grad_ln1_gain: float32 [2048], replicated
- grad_ln1_bias: float32 [2048], replicated
- grad_w_qkv: float32 [2048, 3, 2048], P('fsdp', None, 'tp')
- grad_b_qv: float32 [2, 2048], P(None, 'tp')
- grad_w_attn_out: float32 [2048, 2048], P('tp', 'fsdp')
- grad_b_attn_out: float32 [2048], replicated
- grad_ln2_gain: float32 [2048], replicated
- grad_ln2_bias: float32 [2048], replicated
- grad_w_up: float32 [2048, 8192], P('fsdp', 'tp')
- grad_b_up: float32 [8192], P('tp')
- grad_w_down: float32 [8192, 2048], P('tp', 'fsdp')
- grad_b_down: float32 [2048], replicated
Inputs may be any that keep to these rules, and one draw needn't show every extreme that they name: `segments`: along each sequence the document number starts at 1 and rises by one at each document's end; 0 marks padding, which only follows the documents at the end of a sequence.
All inputs are finite; a program needn't handle non-finite values.
Results may differ from a plain program's by a relative error of at most 0.011.
Values may be sent and summed in bfloat16 or wider, within the bound.
No kernel may reach another device: no remote copies, remote signals or barrier semaphores. Data moves between devices by JAX's collectives and lax.ppermute only.
A program may use at most 320 MiB of HBM per device.

v0:
```python
import jax
import jax.numpy as jnp
from jax import lax
from jax.sharding import PartitionSpec as P

FF = 8192
HD = 128


NORM_EPS = 1e-05
MASKED = -1e30


def norm_parts(values):
    centred = values - jnp.mean(values, axis=-1, keepdims=True)
    norm_scale = lax.rsqrt(jnp.mean(centred * centred, axis=-1, keepdims=True) + NORM_EPS)
    return (centred * norm_scale, norm_scale)


def norm_back(grad_norm, gain, normed, norm_scale):
    lifted = grad_norm * gain
    return norm_scale * (
        lifted
        - jnp.mean(lifted, axis=-1, keepdims=True)
        - normed * jnp.mean(lifted * normed, axis=-1, keepdims=True)
    )


def gelu_tanh(values):
    return jax.nn.gelu(values, approximate=True)


def take_rows(values, row_start, row_count):
    return lax.dynamic_slice_in_dim(values, row_start, row_count, 0)


def slice_share(values):
    row_count = values.shape[0] // lax.axis_size("tp")
    return take_rows(values, lax.axis_index("tp") * row_count, row_count)


def tensor_rows(partial_value, finish):
    row_count = partial_value.shape[0] // lax.axis_size("tp")
    shared = lax.psum_scatter(partial_value, "tp", scatter_dimension=0, tiled=True)
    wide_rows, kept_rows = finish(shared, lax.axis_index("tp") * row_count, row_count)
    return (lax.all_gather(wide_rows, "tp", axis=0, tiled=True), kept_rows)


def scores_of(queries, keys_all, allowed):
    raw_scores = jnp.einsum(
        "sqhe,skhe->shqk", queries, keys_all, preferred_element_type=jnp.float32
    ) * HD ** (-0.5)
    return jnp.where(allowed[:, None], raw_scores, MASKED)


def local(
    block_in,
    segments,
    out_grad,
    ln1_gain,
    ln1_bias,
    w_qkv,
    b_qv,
    w_attn_out,
    b_attn_out,
    ln2_gain,
    ln2_bias,
    w_up,
    b_up,
    w_down,
    b_down,
):
    seq_here, span, width = block_in.shape
    rows = seq_here * span
    start_pos = lax.axis_index("ctx") * span
    qkv_full, up_full = (
        lax.all_gather(w_qkv, "fsdp", axis=0, tiled=True),
        lax.all_gather(w_up, "fsdp", axis=0, tiled=True),
    )
    attn_full, down_full = (
        lax.all_gather(w_attn_out, "fsdp", axis=1, tiled=True),
        lax.all_gather(w_down, "fsdp", axis=1, tiled=True),
    )
    local_width = qkv_full.shape[2]
    local_units = up_full.shape[1]
    heads_here = local_width // HD
    gain_one = ln1_gain.astype(jnp.float32)
    shift_one = ln1_bias.astype(jnp.float32)
    gain_two = ln2_gain.astype(jnp.float32)
    shift_two = ln2_bias.astype(jnp.float32)
    bias_qv = b_qv.astype(jnp.float32)
    bias_out = b_attn_out.astype(jnp.float32)
    bias_down = b_down.astype(jnp.float32)
    query_seg = lax.dynamic_slice_in_dim(segments, start_pos, span, 1)
    key_pos = jnp.arange(segments.shape[1])
    query_pos = start_pos + jnp.arange(span)
    allowed = (query_seg[:, :, None] == segments[:, None, :]) & (
        key_pos[None, None, :] <= query_pos[None, :, None]
    )
    valid_rows = (query_seg != 0).reshape(rows, 1).astype(jnp.float32)
    block_rows = block_in.reshape(rows, width).astype(jnp.float32)
    normed_one, scale_one = norm_parts(block_rows)
    input_one = (normed_one * gain_one + shift_one).astype(jnp.bfloat16)
    projected = jnp.einsum("rd,dcf->rcf", input_one, qkv_full, preferred_element_type=jnp.float32)
    heads_shape = (seq_here, span, heads_here, HD)
    queries = (projected[:, 0] + bias_qv[0]).astype(jnp.bfloat16).reshape(heads_shape)
    keys_here = projected[:, 1].astype(jnp.bfloat16).reshape(heads_shape)
    values_here = (projected[:, 2] + bias_qv[1]).astype(jnp.bfloat16).reshape(heads_shape)
    keys_all, values_all = (
        lax.all_gather(keys_here, "ctx", axis=1, tiled=True),
        lax.all_gather(values_here, "ctx", axis=1, tiled=True),
    )
    scores = scores_of(queries, keys_all, allowed)
    row_max = jnp.max(scores, axis=-1, keepdims=True)
    exp_scores = jnp.exp(scores - row_max)
    row_total = jnp.sum(exp_scores, axis=-1, keepdims=True)
    weights = (exp_scores / row_total).astype(jnp.bfloat16)
    log_total = row_max + jnp.log(row_total)
    attended = jnp.einsum(
        "shqk,skhe->sqhe", weights, values_all, preferred_element_type=jnp.float32
    )
    attended = attended.astype(jnp.bfloat16).reshape(rows, local_width)
    attn_part = jnp.dot(attended, attn_full, preferred_element_type=jnp.float32)

    def after_attention(summed, row_start, row_count):
        mid_rows = take_rows(block_rows, row_start, row_count) + summed + bias_out
        normed, norm_scale = norm_parts(mid_rows)
        return ((normed * gain_two + shift_two).astype(jnp.bfloat16), mid_rows)

    input_two, middle = tensor_rows(attn_part, after_attention)
    hidden_pre = jnp.dot(input_two, up_full, preferred_element_type=jnp.float32) + b_up.astype(
        jnp.float32
    )
    active, gelu_pull = jax.vjp(gelu_tanh, hidden_pre)
    active = active.astype(jnp.bfloat16)
    down_part = jnp.dot(active, down_full, preferred_element_type=jnp.float32)

    def after_feed(summed, row_start, row_count):
        return ((middle + summed + bias_down).astype(jnp.bfloat16), None)

    out_rows, unused = tensor_rows(down_part, after_feed)
    cotan = out_grad.reshape(rows, width).astype(jnp.float32) * valid_rows
    cotan_low = cotan.astype(jnp.bfloat16)
    grad_active = jnp.einsum("rd,fd->rf", cotan_low, down_full, preferred_element_type=jnp.float32)
    grad_hidden = gelu_pull(grad_active)[0].astype(jnp.bfloat16)
    grad_down = jnp.einsum("rf,rd->fd", active, cotan_low, preferred_element_type=jnp.float32)
    grad_up = jnp.einsum("rd,rf->df", input_two, grad_hidden, preferred_element_type=jnp.float32)
    part_two = jnp.einsum("rf,df->rd", grad_hidden, up_full, preferred_element_type=jnp.float32)

    def before_feed(summed, row_start, row_count):
        normed, norm_scale = norm_parts(middle)
        grad_mid = take_rows(cotan, row_start, row_count) + norm_back(
            summed, gain_two, normed, norm_scale
        )
        return (grad_mid.astype(jnp.bfloat16), (grad_mid, summed, normed))

    grad_mid_low, kept_two = tensor_rows(part_two, before_feed)
    grad_attn_w = jnp.einsum(
        "rf,rd->fd", attended, grad_mid_low, preferred_element_type=jnp.float32
    )
    grad_att = jnp.einsum("rd,fd->rf", grad_mid_low, attn_full, preferred_element_type=jnp.float32)
    grad_att = grad_att.astype(jnp.bfloat16).reshape(heads_shape)
    scores = scores_of(queries, keys_all, allowed)
    probs = jnp.exp(scores - log_total)
    probs_low = probs.astype(jnp.bfloat16)
    grad_values = jnp.einsum(
        "shqk,sqhe->skhe", probs_low, grad_att, preferred_element_type=jnp.float32
    )
    grad_probs = jnp.einsum(
        "sqhe,skhe->shqk", grad_att, values_all, preferred_element_type=jnp.float32
    )
    grad_scores = (
        probs * (grad_probs - jnp.sum(probs * grad_probs, axis=-1, keepdims=True))
    ).astype(jnp.bfloat16)
    factor = HD ** (-0.5)
    grad_queries = (
        jnp.einsum("shqk,skhe->sqhe", grad_scores, keys_all, preferred_element_type=jnp.float32)
        * factor
    ).astype(jnp.bfloat16)
    grad_keys = (
        jnp.einsum("shqk,sqhe->skhe", grad_scores, queries, preferred_element_type=jnp.float32)
        * factor
    )
    key_total, value_total = (
        lax.psum_scatter(grad_keys, "ctx", scatter_dimension=1, tiled=True),
        lax.psum_scatter(grad_values, "ctx", scatter_dimension=1, tiled=True),
    )
    grad_proj = jnp.stack(
        [
            grad_queries.reshape(rows, local_width),
            key_total.astype(jnp.bfloat16).reshape(rows, local_width),
            value_total.astype(jnp.bfloat16).reshape(rows, local_width),
        ],
        axis=1,
    )
    grad_qkv = jnp.einsum("rd,rcf->dcf", input_one, grad_proj, preferred_element_type=jnp.float32)
    part_one = jnp.einsum("rcf,dcf->rd", grad_proj, qkv_full, preferred_element_type=jnp.float32)

    def before_attention(summed, row_start, row_count):
        normed, norm_scale = norm_parts(take_rows(block_rows, row_start, row_count))
        grad_input = kept_two[0] + norm_back(summed, gain_one, normed, norm_scale)
        return (grad_input.astype(jnp.bfloat16), (summed, normed))

    grad_in_rows, kept_one = tensor_rows(part_one, before_attention)
    grad_qkv_s, grad_up_s = (
        lax.psum_scatter(grad_qkv, "fsdp", scatter_dimension=0, tiled=True),
        lax.psum_scatter(grad_up, "fsdp", scatter_dimension=0, tiled=True),
    )
    grad_attn_s, grad_down_s = (
        lax.psum_scatter(grad_attn_w, "fsdp", scatter_dimension=1, tiled=True),
        lax.psum_scatter(grad_down, "fsdp", scatter_dimension=1, tiled=True),
    )
    grad_qkv_s, grad_up_s, grad_attn_s, grad_down_s = lax.psum(
        (grad_qkv_s, grad_up_s, grad_attn_s, grad_down_s), "ctx"
    )
    tp_slot = lax.axis_index("tp")
    proj_sums = jnp.sum(grad_proj.astype(jnp.float32), axis=0)
    qv_sums = jnp.stack([proj_sums[0], proj_sums[2]])
    qv_placed = lax.dynamic_update_slice_in_dim(
        jnp.zeros((2, width), jnp.float32), qv_sums, tp_slot * local_width, 1
    )
    up_sums = jnp.sum(grad_hidden.astype(jnp.float32), axis=0)
    up_placed = lax.dynamic_update_slice_in_dim(
        jnp.zeros((FF,), jnp.float32), up_sums, tp_slot * local_units, 0
    )
    norm_grad_two = kept_two[1]
    normed_two = kept_two[2]
    mid_share = kept_two[0].astype(jnp.bfloat16).astype(jnp.float32)
    norm_grad_one = kept_one[0]
    normed_share = kept_one[1]
    stats = lax.psum(
        (
            jnp.sum(norm_grad_one * normed_share, axis=0),
            jnp.sum(norm_grad_one, axis=0),
            qv_placed,
            jnp.sum(mid_share, axis=0),
            jnp.sum(norm_grad_two * normed_two, axis=0),
            jnp.sum(norm_grad_two, axis=0),
            up_placed,
            jnp.sum(slice_share(cotan), axis=0),
        ),
        ("fsdp", "ctx", "tp"),
    )
    grad_bqv = lax.dynamic_slice_in_dim(stats[2], tp_slot * local_width, local_width, 1)
    grad_bup = lax.dynamic_slice_in_dim(stats[6], tp_slot * local_units, local_units, 0)
    return (
        out_rows.reshape(seq_here, span, width),
        grad_in_rows.reshape(seq_here, span, width),
        stats[0],
        stats[1],
        grad_qkv_s,
        grad_bqv,
        grad_attn_s,
        stats[3],
        stats[4],
        stats[5],
        grad_up_s,
        grad_bup,
        grad_down_s,
        stats[7],
    )


def solution(mesh):
    in_specs = (
        P("fsdp", "ctx", None),
        P("fsdp", None),
        P("fsdp", "ctx", None),
        P(),
        P(),
        P("fsdp", None, "tp"),
        P(None, "tp"),
        P("tp", "fsdp"),
        P(),
        P(),
        P(),
        P("fsdp", "tp"),
        P("tp"),
        P("tp", "fsdp"),
        P(),
    )
    out_specs = (
        P("fsdp", "ctx", None),
        P("fsdp", "ctx", None),
        P(),
        P(),
        P("fsdp", None, "tp"),
        P(None, "tp"),
        P("tp", "fsdp"),
        P(),
        P(),
        P(),
        P("fsdp", "tp"),
        P("tp"),
        P("tp", "fsdp"),
        P(),
    )
    return jax.shard_map(local, mesh=mesh, in_specs=in_specs, out_specs=out_specs, check_vma=False)
```

profile of v0, /device:TPU:0, one launch (start us, length us, event | category | flops | bytes accessed | tf_op | source)
XLA Modules:
  0.0 2753.5 jit_solution(11157724352229351513)
XLA Ops:
  16.5 76.2 %all-gather.11.cloned.1.call-done = bf16[2048,3,512]{2,0,1:T(8,128)(2,1)} async-done(((bf16[1024,3,512]{2,0,1:T(8,128)(2,1)}), bf16[2048,3,512]{2,0,1:T(8,128)(2,1)}) %all-gather.11.cloned.1.call-update) | async-done | bytes 6291472 | tf_op jit(solution)/shard_map/all_gather | solution.py:77
  92.7 10.2 fusion.40
  107.2 4.0 fusion.36
  124.0 17.8 all-gather.15.cloned.1.call-done
  141.8 18.5 fusion.39
  160.2 13.7 fusion
  173.9 4.5 all-gather.13.cloned.1.call-done
  178.4 16.0 fusion.25
  195.2 17.8 all-gather.17.cloned.1.call-done
  213.0 7.3 fusion.28
  221.3 6.8 convert.10
  229.9 135.1 %reduce-scatter.11.cloned.1.call-done = f32[256,2048]{1,0:T(8,128)} async-done(((f32[1024,2048]{1,0:T(8,128)}), f32[256,2048]{1,0:T(8,128)}) %reduce-scatter.11.cloned.1.call-update) | async-done | bytes 2097168 | tf_op jit(solution)/shard_map/reduce_scatter | solution.py:44
  370.9 7.3 convert_multiply_fusion
  378.2 92.9 %all-gather.21.cloned.1.call-done = bf16[2048,2048]{1,0:T(8,128)(2,1)} async-done(((bf16[1024,2048]{1,0:T(8,128)(2,1)}), bf16[2048,2048]{1,0:T(8,128)(2,1)}) %all-gather.21.cloned.1.call-update) | async-done | bytes 8388624 | tf_op jit(solution)/shard_map/all_gather | solution.py:78
  471.1 82.9 %all-gather.19.cloned.1.call-done = bf16[1024,2048]{1,0:T(8,128)(2,1)} async-done(((bf16[256,2048]{1,0:T(8,128)(2,1)}), bf16[1024,2048]{1,0:T(8,128)(2,1)}) %all-gather.19.cloned.1.call-update) | async-done | bytes 4194320 | tf_op jit(solution)/shard_map/all_gather | solution.py:46
  554.1 14.5 fusion.41
  568.5 89.6 %all-gather.23.cloned.1.call-done = bf16[2048,2048]{1,0:T(8,128)(2,1)} async-done(((bf16[2048,1024]{1,0:T(8,128)(2,1)}), bf16[2048,2048]{1,0:T(8,128)(2,1)}) %all-gather.23.cloned.1.call-update) | async-done | bytes 8388624 | tf_op jit(solution)/shard_map/all_gather | solution.py:82
  658.2 20.4 convert_reduce_fusion
  680.6 13.8 fusion.42
  694.4 17.6 fusion.34
  712.7 126.3 %reduce-scatter.15.cloned.1.call-done = f32[256,2048]{1,0:T(8,128)} async-done(((f32[1024,2048]{1,0:T(8,128)}), f32[256,2048]{1,0:T(8,128)}) %reduce-scatter.15.cloned.1.call-update) | async-done | bytes 2097168 | tf_op jit(solution)/shard_map/reduce_scatter | solution.py:44
  842.1 144.3 %reduce-scatter.13.cloned.1.call-done = f32[256,2048]{1,0:T(8,128)} async-done(((f32[1024,2048]{1,0:T(8,128)}), f32[256,2048]{1,0:T(8,128)}) %reduce-scatter.13.cloned.1.call-update) | async-done | bytes 2097168 | tf_op jit(solution)/shard_map/reduce_scatter | solution.py:44
  986.5 6.8 convert_reduce_fusion.3
  993.5 81.4 %all-gather.27.cloned.1.call-done = bf16[1024,2048]{1,0:T(8,128)(2,1)} async-done(((bf16[256,2048]{1,0:T(8,128)(2,1)}), bf16[1024,2048]{1,0:T(8,128)(2,1)}) %all-gather.27.cloned.1.call-update) | async-done | bytes 4194320 | tf_op jit(solution)/shard_map/all_gather | solution.py:46
  1074.9 5.2 convolution_convert_fusion
  1081.1 17.1 fusion.13
  1098.3 26.1 multiply_reduce_fusion
  1124.4 28.8 %multiply_convert_fusion = bf16[2,4,512,2048]{3,2,1,0:T(8,128)(2,1)} fusion(f32[2,4,512,2048]{3,2,1,0:T(8,128)} %get-tuple-element.55, f32[2,4,512,2048]{3,2,1,0:T(8,128)} %get-tuple-element.53, f32[2,4,512]{2,1,0:T(4,128)S(1)} %get-tuple-element.54, f32[2,4,512]{2,1,0:T(4,128)S(1)} %bitcast.87), kind=kLoop, calls=%fused_computation | loop fusion | flops 33554432 | bytes 83918848 | tf_op jit(solution)/shard_map/convert_element_type | solution.py:174
  1153.2 11.7 multiply_bitcast_fusion
  1165.2 10.5 fusion.24
  1187.2 56.1 %reduce-scatter.17.cloned.1.call-done = f32[2,512,4,128]{1,3,2,0:T(8,128)} async-done(((f32[2,2048,4,128]{1,3,2,0:T(8,128)}), f32[2,512,4,128]{1,3,2,0:T(8,128)}) %reduce-scatter.17.cloned.1.call-update) | async-done | bytes 2097168 | tf_op jit(solution)/shard_map/reduce_scatter | solution.py:185
  1253.2 12.1 convolution_bitcast_fusion
  1266.5 6.6 fusion.26
  1273.4 20.7 fusion.17
  1294.2 15.3 fusion.44
  1311.4 11.3 fusion.43
  1324.5 85.5 %reduce-scatter.21.cloned.1.call-done = f32[256,2048]{1,0:T(8,128)} async-done(((f32[1024,2048]{1,0:T(8,128)}), f32[256,2048]{1,0:T(8,128)}) %reduce-scatter.21.cloned.1.call-update) | async-done | bytes 2097168 | tf_op jit(solution)/shard_map/reduce_scatter | solution.py:44
  1413.9 4.0 add_convert_fusion.1
  1418.0 49.7 %reduce-scatter.25.cloned.1.call-done = f32[512,1024]{1,0:T(8,128)} async-done(((f32[512,2048]{1,0:T(8,128)}), f32[512,1024]{1,0:T(8,128)}) %reduce-scatter.25.cloned.1.call-update) | async-done | bytes 2097168 | tf_op jit(solution)/shard_map/reduce_scatter | solution.py:210
  1467.7 191.4 %reduce-scatter.29.cloned.1.call-done = f32[2048,1024]{1,0:T(8,128)} async-done(((f32[2048,2048]{1,0:T(8,128)}), f32[2048,1024]{1,0:T(8,128)}) %reduce-scatter.29.cloned.1.call-update) | async-done | bytes 8388624 | tf_op jit(solution)/shard_map/reduce_scatter | solution.py:211
  1659.2 191.3 %reduce-scatter.27.cloned.1.call-done = f32[1024,2048]{1,0:T(8,128)} async-done(((f32[2048,2048]{1,0:T(8,128)}), f32[1024,2048]{1,0:T(8,128)}) %reduce-scatter.27.cloned.1.call-update) | async-done | bytes 8388624 | tf_op jit(solution)/shard_map/reduce_scatter | solution.py:207
  1850.4 146.8 %reduce-scatter.23.cloned.1.call-done = f32[1024,3,512]{2,0,1:T(8,128)} async-done(((f32[2048,3,512]{2,0,1:T(8,128)}), f32[1024,3,512]{2,0,1:T(8,128)}) %reduce-scatter.23.cloned.1.call-update) | async-done | bytes 6291472 | tf_op jit(solution)/shard_map/reduce_scatter | solution.py:206
  1997.2 82.4 %all-gather.25.cloned.1.call-done = bf16[1024,2048]{1,0:T(8,128)(2,1)} async-done(((bf16[256,2048]{1,0:T(8,128)(2,1)}), bf16[1024,2048]{1,0:T(8,128)(2,1)}) %all-gather.25.cloned.1.call-update) | async-done | bytes 4194320 | tf_op jit(solution)/shard_map/all_gather | solution.py:46
  2079.7 130.9 %all-reduce.5.cloned.1.call-done = (f32[2048]{0:T(1024)}, f32[2048]{0:T(1024)}, f32[2,2048]{1,0:T(2,128)}, f32[2048]{0:T(1024)}, f32[2048]{0:T(1024)}, /*index=5*/f32[2048]{0:T(1024)}, f32[8192]{0:T(1024)}, f32[2048]{0:T(1024)}) async-done(((f32[2048]{0:T(1024)}, f32[2048]{0:T(1024)}, f32[2,2048]{1,0:T(2,128)}, f32[2048]{0:T(1024)}, f32[2048]{0:T(1024)}, /*index=5*/f32[2048]{0:T(1024)}, f32[8192]{0:T(1024)}, ...) | async-done | bytes 98320 | tf_op jit(solution)/shard_map/psum | solution.py:231
  2213.2 81.5 %all-gather.29.cloned.1.call-done = bf16[1024,2048]{1,0:T(8,128)(2,1)} async-done(((bf16[256,2048]{1,0:T(8,128)(2,1)}), bf16[1024,2048]{1,0:T(8,128)(2,1)}) %all-gather.29.cloned.1.call-update) | async-done | bytes 4194320 | tf_op jit(solution)/shard_map/all_gather | solution.py:46
  2294.6 426.4 %all-reduce.7.cloned.1.call-done = (f32[1024,3,512]{2,0,1:T(8,128)}, f32[512,1024]{1,0:T(8,128)}, f32[1024,2048]{1,0:T(8,128)}, f32[2048,1024]{1,0:T(8,128)}) async-done(((f32[1024,3,512]{2,0,1:T(8,128)}, f32[512,1024]{1,0:T(8,128)}, f32[1024,2048]{1,0:T(8,128)}, f32[2048,1024]{1,0:T(8,128)}), (f32[1024,3,512]{2,0,1:T(8,128)}, f32[512,1024]{1,0:T(8,128)}, f32[1024,2048]{1,0:T(8,128)}, ...) | async-done | bytes 25165840 | tf_op jit(solution)/shard_map/psum | solution.py:213
  2721.0 5.1 copy.86
  2736.9 4.2 copy.95
  (210 shorter events, 91.8 us)
Async XLA Ops:
  7.2 85.5 %all-gather.11.cloned.1.call-start = ((), (), s32[]{:S(2)}) async-start(), calls=%async_computation.10 | async-start | bytes 9437184 | tf_op jit(solution)/shard_map/all_gather | solution.py:77
  7.9 4.8 copy-start.30
  7.9 4.8 copy-start.31
  7.9 133.8 %all-gather.15.cloned.1.call-start = ((), (), s32[]{:S(2)}) async-start(), calls=%async_computation.12 | async-start | bytes 5242880 | tf_op jit(solution)/shard_map/all_gather | solution.py:110
  8.0 3.5 copy-start
  107.1 71.3 %all-gather.13.cloned.1.call-start = ((), (), s32[]{:S(2)}) async-start(), calls=%async_computation.11 | async-start | bytes 5242880 | tf_op jit(solution)/shard_map/all_gather | solution.py:111
  107.2 34.6 %copy-start.12 = (f32[1,512]{1,0:T(1,128)}, f32[1,512]{1,0:T(1,128)S(1)}, u32[]{:S(2)}) copy-start(f32[1,512]{1,0:T(1,128)S(1)} %get-tuple-element.50) | copy-start | bytes 6148
  116.1 4.2 copy-start.4
  116.2 96.8 %all-gather.17.cloned.1.call-start = ((), (), s32[]{:S(2)}) async-start(), calls=%async_computation.13 | async-start | bytes 3145728 | tf_op jit(solution)/shard_map/all_gather | solution.py:81
  116.8 248.2 %reduce-scatter.11.cloned.1.call-start = ((), (), s32[]{:S(2)}) async-start(), calls=%async_computation.14 | async-start | bytes 10485760 | tf_op jit(solution)/shard_map/reduce_scatter | solution.py:44
  124.0 36.3 %copy-start.1 = (f32[2,512,4,128]{1,3,2,0:T(8,128)}, f32[2,512,4,128]{1,3,2,0:T(8,128)S(1)}, u32[]{:S(2)}) copy-start(f32[2,512,4,128]{1,3,2,0:T(8,128)S(1)} %copy.39) | copy-start | bytes 6291460
  195.2 25.1 copy-start.5
  220.4 250.8 %all-gather.21.cloned.1.call-start = ((), (), s32[]{:S(2)}) async-start(), calls=%async_computation.16 | async-start | bytes 12582912 | tf_op jit(solution)/shard_map/all_gather | solution.py:78
  220.9 333.1 %all-gather.19.cloned.1.call-start = ((), (), s32[]{:S(2)}) async-start(), calls=%async_computation.15 | async-start | bytes 5242880 | tf_op jit(solution)/shard_map/all_gather | solution.py:46
  229.9 138.7 %copy-start.19 = (f32[256]{0:T(256)}, f32[256]{0:T(256)S(1)}, u32[]{:S(2)}) copy-start(f32[256]{0:T(256)S(1)} %broadcast_multiply_fusion.3) | copy-start | bytes 3076
  370.1 288.1 %all-gather.23.cloned.1.call-start = ((), (), s32[]{:S(2)}) async-start(), calls=%async_computation.17 | async-start | bytes 12582912 | tf_op jit(solution)/shard_map/all_gather | solution.py:82
  370.8 468.2 %reduce-scatter.15.cloned.1.call-start = ((), (), s32[]{:S(2)}) async-start(), calls=%async_computation.20 | async-start | bytes 10485760 | tf_op jit(solution)/shard_map/reduce_scatter | solution.py:44
  694.4 292.1 %reduce-scatter.13.cloned.1.call-start = ((), (), s32[]{:S(2)}) async-start(), calls=%async_computation.18 | async-start | bytes 10485760 | tf_op jit(solution)/shard_map/reduce_scatter | solution.py:44
  712.0 362.9 %all-gather.27.cloned.1.call-start = ((), (), s32[]{:S(2)}) async-start(), calls=%async_computation.21 | async-start | bytes 5242880 | tf_op jit(solution)/shard_map/all_gather | solution.py:46
  993.3 185.7 %reduce-scatter.19.cloned.1.call-start = ((), (), s32[]{:S(2)}) async-start(), calls=%async_computation.23 | async-start | bytes 10485760 | tf_op jit(solution)/shard_map/reduce_scatter | solution.py:186
  1098.2 145.0 %reduce-scatter.17.cloned.1.call-start = ((), (), s32[]{:S(2)}) async-start(), calls=%async_computation.22 | async-start | bytes 10485760 | tf_op jit(solution)/shard_map/reduce_scatter | solution.py:185
  1124.4 28.8 %copy-start.2 = (f32[2,512,4,128]{1,3,2,0:T(8,128)S(1)}, f32[2,512,4,128]{1,3,2,0:T(8,128)}, u32[]{:S(2)}) copy-start(f32[2,512,4,128]{1,3,2,0:T(8,128)} %copy-done.1) | copy-start | bytes 6291460
  1124.4 28.8 %copy-start.13 = (f32[1,512]{1,0:T(1,128)S(1)}, f32[1,512]{1,0:T(1,128)}, u32[]{:S(2)}) copy-start(f32[1,512]{1,0:T(1,128)} %copy-done.12) | copy-start | bytes 6148
  1164.9 245.0 %reduce-scatter.21.cloned.1.call-start = ((), (), s32[]{:S(2)}) async-start(), calls=%async_computation.24 | async-start | bytes 10485760 | tf_op jit(solution)/shard_map/reduce_scatter | solution.py:44
  1253.2 12.1 copy-start.7
  1265.3 202.4 %reduce-scatter.25.cloned.1.call-start = ((), (), s32[]{:S(2)}) async-start(), calls=%async_computation.27 | async-start | bytes 6291456 | tf_op jit(solution)/shard_map/reduce_scatter | solution.py:210
  1273.1 386.0 %reduce-scatter.29.cloned.1.call-start = ((), (), s32[]{:S(2)}) async-start(), calls=%async_computation.29 | async-start | bytes 25165824 | tf_op jit(solution)/shard_map/reduce_scatter | solution.py:211
  1294.2 556.3 %reduce-scatter.27.cloned.1.call-start = ((), (), s32[]{:S(2)}) async-start(), calls=%async_computation.28 | async-start | bytes 25165824 | tf_op jit(solution)/shard_map/reduce_scatter | solution.py:207
  1309.6 687.6 %reduce-scatter.23.cloned.1.call-start = ((), (), s32[]{:S(2)}) async-start(), calls=%async_computation.26 | async-start | bytes 18874368 | tf_op jit(solution)/shard_map/reduce_scatter | solution.py:206
  1322.8 87.2 %copy-start.16 = (f32[2048]{0:T(1024)S(1)}, f32[2048]{0:T(1024)}, u32[]{:S(2)}) copy-start(f32[2048]{0:T(1024)} %copy-done.15) | copy-start | bytes 24580
  1322.8 87.2 %copy-start.20 = (f32[256]{0:T(256)S(1)}, f32[256]{0:T(256)}, u32[]{:S(2)}) copy-start(f32[256]{0:T(256)} %copy-done.19) | copy-start | bytes 3076
  1322.8 756.9 %all-gather.25.cloned.1.call-start = ((), (), s32[]{:S(2)}) async-start(), calls=%async_computation.19 | async-start | bytes 5242880 | tf_op jit(solution)/shard_map/all_gather | solution.py:46
  1323.6 887.0 %all-reduce.5.cloned.1.call-start = ((), (), s32[]{:S(2)}) async-start(), calls=%async_computation.30 | async-start | bytes 196608 | tf_op jit(solution)/shard_map/psum | solution.py:231
  1324.0 89.9 %copy-start.14 = (f32[8192]{0:T(1024)}, f32[8192]{0:T(1024)S(1)}, u32[]{:S(2)}) copy-start(f32[8192]{0:T(1024)S(1)} %dynamic_update_slice.7) | copy-start | bytes 98308
  1324.5 89.4 %copy-start.17 = (f32[2,2048]{1,0:T(2,128)}, f32[2,2048]{1,0:T(2,128)S(1)}, u32[]{:S(2)}) copy-start(f32[2,2048]{1,0:T(2,128)S(1)} %maximum_dynamic-update-slice_fusion) | copy-start | bytes 49156
  1410.0 4.0 copy-start.3
  1413.9 880.7 %all-gather.29.cloned.1.call-start = ((), (), s32[]{:S(2)}) async-start(), calls=%async_computation.25 | async-start | bytes 5242880 | tf_op jit(solution)/shard_map/all_gather | solution.py:46
  1418.0 1303.0 %all-reduce.7.cloned.1.call-start = ((), (), s32[]{:S(2)}) async-start(), calls=%async_computation.31 | async-start | bytes 50331648 | tf_op jit(solution)/shard_map/psum | solution.py:213
  2721.0 5.1 copy-start.10
  2721.0 8.4 slice-start.4
  2726.0 3.5 slice-start.5
  2728.8 8.1 slice-start.2
  2729.6 4.2 copy-start.11
  2729.6 5.5 copy-start.25
  2729.6 7.3 slice-start.3
  2733.8 7.4 slice-start
  2736.9 5.2 slice-start.1
  2742.2 3.4 copy-start.22
  (18 other events, 29.3 us)
Sparse Core Ops, SparseCore 0:
  9.6 83.0 all-gather.10
  107.2 34.4 all-gather.14
  143.9 34.4 all-gather.12
  179.8 33.1 all-gather.16
  220.4 144.4 reduce-scatter.10
  366.3 104.7 all-gather.20
  473.3 80.7 all-gather.18
  555.6 102.5 all-gather.22
  694.5 144.4 reduce-scatter.14
  841.2 145.1 reduce-scatter.12
  993.4 81.4 all-gather.26
  1098.4 70.2 reduce-scatter.18
  1171.4 71.7 reduce-scatter.16
  1265.5 144.4 reduce-scatter.20
  1412.7 55.0 reduce-scatter.24
  1470.0 189.1 reduce-scatter.28
  1661.3 189.0 reduce-scatter.26
  1852.7 144.4 reduce-scatter.22
  1998.9 80.7 all-gather.24
  2088.2 122.3 all-reduce.4
  2212.7 81.8 all-gather.28
  2297.4 423.5 all-reduce.6
where the time goes:
time: 2760 us; the launch traced here: 2750 us
  waiting for transfers between devices  2310 us (84%)
  matrix products  255 us (9%)
  other arithmetic  99.7 us (4%)
  local copies, waits for them, and re-layouts  67.3 us (2%)
    reduce_scatter x4, waiting for transfers between devices, tensor_rows(): lax.psum_scatter(partial_value, 'tp', scatter_dimension=0, tiled=True)  491 us
    psum x1, waiting for transfers between devices, local(): lax.psum((grad_qkv_s, grad_up_s, grad_attn_s, grad_down_s), 'ctx')  426 us
    all_gather x4, waiting for transfers between devices, tensor_rows(): return (lax.all_gather(wide_rows, 'tp', axis=0, tiled=True), kept_rows)  328 us
    reduce_scatter x1, waiting for transfers between devices, local(): lax.psum_scatter(grad_down, 'fsdp', scatter_dimension=1, tiled=True)  191 us
    reduce_scatter x1, waiting for transfers between devices, local(): lax.psum_scatter(grad_up, 'fsdp', scatter_dimension=0, tiled=True)  191 us
    reduce_scatter x1, waiting for transfers between devices, local(): lax.psum_scatter(grad_qkv, 'fsdp', scatter_dimension=0, tiled=True)  147 us
    psum x1, waiting for transfers between devices, local(): lax.psum((jnp.sum(norm_grad_one * normed_share, axis=0), jnp.sum(norm_gra...  131 us
    all_gather x1, waiting for transfers between devices, local(): lax.all_gather(w_up, 'fsdp', axis=0, tiled=True)  92.9 us
  transfers between devices with their start and end apart: 22, of which 21 were waited for; matrix products, arithmetic and copies ran while one was open for 10% of the time, Pallas kernels for 0%

commit v1 on v0

v1 whole, which is shorter than its diff:
```python
import jax
import jax.numpy as jnp
from jax import lax
from jax.sharding import PartitionSpec as P

HD = 128
NORM_EPS = 1e-05
MASKED = -1e30
F32 = jnp.float32
BF16 = jnp.bfloat16

X_SWAP = [(0, 1), (1, 0)]


def xor_pairs(count, bit):
    return [(j, j ^ bit) for j in range(count)]


def core_swap(values):
    return lax.ppermute(values, "ctx", xor_pairs(lax.axis_size("ctx"), 1))


def y_swap(values):
    return lax.ppermute(values, "ctx", xor_pairs(lax.axis_size("ctx"), 2))


def x_swap(values):
    return lax.ppermute(values, "fsdp", X_SWAP)


def norm_parts(values):
    centred = values - jnp.mean(values, axis=-1, keepdims=True)
    norm_scale = lax.rsqrt(jnp.mean(centred * centred, axis=-1, keepdims=True) + NORM_EPS)
    return (centred * norm_scale, norm_scale)


def norm_back(grad_norm, gain, normed, norm_scale):
    lifted = grad_norm * gain
    return norm_scale * (
        lifted
        - jnp.mean(lifted, axis=-1, keepdims=True)
        - normed * jnp.mean(lifted * normed, axis=-1, keepdims=True)
    )


def gelu_tanh(values):
    return jax.nn.gelu(values, approximate=True)


def piece(values, start, count, axis):
    return lax.dynamic_slice_in_dim(values, start, count, axis)


def dot(a, b):
    return jnp.dot(a, b, preferred_element_type=F32)


def dot_t(a, b):
    return lax.dot_general(a, b, (((1,), (1,)), ((), ())), preferred_element_type=F32)


def t_dot(a, b):
    return lax.dot_general(a, b, (((0,), (0,)), ((), ())), preferred_element_type=F32)


def to_relative(values):
    i, c = lax.axis_index("fsdp"), lax.axis_index("ctx") & 1
    size = values.shape[-1] // 4
    axis = values.ndim - 1
    return jnp.concatenate(
        [piece(values, (((k & 1) ^ i) * 2 + ((k >> 1) ^ c)) * size, size, axis) for k in range(4)],
        axis=axis,
    )


def to_natural(values):
    i, c = lax.axis_index("fsdp"), lax.axis_index("ctx") & 1
    size = values.shape[-1] // 4
    axis = values.ndim - 1
    return jnp.concatenate(
        [piece(values, (((b >> 1) ^ i) + 2 * ((b & 1) ^ c)) * size, size, axis) for b in range(4)],
        axis=axis,
    )


def roll_rows(values):
    n = lax.axis_size("tp")
    z = lax.axis_index("tp")
    size = values.shape[0] // n
    return jnp.concatenate(
        [piece(values, lax.rem(z + k, n) * size, size, 0) for k in range(n)], axis=0
    )


def gather_weight(values, axis):
    c = lax.axis_index("ctx") & 1
    size = values.shape[axis] // 2
    mine_c = piece(values, c * size, size, axis)
    mine_n = piece(values, (1 - c) * size, size, axis)
    other_c = x_swap(mine_c)
    other_n = core_swap(other_c)
    return jnp.concatenate([mine_c, other_c, mine_n, other_n], axis=axis)


def reduce_weight(values, axis):
    c = lax.axis_index("ctx") & 1
    size = values.shape[axis] // 4

    def cut(array, k, count):
        return lax.slice_in_dim(array, k * size, (k + count) * size, axis=axis)

    got = core_swap(cut(values, 2, 2))
    pair = cut(values, 0, 2).astype(F32) + got.astype(F32)
    got = x_swap(cut(pair, 1, 1).astype(BF16))
    four = lax.optimization_barrier((cut(pair, 0, 1) + got.astype(F32)).astype(BF16))
    got = y_swap(four)
    total = lax.optimization_barrier((four.astype(F32) + got.astype(F32)).astype(BF16))
    other = core_swap(total)
    first = jnp.where(c == 0, total, other)
    second = jnp.where(c == 0, other, total)
    return jnp.concatenate([first, second], axis=axis).astype(F32)


def line_reduce(partial):
    n = lax.axis_size("tp")
    size = partial.shape[0] // n

    def block(k):
        return partial[k * size : (k + 1) * size]

    ahead = behind = None
    for step in range(1, n):
        up, down = block(n - step), block(step)
        if ahead is not None:
            up = (up.astype(F32) + ahead.astype(F32)).astype(BF16)
            down = (down.astype(F32) + behind.astype(F32)).astype(BF16)
        ahead = lax.ppermute(up, "tp", [(j, j + 1) for j in range(step)])
        behind = lax.ppermute(down, "tp", [(n - 1 - j, n - 2 - j) for j in range(step)])
    total = block(0).astype(F32)
    if ahead is not None:
        total = total + ahead.astype(F32) + behind.astype(F32)
    return total


def line_gather(own):
    n = lax.axis_size("tp")
    z = lax.axis_index("tp")
    ahead, behind = [own], [own]
    for k in range(1, n):
        ahead.append(lax.ppermute(ahead[-1], "tp", [(j, j + 1) for j in range(k - 1, n - 1)]))
        behind.append(lax.ppermute(behind[-1], "tp", [(j, j - 1) for j in range(1, n - k + 1)]))
    return [own] + [jnp.where(z + k < n, behind[k], ahead[n - k]) for k in range(1, n)]


def natural_rows(blocks):
    n = len(blocks)
    z = lax.axis_index("tp")
    size = blocks[0].shape[0]
    doubled = jnp.concatenate(blocks, axis=0)
    return jnp.concatenate(
        [piece(doubled, lax.rem(j - z + n, n) * size, size, 0) for j in range(n)], axis=0
    )


def scores_of(queries, keys, allowed):
    raw = jnp.einsum("qhe,khe->hqk", queries, keys, preferred_element_type=F32) * HD ** (-0.5)
    return jnp.where(allowed[None], raw, MASKED)


def attend(queries, keys, values, allowed):
    scores = scores_of(queries, keys, allowed)
    row_max = jnp.max(scores, axis=-1, keepdims=True)
    exp_scores = jnp.exp(scores - row_max)
    row_total = jnp.sum(exp_scores, axis=-1, keepdims=True)
    weights = (exp_scores / row_total).astype(BF16)
    attended = jnp.einsum("hqk,khe->qhe", weights, values, preferred_element_type=F32)
    return attended.astype(BF16), row_max + jnp.log(row_total)


def attend_back(queries, keys, values, allowed, log_total, grad_att):
    scores = scores_of(queries, keys, allowed)
    probs = jnp.exp(scores - log_total)
    probs_low = probs.astype(BF16)
    grad_values = jnp.einsum("hqk,qhe->khe", probs_low, grad_att, preferred_element_type=F32)
    grad_probs = jnp.einsum("qhe,khe->hqk", grad_att, values, preferred_element_type=F32)
    grad_scores = (
        probs * (grad_probs - jnp.sum(probs * grad_probs, axis=-1, keepdims=True))
    ).astype(BF16)
    factor = HD ** (-0.5)
    grad_queries = jnp.einsum("hqk,khe->qhe", grad_scores, keys, preferred_element_type=F32)
    grad_keys = jnp.einsum("hqk,qhe->khe", grad_scores, queries, preferred_element_type=F32)
    return (
        (grad_queries * factor).astype(BF16),
        (grad_keys * factor).astype(BF16),
        grad_values.astype(BF16),
    )


def sum_pairs(values, tp_too):
    values = values + core_swap(values)
    values = values + y_swap(values)
    values = values + x_swap(values)
    if tp_too:
        n = lax.axis_size("tp")
        bit = 1
        while bit < n:
            values = values + lax.ppermute(values, "tp", xor_pairs(n, bit))
            bit *= 2
    return values


def local(
    block_in,
    segments,
    out_grad,
    ln1_gain,
    ln1_bias,
    w_qkv,
    b_qv,
    w_attn_out,
    b_attn_out,
    ln2_gain,
    ln2_bias,
    w_up,
    b_up,
    w_down,
    b_down,
):
    seqs, span, width = block_in.shape
    n = lax.axis_size("tp")
    cx = lax.axis_index("ctx")
    blocks = lax.axis_size("ctx")
    part = span // n
    local_width = w_qkv.shape[2]
    heads = local_width // HD
    each = range(seqs)

    wk = gather_weight(w_qkv[:, 1], 0)
    wv = gather_weight(w_qkv[:, 2], 0)
    wq = gather_weight(w_qkv[:, 0], 0)
    wo = gather_weight(w_attn_out, 1)
    wu = gather_weight(w_up, 0)
    wd = gather_weight(w_down, 1)

    gain_one = to_relative(ln1_gain.astype(F32))
    shift_one = to_relative(ln1_bias.astype(F32))
    gain_two = to_relative(ln2_gain.astype(F32))
    shift_two = to_relative(ln2_bias.astype(F32))
    bias_out = to_relative(b_attn_out.astype(F32))
    bias_down = to_relative(b_down.astype(F32))
    bias_q, bias_v = b_qv[0].astype(F32), b_qv[1].astype(F32)
    bias_up = b_up.astype(F32)

    spot = lax.rem(lax.axis_index("tp") * part + jnp.arange(span), span)

    x_rows, n1, queries, kv_all, allowed, cot = [], [], [], [], [], []
    for s in each:
        rows = to_relative(roll_rows(block_in[s]))
        x_rows.append(rows)
        normed, unused = norm_parts(rows.astype(F32))
        n1.append((normed * gain_one + shift_one).astype(BF16))
    for s in each:
        keys_here = dot(n1[s], wk).astype(BF16)
        values_here = (dot(n1[s], wv) + bias_v).astype(BF16)
        kv = jnp.concatenate([keys_here, values_here], axis=1)
        kv1 = core_swap(kv)
        kv2 = y_swap(kv)
        kv3 = core_swap(kv2)
        kv_all.append(jnp.concatenate([kv, kv1, kv2, kv3], axis=0))
    for s in each:
        queries.append((dot(n1[s], wq) + bias_q).astype(BF16))
        query_seg = roll_rows(piece(segments[s], cx * span, span, 0))
        key_seg = jnp.concatenate(
            [roll_rows(piece(segments[s], (cx ^ b) * span, span, 0)) for b in range(blocks)]
        )
        key_pos = jnp.concatenate([(cx ^ b) * span + spot for b in range(blocks)])
        allowed.append(
            (query_seg[:, None] == key_seg[None, :])
            & (key_pos[None, :] <= (cx * span + spot)[:, None])
        )
        valid = (query_seg != 0).astype(BF16)[:, None]
        cot.append(to_relative(roll_rows(out_grad[s])) * valid)

    def heads_of(values):
        return values.reshape(values.shape[0], heads, HD)

    def halves(s):
        return heads_of(kv_all[s][:, :local_width]), heads_of(kv_all[s][:, local_width:])

    attended, log_total, middle = [], [], []
    n2 = []
    for s in each:
        keys, values = halves(s)
        out, total = attend(heads_of(queries[s]), keys, values, allowed[s])
        attended.append(out.reshape(span, local_width))
        log_total.append(total)
        summed = line_reduce(dot(attended[s], wo).astype(BF16))
        mid = x_rows[s][:part].astype(F32) + summed + bias_out
        middle.append(mid)
        normed, unused = norm_parts(mid)
        own = (normed * gain_two + shift_two).astype(BF16)
        n2.append(jnp.concatenate(line_gather(own), axis=0))

    active, grad_hidden, kept_two, gm = [], [], [], []
    out_rows = []
    for s in each:
        hidden = dot(n2[s], wu) + bias_up
        act, pull = jax.vjp(gelu_tanh, hidden)
        active.append(act.astype(BF16))
        grad_hidden.append(pull(dot_t(cot[s], wd))[0].astype(BF16))
        summed = line_reduce(dot_t(grad_hidden[s], wu).astype(BF16))
        normed, norm_scale = norm_parts(middle[s])
        grad_mid = cot[s][:part].astype(F32) + norm_back(summed, gain_two, normed, norm_scale)
        own = grad_mid.astype(BF16)
        kept_two.append((grad_mid, summed, normed, own))
        gm.append(jnp.concatenate(line_gather(own), axis=0))
    for s in each:
        summed = line_reduce(dot(active[s], wd).astype(BF16))
        own = to_natural((middle[s] + summed + bias_down).astype(BF16))
        out_rows.append(natural_rows(line_gather(own)))

    grads, kept_one, in_rows = [], [], []
    for s in each:
        grad_att = dot_t(gm[s], wo).astype(BF16)
        keys, values = halves(s)
        gq, gk, gv = attend_back(
            heads_of(queries[s]), keys, values, allowed[s], log_total[s], heads_of(grad_att)
        )
        gq = gq.reshape(span, local_width)
        gkv = jnp.concatenate(
            [gk.reshape(blocks, span, local_width), gv.reshape(blocks, span, local_width)], axis=2
        )
        got = core_swap(jnp.stack([gkv[1], gkv[3]]))
        far = (gkv[2].astype(F32) + got[1].astype(F32)).astype(BF16)
        near = gkv[0].astype(F32) + got[0].astype(F32)
        total = (near + y_swap(far).astype(F32)).astype(BF16)
        gk, gv = total[:, :local_width], total[:, local_width:]
        grads.append((gq, gk, gv))
        summed = line_reduce((dot_t(gq, wq) + dot_t(gk, wk) + dot_t(gv, wv)).astype(BF16))
        normed, norm_scale = norm_parts(x_rows[s][:part].astype(F32))
        grad_in = kept_two[s][0] + norm_back(summed, gain_one, normed, norm_scale)
        kept_one.append((summed, normed))
        own = to_natural(grad_in.astype(BF16))
        in_rows.append(natural_rows(line_gather(own)))

    def stack(items):
        return jnp.concatenate(list(items), axis=0)

    n1_all, n2_all = stack(n1), stack(n2)
    g_down = reduce_weight(t_dot(stack(active), stack(cot)).astype(BF16), 1)
    g_up = reduce_weight(t_dot(n2_all, stack(grad_hidden)).astype(BF16), 0)
    g_out = reduce_weight(t_dot(stack(attended), stack(gm)).astype(BF16), 1)
    g_qkv = jnp.stack(
        [reduce_weight(t_dot(n1_all, stack(g[k] for g in grads)).astype(BF16), 0) for k in range(3)],
        axis=1,
    )

    def over_rows(items):
        return sum(jnp.sum(item.astype(F32), axis=0) for item in items)

    wide = [
        over_rows([kept_one[s][0] * kept_one[s][1] for s in each]),
        over_rows([kept_one[s][0] for s in each]),
        over_rows([kept_two[s][3] for s in each]),
        over_rows([kept_two[s][1] * kept_two[s][2] for s in each]),
        over_rows([kept_two[s][1] for s in each]),
        over_rows([cot[s][:part] for s in each]),
    ]
    wide_sum = sum_pairs(to_natural(jnp.stack(wide)), True)
    narrow = jnp.concatenate(
        [
            over_rows([g[0] for g in grads]),
            over_rows([g[2] for g in grads]),
            over_rows(grad_hidden),
        ]
    )
    narrow_sum = sum_pairs(narrow, False)
    g_bqv = narrow_sum[: 2 * local_width].reshape(2, local_width)
    g_bup = narrow_sum[2 * local_width :]
    return (
        jnp.stack(out_rows),
        jnp.stack(in_rows),
        wide_sum[0],
        wide_sum[1],
        g_qkv,
        g_bqv,
        g_out,
        wide_sum[2],
        wide_sum[3],
        wide_sum[4],
        g_up,
        g_bup,
        g_down,
        wide_sum[5],
    )


def solution(mesh):
    in_specs = (
        P("fsdp", "ctx", None),
        P("fsdp", None),
        P("fsdp", "ctx", None),
        P(),
        P(),
        P("fsdp", None, "tp"),
        P(None, "tp"),
        P("tp", "fsdp"),
        P(),
        P(),
        P(),
        P("fsdp", "tp"),
        P("tp"),
        P("tp", "fsdp"),
        P(),
    )
    out_specs = (
        P("fsdp", "ctx", None),
        P("fsdp", "ctx", None),
        P(),
        P(),
        P("fsdp", None, "tp"),
        P(None, "tp"),
        P("tp", "fsdp"),
        P(),
        P(),
        P(),
        P("fsdp", "tp"),
        P("tp"),
        P("tp", "fsdp"),
        P(),
    )
    return jax.shard_map(local, mesh=mesh, in_specs=in_specs, out_specs=out_specs, check_vma=False)
```

time: 2760 us -> 1270 us (0.46)
  waiting for transfers between devices: 2310 us -> 472 us
  starting transfers between devices: 2.04 us -> 231 us
  other arithmetic: 99.7 us -> 208 us
    reduce_scatter x10 -> x0, waiting for transfers between devices: 1130 us -> none  [the longest x4 491 us: tensor_rows(): lax.psum_scatter(partial_value, 'tp', scatter_dimension=0, tiled=True)]
    all_gather x10 -> x0, waiting for transfers between devices: 627 us -> none  [the longest x4 328 us: tensor_rows(): return (lax.all_gather(wide_rows, 'tp', axis=0, tiled=True), kept_rows)]
    psum x2 -> x0, waiting for transfers between devices: 557 us -> none  [the longest x1 426 us: local(): lax.psum((grad_qkv_s, grad_up_s, grad_attn_s, grad_down_s), 'ctx')]
    ppermute x0 -> x150, waiting for transfers between devices: none -> 472 us  [the longest x24 155 us: line_gather(): lax.ppermute(behind[-1], 'tp', [(j, j - 1) for j in range(1, n - k + 1)])]
    ppermute x0 -> x150, starting transfers between devices: none -> 231 us  [the longest x24 77.3 us: line_reduce(): ahead = lax.ppermute(up, 'tp', [(j, j + 1) for j in range(step)])]
    concatenate x0 -> x32, other arithmetic: none -> 33.3 us  [the longest x4 12.9 us: natural_rows(): doubled = jnp.concatenate(blocks, axis=0)]
    reshape x2 -> x8, local copies, waits for them, and re-layouts: 0.96 us -> 29.9 us  [the longest x4 17.9 us: local(): gk.reshape(blocks, span, local_width)]
    convert_element_type x15 -> x41, other arithmetic: 51.3 us -> 75.2 us  [the longest x16 19.2 us: line_reduce(): up = (up.astype(F32) + ahead.astype(F32)).astype(BF16)]
  transfers between devices with their start and end apart: 22 -> 150, of which waited for: 21 -> 55; matrix products, arithmetic and copies ran while one was open for 10% -> 40% of each run, Pallas kernels for 0% -> 0%
where the time goes in v1:
time: 1270 us; the launch traced here: 1260 us
  waiting for transfers between devices  472 us (37%)
  matrix products  251 us (20%)
  starting transfers between devices  231 us (18%)
  other arithmetic  208 us (16%)
  local copies, waits for them, and re-layouts  93.6 us (7%)
    ppermute x24, waiting for transfers between devices, line_gather(): lax.ppermute(behind[-1], 'tp', [(j, j - 1) for j in range(1, n - k + 1)])  155 us
    ppermute x12, waiting for transfers between devices, y_swap(): return lax.ppermute(values, 'ctx', xor_pairs(lax.axis_size('ctx'), 2))  132 us
    ppermute x24, waiting for transfers between devices, line_reduce(): ahead = lax.ppermute(up, 'tp', [(j, j + 1) for j in range(step)])  83.8 us
    ppermute x24, starting transfers between devices, line_reduce(): ahead = lax.ppermute(up, 'tp', [(j, j + 1) for j in range(step)])  77.3 us
    dot_general x12, matrix products, dot_t(): lax.dot_general(a, b, (((1,), (1,)), ((), ())), preferred_element_type=F32)  66.7 us
    ppermute x14, waiting for transfers between devices, x_swap(): return lax.ppermute(values, 'fsdp', X_SWAP)  64.7 us
    dot_general x12, matrix products, dot(): return jnp.dot(a, b, preferred_element_type=F32)  57 us
    ppermute x24, starting transfers between devices, line_gather(): lax.ppermute(ahead[-1], 'tp', [(j, j + 1) for j in range(k - 1, n - 1)])  49.3 us
  transfers between devices with their start and end apart: 150, of which 55 were waited for; matrix products, arithmetic and copies ran while one was open for 40% of the time, Pallas kernels for 0%

profile of v1, /device:TPU:0, one launch (start us, length us, event | category | flops | bytes accessed | tf_op | source)
XLA Modules:
  0.0 1260.9 jit_solution(1064969970400197513)
XLA Ops:
  39.0 8.3 collective-permute-done
  50.0 8.2 collective-permute-done.2
  73.4 17.6 %collective-permute-done.40 = bf16[512,1024]{0,1:T(8,128)(2,1)S(1)} collective-permute-done((bf16[512,1024]{0,1:T(8,128)(2,1)S(1)}, bf16[512,1024]{0,1:T(8,128)(2,1)S(1)}, u32[]{:S(2)}, u32[]{:S(2)}) %collective-permute-start.40) | collective-permute-done | bytes 1048608 | tf_op jit(solution)/shard_map/ppermute | solution.py:24
  97.5 15.1 %collective-permute-done.5 = bf16[512,1024]{0,1:T(8,128)(2,1)} collective-permute-done((bf16[512,1024]{0,1:T(8,128)(2,1)}, bf16[512,1024]{0,1:T(8,128)(2,1)}, u32[]{:S(2)}, u32[]{:S(2)}) %collective-permute-start.5) | collective-permute-done | bytes 1048608 | tf_op jit(solution)/shard_map/ppermute | solution.py:24
  119.8 7.6 fusion.278
  127.5 8.1 fusion.1
  135.6 8.2 fusion.109
  163.2 7.6 fusion.279
  170.9 8.1 fusion
  179.0 8.2 fusion.110
  196.0 7.8 collective-permute-done.11
  238.1 9.8 collective-permute-done.13
  258.3 8.8 collective-permute-done.18
  295.1 10.6 collective-permute-done.22
  306.6 8.9 multiply_convert_fusion.5
  315.6 11.4 convert_reduce_fusion.3
  327.0 10.5 convolution_convert_fusion.7
  340.0 8.4 convolution_convert_fusion.10
  396.1 9.6 collective-permute-done.29
  437.9 8.8 collective-permute-done.49
  482.0 9.7 collective-permute-done.76
  496.2 25.8 %collective-permute-done.77 = bf16[128,2048]{1,0:T(8,128)(2,1)S(1)} collective-permute-done((bf16[128,2048]{1,0:T(8,128)(2,1)S(1)}, bf16[128,2048]{1,0:T(8,128)(2,1)S(1)}, u32[]{:S(2)}, u32[]{:S(2)}) %collective-permute-start.77) | collective-permute-done | bytes 524320 | tf_op jit(solution)/shard_map/ppermute | solution.py:151
  526.0 14.0 %multiply_reduce_fusion.1 = (f32[4,512]{1,0:T(4,128)}, f32[4,512,2048]{2,1,0:T(8,128)}) fusion(f32[4,512,2048]{2,1,0:T(8,128)} %get-tuple-element.307, f32[4,512]{1,0:T(4,128)S(1)} %log_add_fusion.1, bf16[512,4,128]{0,2,1:T(8,128)(2,1)S(1)} %bitcast.310, bf16[2048,4,128]{0,2,1:T(8,128)(2,1)} %bitcast.301), kind=kOutput, calls=%fused_computation.4 | convolution fusion | flops 1086322688 | bytes 36192256 | tf_op jit(solution)/shard_map/qhe,khe->hqk/dot_general | solution.py:185
  555.9 8.7 multiply_convert_fusion.4
  564.6 10.2 convert_reduce_fusion.2
  574.8 10.3 convolution_convert_fusion.6
  589.5 13.7 %convolution_convert_fusion = bf16[2048,2048]{1,0:T(8,128)(2,1)} fusion(bf16[512,2048]{1,0:T(8,128)(2,1)} %get-tuple-element.310, bf16[512,2048]{1,0:T(8,128)(2,1)} %copy-done.195, bf16[512,2048]{1,0:T(8,128)(2,1)S(1)} %copy-done.40, bf16[512,2048]{1,0:T(8,128)(2,1)S(1)} %copy-done.38), kind=kOutput, calls=%fused_computation.26 | convolution fusion | flops 8610906112 | bytes 16777216 | tf_op jit(solution)/shard_map/dot_general | solution.py:63
  603.2 8.3 convolution_convert_fusion.8
  615.6 14.2 %convolution_convert_fusion.1 = bf16[2048,2048]{1,0:T(8,128)(2,1)} fusion(bf16[1024,2048]{1,0:T(8,128)(2,1)} %get-tuple-element.30, bf16[512,2048]{1,0:T(8,128)(2,1)} %get-tuple-element.319, bf16[512,2048]{1,0:T(8,128)(2,1)} %copy-done.194), kind=kOutput, calls=%fused_computation.27 | convolution fusion | flops 8602517504 | bytes 16777216 | tf_op jit(solution)/shard_map/dot_general | solution.py:63
  629.8 7.8 multiply_convert_fusion.1
  701.3 11.0 collective-permute-done.56
  746.4 7.4 collective-permute-done.98
  755.6 7.3 collective-permute-done.64
  781.8 20.6 %collective-permute-done.103 = bf16[128,2048]{1,0:T(8,128)(2,1)S(1)} collective-permute-done((bf16[128,2048]{1,0:T(8,128)(2,1)S(1)}, bf16[128,2048]{1,0:T(8,128)(2,1)S(1)}, u32[]{:S(2)}, u32[]{:S(2)}) %collective-permute-start.103) | collective-permute-done | bytes 524320 | tf_op jit(solution)/shard_map/ppermute | solution.py:151
  813.6 10.2 multiply_reduce_fusion
  829.9 10.2 multiply_convert_fusion
  840.1 7.9 convert_reduce_fusion.10
  922.6 9.5 collective-permute-done.124
  938.6 8.4 collective-permute-done.140
  947.2 9.2 collective-permute-done.125
  961.6 15.3 %collective-permute-done.147 = bf16[2048,512]{1,0:T(8,128)(2,1)S(1)} collective-permute-done((bf16[2048,512]{1,0:T(8,128)(2,1)S(1)}, bf16[2048,512]{1,0:T(8,128)(2,1)S(1)}, u32[]{:S(2)}, u32[]{:S(2)}) %collective-permute-start.147) | collective-permute-done | bytes 2097184 | tf_op jit(solution)/shard_map/ppermute | solution.py:28
  1011.2 10.5 collective-permute-done.143
  1071.5 65.0 %collective-permute-done.119 = f32[6,2048]{1,0:T(8,128)S(1)} collective-permute-done((f32[6,2048]{1,0:T(8,128)S(1)}, f32[6,2048]{1,0:T(8,128)S(1)}, u32[]{:S(2)}, u32[]{:S(2)}) %collective-permute-start.119) | collective-permute-done | bytes 49184 | tf_op jit(solution)/shard_map/ppermute | solution.py:24
  1166.1 9.3 collective-permute-done.129
  1188.1 12.6 collective-permute-done.112
  1201.3 7.9 collective-permute-done.90
  1215.6 10.3 collective-permute-done.116
  1228.1 9.1 collective-permute-done.91
  (1009 shorter events, 699.8 us)
Async XLA Ops:
  2.9 88.0 %collective-permute-start.9 = (bf16[512,512]{1,0:T(8,128)(2,1)}, bf16[512,512]{1,0:T(8,128)(2,1)}, u32[]{:S(2)}, u32[]{:S(2)}) collective-permute-start(bf16[512,512]{1,0:T(8,128)(2,1)} %get-tuple-element.228), channel_id=1, source_target_pairs={{0,16},{16,0},{1,17},{17,1},{2,18},{18,2},{3,19},{19,3},{4,20},{20... | collective-permute-start | bytes 1572872 | tf_op jit(solution)/shard_map/ppermute | solution.py:28
  13.1 45.7 %collective-permute-start.7 = (bf16[512,512]{1,0:T(8,128)(2,1)}, bf16[512,512]{1,0:T(8,128)(2,1)}, u32[]{:S(2)}, u32[]{:S(2)}) collective-permute-start(bf16[512,512]{1,0:T(8,128)(2,1)} %get-tuple-element.230), channel_id=1, source_target_pairs={{0,16},{16,0},{1,17},{17,1},{2,18},{18,2},{3,19},{19,3},{4,20},{20... | collective-permute-start | bytes 1572872 | tf_op jit(solution)/shard_map/ppermute | solution.py:28
  16.1 31.3 %collective-permute-start = (bf16[512,512]{1,0:T(8,128)(2,1)}, bf16[512,512]{1,0:T(8,128)(2,1)}, u32[]{:S(2)}, u32[]{:S(2)}) collective-permute-start(bf16[512,512]{1,0:T(8,128)(2,1)} %get-tuple-element.232), channel_id=1, source_target_pairs={{0,16},{16,0},{1,17},{17,1},{2,18},{18,2},{3,19},{19,3},{4,20},{20... | collective-permute-start | bytes 1572872 | tf_op jit(solution)/shard_map/ppermute | solution.py:28
  17.3 40.8 %collective-permute-start.2 = (bf16[512,512]{1,0:T(8,128)(2,1)}, bf16[512,512]{1,0:T(8,128)(2,1)}, u32[]{:S(2)}, u32[]{:S(2)}) collective-permute-start(bf16[512,512]{1,0:T(8,128)(2,1)} %get-tuple-element.234), channel_id=1, source_target_pairs={{0,16},{16,0},{1,17},{17,1},{2,18},{18,2},{3,19},{19,3},{4,20},{20... | collective-permute-start | bytes 1572872 | tf_op jit(solution)/shard_map/ppermute | solution.py:28
  58.8 32.6 %collective-permute-start.8 = (bf16[512,512]{1,0:T(8,128)(2,1)}, bf16[512,512]{1,0:T(8,128)(2,1)S(1)}, u32[]{:S(2)}, u32[]{:S(2)}) collective-permute-start(bf16[512,512]{1,0:T(8,128)(2,1)} %collective-permute-done.7), channel_id=1, source_target_pairs={{0,4},{4,0},{8,12},{12,8},{1,5},{5,1},{9,13},{13,9},{2,6},{6,2},{1... | collective-permute-start | bytes 1572872 | tf_op jit(solution)/shard_map/ppermute | solution.py:20
  66.4 46.2 %collective-permute-start.39 = (bf16[512,1024]{0,1:T(8,128)(2,1)S(1)}, bf16[512,1024]{0,1:T(8,128)(2,1)S(1)}, u32[]{:S(2)}, u32[]{:S(2)}) collective-permute-start(bf16[512,1024]{0,1:T(8,128)(2,1)S(1)} %pad_maximum_fusion.29), channel_id=1, source_target_pairs={{0,4},{4,0},{8,12},{12,8},{1,5},{5,1},{9,13},{13,9},{2,6},{6,2},{1... | collective-permute-start | bytes 3145736 | tf_op jit(solution)/shard_map/ppermute | solution.py:20
  72.8 39.8 %collective-permute-start.5 = (bf16[512,1024]{0,1:T(8,128)(2,1)}, bf16[512,1024]{0,1:T(8,128)(2,1)}, u32[]{:S(2)}, u32[]{:S(2)}) collective-permute-start(bf16[512,1024]{0,1:T(8,128)(2,1)} %pad_maximum_fusion.28), channel_id=1, source_target_pairs={{0,8},{4,12},{8,0},{12,4},{1,9},{5,13},{9,1},{13,5},{2,10},{6,14},... | collective-permute-start | bytes 3145736 | tf_op jit(solution)/shard_map/ppermute | solution.py:24
  91.0 178.1 %collective-permute-start.23 = (bf16[512,2048]{1,0:T(8,128)(2,1)}, bf16[512,2048]{1,0:T(8,128)(2,1)}, u32[]{:S(2)}, u32[]{:S(2)}) collective-permute-start(bf16[512,2048]{1,0:T(8,128)(2,1)} %get-tuple-element.105), channel_id=1, source_target_pairs={{0,16},{16,0},{1,17},{17,1},{2,18},{18,2},{3,19},{19,3},{4,20},{20... | collective-permute-start | bytes 6291464 | tf_op jit(solution)/shard_map/ppermute | solution.py:28
  91.4 60.3 %collective-permute-start.10 = (bf16[512,512]{1,0:T(8,128)(2,1)}, bf16[512,512]{1,0:T(8,128)(2,1)}, u32[]{:S(2)}, u32[]{:S(2)}) collective-permute-start(bf16[512,512]{1,0:T(8,128)(2,1)} %collective-permute-done.9), channel_id=1, source_target_pairs={{0,4},{4,0},{8,12},{12,8},{1,5},{5,1},{9,13},{13,9},{2,6},{6,2},{1... | collective-permute-start | bytes 1572872 | tf_op jit(solution)/shard_map/ppermute | solution.py:20
  112.6 31.2 %collective-permute-start.4 = (bf16[512,1024]{0,1:T(8,128)(2,1)}, bf16[512,1024]{0,1:T(8,128)(2,1)}, u32[]{:S(2)}, u32[]{:S(2)}) collective-permute-start(bf16[512,1024]{0,1:T(8,128)(2,1)} %pad_maximum_fusion.28), channel_id=1, source_target_pairs={{0,4},{4,0},{8,12},{12,8},{1,5},{5,1},{9,13},{13,9},{2,6},{6,2},{1... | collective-permute-start | bytes 3145736 | tf_op jit(solution)/shard_map/ppermute | solution.py:20
  112.6 31.2 %collective-permute-start.6 = (bf16[512,1024]{0,1:T(8,128)(2,1)}, bf16[512,1024]{0,1:T(8,128)(2,1)}, u32[]{:S(2)}, u32[]{:S(2)}) collective-permute-start(bf16[512,1024]{0,1:T(8,128)(2,1)} %collective-permute-done.5), channel_id=1, source_target_pairs={{0,4},{4,0},{8,12},{12,8},{1,5},{5,1},{9,13},{13,9},{2,6},{6,2},{1... | collective-permute-start | bytes 3145736 | tf_op jit(solution)/shard_map/ppermute | solution.py:20
  157.6 34.7 %collective-permute-start.42 = (bf16[128,2048]{1,0:T(8,128)(2,1)}, bf16[128,2048]{1,0:T(8,128)(2,1)}, u32[]{:S(2)}, u32[]{:S(2)}) collective-permute-start(bf16[128,2048]{1,0:T(8,128)(2,1)} %get-tuple-element.203), channel_id=1, source_target_pairs={{0,1},{4,5},{8,9},{12,13},{16,17},{20,21},{24,25},{28,29}} | collective-permute-start | bytes 1572872 | tf_op jit(solution)/shard_map/ppermute | solution.py:137
  161.8 30.5 %collective-permute-start.45 = (bf16[128,2048]{1,0:T(8,128)(2,1)}, bf16[128,2048]{1,0:T(8,128)(2,1)}, u32[]{:S(2)}, u32[]{:S(2)}) collective-permute-start(bf16[128,2048]{1,0:T(8,128)(2,1)} %get-tuple-element.204), channel_id=1, source_target_pairs={{3,2},{7,6},{11,10},{15,14},{19,18},{23,22},{27,26},{31,30}} | collective-permute-start | bytes 1572872 | tf_op jit(solution)/shard_map/ppermute | solution.py:138
  237.5 46.1 %collective-permute-start.25 = (bf16[2048,512]{1,0:T(8,128)(2,1)}, bf16[2048,512]{1,0:T(8,128)(2,1)}, u32[]{:S(2)}, u32[]{:S(2)}) collective-permute-start(bf16[2048,512]{1,0:T(8,128)(2,1)} %get-tuple-element.103), channel_id=1, source_target_pairs={{0,16},{16,0},{1,17},{17,1},{2,18},{18,2},{3,19},{19,3},{4,20},{20... | collective-permute-start | bytes 6291464 | tf_op jit(solution)/shard_map/ppermute | solution.py:28
  269.1 37.5 %collective-permute-start.24 = (bf16[512,2048]{1,0:T(8,128)(2,1)}, bf16[512,2048]{1,0:T(8,128)(2,1)}, u32[]{:S(2)}, u32[]{:S(2)}) collective-permute-start(bf16[512,2048]{1,0:T(8,128)(2,1)} %collective-permute-done.23), channel_id=1, source_target_pairs={{0,4},{4,0},{8,12},{12,8},{1,5},{5,1},{9,13},{13,9},{2,6},{6,2},{1... | collective-permute-start | bytes 6291464 | tf_op jit(solution)/shard_map/ppermute | solution.py:20
  283.6 31.9 %collective-permute-start.26 = (bf16[2048,512]{1,0:T(8,128)(2,1)}, bf16[2048,512]{1,0:T(8,128)(2,1)S(1)}, u32[]{:S(2)}, u32[]{:S(2)}) collective-permute-start(bf16[2048,512]{1,0:T(8,128)(2,1)} %collective-permute-done.25), channel_id=1, source_target_pairs={{0,4},{4,0},{8,12},{12,8},{1,5},{5,1},{9,13},{13,9},{2,6},{6,2},{1... | collective-permute-start | bytes 6291464 | tf_op jit(solution)/shard_map/ppermute | solution.py:20
  459.3 32.4 %collective-permute-start.76 = (bf16[128,2048]{1,0:T(8,128)(2,1)S(1)}, bf16[128,2048]{1,0:T(8,128)(2,1)S(1)}, u32[]{:S(2)}, u32[]{:S(2)}) collective-permute-start(bf16[128,2048]{1,0:T(8,128)(2,1)S(1)} %collective-permute-done.72), channel_id=1, source_target_pairs={{1,0},{2,1},{5,4},{6,5},{9,8},{10,9},{13,12},{14,13},{17,16},{18,1... | collective-permute-start | bytes 1572872 | tf_op jit(solution)/shard_map/ppermute | solution.py:151
  460.6 32.4 %collective-permute-start.75 = (bf16[128,2048]{1,0:T(8,128)(2,1)S(1)}, bf16[128,2048]{1,0:T(8,128)(2,1)S(1)}, u32[]{:S(2)}, u32[]{:S(2)}) collective-permute-start(bf16[128,2048]{1,0:T(8,128)(2,1)S(1)} %collective-permute-done.74), channel_id=1, source_target_pairs={{2,3},{6,7},{10,11},{14,15},{18,19},{22,23},{26,27},{30,31}} | collective-permute-start | bytes 1572872 | tf_op jit(solution)/shard_map/ppermute | solution.py:150
  469.3 191.7 %collective-permute-start.36 = (bf16[128,2048]{1,0:T(8,128)(2,1)}, bf16[128,2048]{1,0:T(8,128)(2,1)}, u32[]{:S(2)}, u32[]{:S(2)}) collective-permute-start(bf16[128,2048]{1,0:T(8,128)(2,1)} %collective-permute-done.35), channel_id=1, source_target_pairs={{2,3},{6,7},{10,11},{14,15},{18,19},{22,23},{26,27},{30,31}} | collective-permute-start | bytes 1572872 | tf_op jit(solution)/shard_map/ppermute | solution.py:150
  472.7 197.4 %collective-permute-start.38 = (bf16[128,2048]{1,0:T(8,128)(2,1)}, bf16[128,2048]{1,0:T(8,128)(2,1)}, u32[]{:S(2)}, u32[]{:S(2)}) collective-permute-start(bf16[128,2048]{1,0:T(8,128)(2,1)} %collective-permute-done.37), channel_id=1, source_target_pairs={{1,0},{5,4},{9,8},{13,12},{17,16},{21,20},{25,24},{29,28}} | collective-permute-start | bytes 1572872 | tf_op jit(solution)/shard_map/ppermute | solution.py:151
  480.6 63.7 %collective-permute-start.51 = (bf16[128,2048]{1,0:T(8,128)(2,1)}, bf16[128,2048]{1,0:T(8,128)(2,1)}, u32[]{:S(2)}, u32[]{:S(2)}) collective-permute-start(bf16[128,2048]{1,0:T(8,128)(2,1)} %collective-permute-done.50), channel_id=1, source_target_pairs={{2,3},{6,7},{10,11},{14,15},{18,19},{22,23},{26,27},{30,31}} | collective-permute-start | bytes 1572872 | tf_op jit(solution)/shard_map/ppermute | solution.py:150
  491.7 62.3 %collective-permute-start.53 = (bf16[128,2048]{1,0:T(8,128)(2,1)}, bf16[128,2048]{1,0:T(8,128)(2,1)}, u32[]{:S(2)}, u32[]{:S(2)}) collective-permute-start(bf16[128,2048]{1,0:T(8,128)(2,1)} %collective-permute-done.52), channel_id=1, source_target_pairs={{1,0},{5,4},{9,8},{13,12},{17,16},{21,20},{25,24},{29,28}} | collective-permute-start | bytes 1572872 | tf_op jit(solution)/shard_map/ppermute | solution.py:151
  493.0 29.0 %collective-permute-start.77 = (bf16[128,2048]{1,0:T(8,128)(2,1)S(1)}, bf16[128,2048]{1,0:T(8,128)(2,1)S(1)}, u32[]{:S(2)}, u32[]{:S(2)}) collective-permute-start(bf16[128,2048]{1,0:T(8,128)(2,1)S(1)} %collective-permute-done.76), channel_id=1, source_target_pairs={{1,0},{5,4},{9,8},{13,12},{17,16},{21,20},{25,24},{29,28}} | collective-permute-start | bytes 1572872 | tf_op jit(solution)/shard_map/ppermute | solution.py:151
  586.3 77.4 %collective-permute-start.92 = (bf16[128,2048]{1,0:T(8,128)(2,1)}, bf16[128,2048]{1,0:T(8,128)(2,1)S(1)}, u32[]{:S(2)}, u32[]{:S(2)}) collective-permute-start(bf16[128,2048]{1,0:T(8,128)(2,1)} %get-tuple-element.141), channel_id=1, source_target_pairs={{0,1},{4,5},{8,9},{12,13},{16,17},{20,21},{24,25},{28,29}} | collective-permute-start | bytes 1572872 | tf_op jit(solution)/shard_map/ppermute | solution.py:137
  588.0 75.8 %collective-permute-start.95 = (bf16[128,2048]{1,0:T(8,128)(2,1)}, bf16[128,2048]{1,0:T(8,128)(2,1)}, u32[]{:S(2)}, u32[]{:S(2)}) collective-permute-start(bf16[128,2048]{1,0:T(8,128)(2,1)} %get-tuple-element.142), channel_id=1, source_target_pairs={{3,2},{7,6},{11,10},{15,14},{19,18},{23,22},{27,26},{31,30}} | collective-permute-start | bytes 1572872 | tf_op jit(solution)/shard_map/ppermute | solution.py:138
  613.2 53.3 %collective-permute-start.54 = (bf16[128,2048]{1,0:T(8,128)(2,1)}, bf16[128,2048]{1,0:T(8,128)(2,1)}, u32[]{:S(2)}, u32[]{:S(2)}) collective-permute-start(bf16[128,2048]{1,0:T(8,128)(2,1)} %get-tuple-element.183), channel_id=1, source_target_pairs={{0,1},{4,5},{8,9},{12,13},{16,17},{20,21},{24,25},{28,29}} | collective-permute-start | bytes 1572872 | tf_op jit(solution)/shard_map/ppermute | solution.py:137
  663.8 64.4 %collective-permute-start.78 = (bf16[2,512,1024]{2,1,0:T(8,128)(2,1)S(1)}, bf16[2,512,1024]{2,1,0:T(8,128)(2,1)S(1)}, u32[]{:S(2)}, u32[]{:S(2)}) collective-permute-start(bf16[2,512,1024]{2,1,0:T(8,128)(2,1)S(1)} %pad_maximum_fusion.18), channel_id=1, source_target_pairs={{0,4},{4,0},{8,12},{12,8},{1,5},{5,1},{9,13},{13,9},{2,6},{6,2},{1... | collective-permute-start | bytes 6291464 | tf_op jit(solution)/shard_map/ppermute | solution.py:20
  728.5 39.2 %collective-permute-start.79 = (bf16[512,1024]{1,0:T(8,128)(2,1)S(1)}, bf16[512,1024]{1,0:T(8,128)(2,1)S(1)}, u32[]{:S(2)}, u32[]{:S(2)}) collective-permute-start(bf16[512,1024]{1,0:T(8,128)(2,1)S(1)} %fusion.153), channel_id=1, source_target_pairs={{0,8},{4,12},{8,0},{12,4},{1,9},{5,13},{9,1},{13,5},{2,10},{6,14},... | collective-permute-start | bytes 3145736 | tf_op jit(solution)/shard_map/ppermute | solution.py:24
  753.8 141.0 %collective-permute-start.146 = (bf16[2048,1024]{1,0:T(8,128)(2,1)}, bf16[2048,1024]{1,0:T(8,128)(2,1)}, u32[]{:S(2)}, u32[]{:S(2)}) collective-permute-start(bf16[2048,1024]{1,0:T(8,128)(2,1)} %slice.541), channel_id=1, source_target_pairs={{0,4},{4,0},{8,12},{12,8},{1,5},{5,1},{9,13},{13,9},{2,6},{6,2},{1... | collective-permute-start | bytes 12582920 | tf_op jit(solution)/shard_map/ppermute | solution.py:20
  755.2 153.7 %collective-permute-start.142 = (bf16[1024,2048]{1,0:T(8,128)(2,1)}, bf16[1024,2048]{1,0:T(8,128)(2,1)}, u32[]{:S(2)}, u32[]{:S(2)}) collective-permute-start(bf16[1024,2048]{1,0:T(8,128)(2,1)} %slice.536), channel_id=1, source_target_pairs={{0,4},{4,0},{8,12},{12,8},{1,5},{5,1},{9,13},{13,9},{2,6},{6,2},{1... | collective-permute-start | bytes 12582920 | tf_op jit(solution)/shard_map/ppermute | solution.py:20
  766.1 108.7 %collective-permute-start.63 = (bf16[128,2048]{1,0:T(8,128)(2,1)}, bf16[128,2048]{1,0:T(8,128)(2,1)}, u32[]{:S(2)}, u32[]{:S(2)}) collective-permute-start(bf16[128,2048]{1,0:T(8,128)(2,1)} %collective-permute-done.62), channel_id=1, source_target_pairs={{2,3},{6,7},{10,11},{14,15},{18,19},{22,23},{26,27},{30,31}} | collective-permute-start | bytes 1572872 | tf_op jit(solution)/shard_map/ppermute | solution.py:150
  777.3 99.2 %collective-permute-start.65 = (bf16[128,2048]{1,0:T(8,128)(2,1)}, bf16[128,2048]{1,0:T(8,128)(2,1)}, u32[]{:S(2)}, u32[]{:S(2)}) collective-permute-start(bf16[128,2048]{1,0:T(8,128)(2,1)} %collective-permute-done.64), channel_id=1, source_target_pairs={{1,0},{5,4},{9,8},{13,12},{17,16},{21,20},{25,24},{29,28}} | collective-permute-start | bytes 1572872 | tf_op jit(solution)/shard_map/ppermute | solution.py:151
  802.4 89.6 %collective-permute-start.80 = (bf16[128,2048]{1,0:T(8,128)(2,1)}, bf16[128,2048]{1,0:T(8,128)(2,1)}, u32[]{:S(2)}, u32[]{:S(2)}) collective-permute-start(bf16[128,2048]{1,0:T(8,128)(2,1)} %get-tuple-element.123), channel_id=1, source_target_pairs={{0,1},{4,5},{8,9},{12,13},{16,17},{20,21},{24,25},{28,29}} | collective-permute-start | bytes 1572872 | tf_op jit(solution)/shard_map/ppermute | solution.py:137
  892.0 64.6 %collective-permute-start.104 = (bf16[2,512,1024]{2,1,0:T(8,128)(2,1)}, bf16[2,512,1024]{2,1,0:T(8,128)(2,1)}, u32[]{:S(2)}, u32[]{:S(2)}) collective-permute-start(bf16[2,512,1024]{2,1,0:T(8,128)(2,1)} %pad_maximum_fusion.21), channel_id=1, source_target_pairs={{0,4},{4,0},{8,12},{12,8},{1,5},{5,1},{9,13},{13,9},{2,6},{6,2},{1... | collective-permute-start | bytes 6291464 | tf_op jit(solution)/shard_map/ppermute | solution.py:20
  894.8 39.1 %collective-permute-start.81 = (bf16[128,2048]{1,0:T(8,128)(2,1)}, bf16[128,2048]{1,0:T(8,128)(2,1)}, u32[]{:S(2)}, u32[]{:S(2)}) collective-permute-start(bf16[128,2048]{1,0:T(8,128)(2,1)} %get-tuple-element.121), channel_id=1, source_target_pairs={{0,1},{1,2},{4,5},{5,6},{8,9},{9,10},{12,13},{13,14},{16,17},{17,1... | collective-permute-start | bytes 1572872 | tf_op jit(solution)/shard_map/ppermute | solution.py:137
  901.1 33.4 %collective-permute-start.84 = (bf16[128,2048]{1,0:T(8,128)(2,1)S(1)}, bf16[128,2048]{1,0:T(8,128)(2,1)}, u32[]{:S(2)}, u32[]{:S(2)}) collective-permute-start(bf16[128,2048]{1,0:T(8,128)(2,1)S(1)} %get-tuple-element.122), channel_id=1, source_target_pairs={{3,2},{2,1},{7,6},{6,5},{11,10},{10,9},{15,14},{14,13},{19,18},{18... | collective-permute-start | bytes 1572872 | tf_op jit(solution)/shard_map/ppermute | solution.py:138
  920.9 56.1 %collective-permute-start.147 = (bf16[2048,512]{1,0:T(8,128)(2,1)S(1)}, bf16[2048,512]{1,0:T(8,128)(2,1)S(1)}, u32[]{:S(2)}, u32[]{:S(2)}) collective-permute-start(bf16[2048,512]{1,0:T(8,128)(2,1)S(1)} %slice.731), channel_id=1, source_target_pairs={{0,16},{16,0},{1,17},{17,1},{2,18},{18,2},{3,19},{19,3},{4,20},{20... | collective-permute-start | bytes 6291464 | tf_op jit(solution)/shard_map/ppermute | solution.py:28
  933.9 87.8 %collective-permute-start.143 = (bf16[512,2048]{1,0:T(8,128)(2,1)S(1)}, bf16[512,2048]{1,0:T(8,128)(2,1)}, u32[]{:S(2)}, u32[]{:S(2)}) collective-permute-start(bf16[512,2048]{1,0:T(8,128)(2,1)S(1)} %slice.732), channel_id=1, source_target_pairs={{0,16},{16,0},{1,17},{17,1},{2,18},{18,2},{3,19},{19,3},{4,20},{20... | collective-permute-start | bytes 6291464 | tf_op jit(solution)/shard_map/ppermute | solution.py:28
  1001.1 38.3 %collective-permute-start.127 = (bf16[1024,512]{1,0:T(8,128)(2,1)S(1)}, bf16[1024,512]{1,0:T(8,128)(2,1)}, u32[]{:S(2)}, u32[]{:S(2)}) collective-permute-start(bf16[1024,512]{1,0:T(8,128)(2,1)S(1)} %slice.520), channel_id=1, source_target_pairs={{0,4},{4,0},{8,12},{12,8},{1,5},{5,1},{9,13},{13,9},{2,6},{6,2},{1... | collective-permute-start | bytes 3145736 | tf_op jit(solution)/shard_map/ppermute | solution.py:20
  1001.4 42.3 %collective-permute-start.131 = (bf16[1024,512]{1,0:T(8,128)(2,1)}, bf16[1024,512]{1,0:T(8,128)(2,1)}, u32[]{:S(2)}, u32[]{:S(2)}) collective-permute-start(bf16[1024,512]{1,0:T(8,128)(2,1)} %slice.524), channel_id=1, source_target_pairs={{0,4},{4,0},{8,12},{12,8},{1,5},{5,1},{9,13},{13,9},{2,6},{6,2},{1... | collective-permute-start | bytes 3145736 | tf_op jit(solution)/shard_map/ppermute | solution.py:20
  1044.2 118.5 %collective-permute-start.148 = (bf16[2048,512]{1,0:T(8,128)(2,1)}, bf16[2048,512]{1,0:T(8,128)(2,1)}, u32[]{:S(2)}, u32[]{:S(2)}) collective-permute-start(bf16[2048,512]{1,0:T(8,128)(2,1)} %fusion.38), channel_id=1, source_target_pairs={{0,8},{4,12},{8,0},{12,4},{1,9},{5,13},{9,1},{13,5},{2,10},{6,14},... | collective-permute-start | bytes 6291464 | tf_op jit(solution)/shard_map/ppermute | solution.py:24
  1048.5 129.2 %collective-permute-start.144 = (bf16[512,2048]{1,0:T(8,128)(2,1)}, bf16[512,2048]{1,0:T(8,128)(2,1)}, u32[]{:S(2)}, u32[]{:S(2)}) collective-permute-start(bf16[512,2048]{1,0:T(8,128)(2,1)} %fusion.39), channel_id=1, source_target_pairs={{0,8},{4,12},{8,0},{12,4},{1,9},{5,13},{9,1},{13,5},{2,10},{6,14},... | collective-permute-start | bytes 6291464 | tf_op jit(solution)/shard_map/ppermute | solution.py:24
  1055.2 82.8 %collective-permute-start.132 = (bf16[512,512]{1,0:T(8,128)(2,1)}, bf16[512,512]{1,0:T(8,128)(2,1)}, u32[]{:S(2)}, u32[]{:S(2)}) collective-permute-start(bf16[512,512]{1,0:T(8,128)(2,1)} %slice.734), channel_id=1, source_target_pairs={{0,16},{16,0},{1,17},{17,1},{2,18},{18,2},{3,19},{19,3},{4,20},{20... | collective-permute-start | bytes 1572872 | tf_op jit(solution)/shard_map/ppermute | solution.py:28
  1065.2 119.9 %collective-permute-start.87 = (bf16[128,2048]{1,0:T(8,128)(2,1)S(1)}, bf16[128,2048]{1,0:T(8,128)(2,1)S(1)}, u32[]{:S(2)}, u32[]{:S(2)}) collective-permute-start(bf16[128,2048]{1,0:T(8,128)(2,1)S(1)} %pad_maximum_fusion.32), channel_id=1, source_target_pairs={{0,1},{1,2},{2,3},{4,5},{5,6},{6,7},{8,9},{9,10},{10,11},{12,13},{... | collective-permute-start | bytes 1572872 | tf_op jit(solution)/shard_map/ppermute | solution.py:150
  1068.5 68.1 %collective-permute-start.119 = (f32[6,2048]{1,0:T(8,128)S(1)}, f32[6,2048]{1,0:T(8,128)S(1)}, u32[]{:S(2)}, u32[]{:S(2)}) collective-permute-start(f32[6,2048]{1,0:T(8,128)S(1)} %fusion.222), channel_id=1, source_target_pairs={{0,8},{4,12},{8,0},{12,4},{1,9},{5,13},{9,1},{13,5},{2,10},{6,14},... | collective-permute-start | bytes 147464 | tf_op jit(solution)/shard_map/ppermute | solution.py:24
  1136.6 49.3 %collective-permute-start.86 = (bf16[128,2048]{1,0:T(8,128)(2,1)S(1)}, bf16[128,2048]{1,0:T(8,128)(2,1)S(1)}, u32[]{:S(2)}, u32[]{:S(2)}) collective-permute-start(bf16[128,2048]{1,0:T(8,128)(2,1)S(1)} %pad_maximum_fusion.32), channel_id=1, source_target_pairs={{1,0},{2,1},{3,2},{5,4},{6,5},{7,6},{9,8},{10,9},{11,10},{13,12},{... | collective-permute-start | bytes 1572872 | tf_op jit(solution)/shard_map/ppermute | solution.py:151
  1187.5 63.8 %collective-permute-start.149 = (bf16[2048,512]{1,0:T(8,128)(2,1)S(1)}, bf16[2048,512]{1,0:T(8,128)(2,1)S(1)}, u32[]{:S(2)}, u32[]{:S(2)}) collective-permute-start(bf16[2048,512]{1,0:T(8,128)(2,1)S(1)} %add_convert_fusion), channel_id=1, source_target_pairs={{0,4},{4,0},{8,12},{12,8},{1,5},{5,1},{9,13},{13,9},{2,6},{6,2},{1... | collective-permute-start | bytes 6291464 | tf_op jit(solution)/shard_map/ppermute | solution.py:20
  1200.6 55.6 %collective-permute-start.145 = (bf16[512,2048]{1,0:T(8,128)(2,1)S(1)}, bf16[512,2048]{1,0:T(8,128)(2,1)S(1)}, u32[]{:S(2)}, u32[]{:S(2)}) collective-permute-start(bf16[512,2048]{1,0:T(8,128)(2,1)S(1)} %add_convert_fusion.1), channel_id=1, source_target_pairs={{0,4},{4,0},{8,12},{12,8},{1,5},{5,1},{9,13},{13,9},{2,6},{6,2},{1... | collective-permute-start | bytes 6291464 | tf_op jit(solution)/shard_map/ppermute | solution.py:20
  (317 other events, 5673.3 us)

commit v2 on v1

--- a/solution.py
+++ b/solution.py
@@ -1,11 +1,14 @@
 import jax
 import jax.numpy as jnp
 from jax import lax
+from jax.experimental import pallas as pl
+from jax.experimental.pallas import tpu as pltpu
 from jax.sharding import PartitionSpec as P
 
 HD = 128
 NORM_EPS = 1e-05
 MASKED = -1e30
+LOG2E = 1.4426950408889634
 F32 = jnp.float32
 BF16 = jnp.bfloat16
 
@@ -83,13 +86,11 @@
     )
 
 
-def roll_rows(values):
+def mix_rows(values):
     n = lax.axis_size("tp")
     z = lax.axis_index("tp")
     size = values.shape[0] // n
-    return jnp.concatenate(
-        [piece(values, lax.rem(z + k, n) * size, size, 0) for k in range(n)], axis=0
-    )
+    return jnp.concatenate([piece(values, (z ^ k) * size, size, 0) for k in range(n)], axis=0)
 
 
 def gather_weight(values, axis):
@@ -121,79 +122,205 @@
     return jnp.concatenate([first, second], axis=axis).astype(F32)
 
 
+def tp_swap(values, bit):
+    return lax.ppermute(values, "tp", xor_pairs(lax.axis_size("tp"), bit))
+
+
 def line_reduce(partial):
     n = lax.axis_size("tp")
     size = partial.shape[0] // n
-
-    def block(k):
-        return partial[k * size : (k + 1) * size]
-
-    ahead = behind = None
-    for step in range(1, n):
-        up, down = block(n - step), block(step)
-        if ahead is not None:
-            up = (up.astype(F32) + ahead.astype(F32)).astype(BF16)
-            down = (down.astype(F32) + behind.astype(F32)).astype(BF16)
-        ahead = lax.ppermute(up, "tp", [(j, j + 1) for j in range(step)])
-        behind = lax.ppermute(down, "tp", [(n - 1 - j, n - 2 - j) for j in range(step)])
-    total = block(0).astype(F32)
-    if ahead is not None:
-        total = total + ahead.astype(F32) + behind.astype(F32)
-    return total
+    blocks = [partial[k * size : (k + 1) * size] for k in range(n)]
+    if n == 4:
+        got = tp_swap(blocks[3], 1)
+        passed = (blocks[2].astype(F32) + got.astype(F32)).astype(BF16)
+        far = tp_swap(passed, 2)
+        near = tp_swap(blocks[1], 1)
+        return blocks[0].astype(F32) + near.astype(F32) + far.astype(F32)
+    bit = 1
+    order = list(range(n))
+    held = dict(zip(order, blocks))
+    while bit < n:
+        away = [k for k in held if k & bit]
+        got = tp_swap(jnp.concatenate([held[k] for k in away], axis=0), bit)
+        for j, k in enumerate(away):
+            summed = held[k ^ bit].astype(F32) + got[j * size : (j + 1) * size].astype(F32)
+            held[k ^ bit] = summed.astype(BF16)
+            del held[k]
+        bit *= 2
+    return held[0].astype(F32)
 
 
 def line_gather(own):
     n = lax.axis_size("tp")
-    z = lax.axis_index("tp")
-    ahead, behind = [own], [own]
-    for k in range(1, n):
-        ahead.append(lax.ppermute(ahead[-1], "tp", [(j, j + 1) for j in range(k - 1, n - 1)]))
-        behind.append(lax.ppermute(behind[-1], "tp", [(j, j - 1) for j in range(1, n - k + 1)]))
-    return [own] + [jnp.where(z + k < n, behind[k], ahead[n - k]) for k in range(1, n)]
+    if n == 4:
+        far = tp_swap(own, 2)
+        near = tp_swap(own, 1)
+        return [own, near, far, tp_swap(far, 1)]
+    blocks = [own]
+    bit = 1
+    while bit < n:
+        size = own.shape[0]
+        got = tp_swap(jnp.concatenate(blocks, axis=0), bit)
+        blocks = blocks + [got[k * size : (k + 1) * size] for k in range(bit)]
+        bit *= 2
+    return blocks
 
 
 def natural_rows(blocks):
     n = len(blocks)
     z = lax.axis_index("tp")
     size = blocks[0].shape[0]
-    doubled = jnp.concatenate(blocks, axis=0)
-    return jnp.concatenate(
-        [piece(doubled, lax.rem(j - z + n, n) * size, size, 0) for j in range(n)], axis=0
-    )
-
-
-def scores_of(queries, keys, allowed):
-    raw = jnp.einsum("qhe,khe->hqk", queries, keys, preferred_element_type=F32) * HD ** (-0.5)
-    return jnp.where(allowed[None], raw, MASKED)
-
-
-def attend(queries, keys, values, allowed):
-    scores = scores_of(queries, keys, allowed)
-    row_max = jnp.max(scores, axis=-1, keepdims=True)
-    exp_scores = jnp.exp(scores - row_max)
-    row_total = jnp.sum(exp_scores, axis=-1, keepdims=True)
-    weights = (exp_scores / row_total).astype(BF16)
-    attended = jnp.einsum("hqk,khe->qhe", weights, values, preferred_element_type=F32)
-    return attended.astype(BF16), row_max + jnp.log(row_total)
-
-
-def attend_back(queries, keys, values, allowed, log_total, grad_att):
-    scores = scores_of(queries, keys, allowed)
-    probs = jnp.exp(scores - log_total)
-    probs_low = probs.astype(BF16)
-    grad_values = jnp.einsum("hqk,qhe->khe", probs_low, grad_att, preferred_element_type=F32)
-    grad_probs = jnp.einsum("qhe,khe->hqk", grad_att, values, preferred_element_type=F32)
-    grad_scores = (
-        probs * (grad_probs - jnp.sum(probs * grad_probs, axis=-1, keepdims=True))
-    ).astype(BF16)
+    mixed = jnp.concatenate(blocks, axis=0)
+    return jnp.concatenate([piece(mixed, (j ^ z) * size, size, 0) for j in range(n)], axis=0)
+
+
+def fwd_kernel(live, q, kv0, kv1, kv2, kv3, kseg, qseg, kpos, qpos, out, lse, m_s, l_s, acc_s):
+    queries = q[...]
+    rate = HD ** (-0.5) * LOG2E
+
+    def scores(kv, b):
+        t = dot_t(kv[0], queries) * rate
+        allowed = kseg[b] == qseg[...]
+        if b == 0:
+            allowed = allowed & (kpos[...] <= qpos[...])
+        return jnp.where(allowed, t, MASKED)
+
+    t = scores(kv0, 0)
+    top = jnp.max(t, axis=0, keepdims=True)
+    p = jnp.exp2(t - top)
+    m_s[...] = top
+    l_s[...] = jnp.sum(p, axis=0, keepdims=True)
+    acc_s[...] = t_dot(kv0[1], p.astype(BF16))
+    for b, kv in ((1, kv1), (2, kv2), (3, kv3)):
+
+        @pl.when(live[b] > 0)
+        def _(b=b, kv=kv):
+            t = scores(kv, b)
+            old = m_s[...]
+            top = jnp.maximum(old, jnp.max(t, axis=0, keepdims=True))
+            p = jnp.exp2(t - top)
+            fade = jnp.exp2(old - top)
+            m_s[...] = top
+            l_s[...] = l_s[...] * fade + jnp.sum(p, axis=0, keepdims=True)
+            acc_s[...] = acc_s[...] * fade + t_dot(kv[1], p.astype(BF16))
+
+    total = l_s[...]
+    out[...] = (acc_s[...] / total).T.astype(BF16)
+    lse[0] = m_s[...] + jnp.log2(total)
+
+
+def bwd_kernel(
+    live, q, kv0, kv1, kv2, kv3, kseg, qseg, kpos, qpos, att, grad, lse, gq, near, far, gq_s
+):
+    queries = q[...]
+    rate = HD ** (-0.5) * LOG2E
     factor = HD ** (-0.5)
-    grad_queries = jnp.einsum("hqk,khe->qhe", grad_scores, keys, preferred_element_type=F32)
-    grad_keys = jnp.einsum("hqk,qhe->khe", grad_scores, queries, preferred_element_type=F32)
-    return (
-        (grad_queries * factor).astype(BF16),
-        (grad_keys * factor).astype(BF16),
-        grad_values.astype(BF16),
-    )
+    grad_out = grad[...]
+    product = grad_out.astype(F32) * att[...].astype(F32)
+    delta = jnp.sum(product.T, axis=0, keepdims=True)
+    total = lse[0]
+
+    def grads(kv, b):
+        t = dot_t(kv[0], queries) * rate
+        allowed = kseg[b] == qseg[...]
+        if b == 0:
+            allowed = allowed & (kpos[...] <= qpos[...])
+        p = jnp.exp2(jnp.where(allowed, t, MASKED) - total)
+        gv = dot(p.astype(BF16), grad_out)
+        gp = dot_t(kv[1], grad_out)
+        gs = (p * (gp - delta)).astype(BF16)
+        gk = dot(gs, queries) * factor
+        return gk.astype(BF16), gv.astype(BF16), t_dot(kv[0], gs)
+
+    gk, gv, turned = grads(kv0, 0)
+    near[0, 0] = gk
+    near[0, 1] = gv
+    gq_s[...] = turned
+    for b, kv, place, slot in ((1, kv1, far, 0), (2, kv2, near, 1), (3, kv3, far, 1)):
+
+        @pl.when(live[b] > 0)
+        def _(b=b, kv=kv, place=place, slot=slot):
+            gk, gv, turned = grads(kv, b)
+            place[slot, 0] = gk
+            place[slot, 1] = gv
+            gq_s[...] += turned
+
+        @pl.when(live[b] == 0)
+        def _(place=place, slot=slot):
+            place[slot] = jnp.zeros(place.shape[1:], BF16)
+
+    gq[...] = (gq_s[...] * factor).T.astype(BF16)
+
+
+def attend_specs(span):
+    def whole(*shape):
+        return pl.BlockSpec(shape, lambda h, *_: (0,) * len(shape))
+
+    head = pl.BlockSpec((span, HD), lambda h, *_: (0, h))
+    pair = pl.BlockSpec((2, span, HD), lambda h, *_: (0, 0, h))
+    stat = pl.BlockSpec((1, 1, span), lambda h, *_: (h, 0, 0))
+    both = pl.BlockSpec((2, 2, span, HD), lambda h, *_: (0, 0, 0, h))
+    ins = [head] + [pair] * 4 + [whole(4, span, 1), whole(1, span), whole(span, 1), whole(1, span)]
+    return head, stat, both, ins
+
+
+def attend(live, queries, kvs, marks):
+    span, local_width = queries.shape
+    heads = local_width // HD
+    head, stat, both, ins = attend_specs(span)
+    return pl.pallas_call(
+        fwd_kernel,
+        grid_spec=pltpu.PrefetchScalarGridSpec(
+            num_scalar_prefetch=1,
+            grid=(heads,),
+            in_specs=ins,
+            out_specs=[head, stat],
+            scratch_shapes=[
+                pltpu.VMEM((1, span), F32),
+                pltpu.VMEM((1, span), F32),
+                pltpu.VMEM((HD, span), F32),
+            ],
+        ),
+        out_shape=[
+            jax.ShapeDtypeStruct((span, local_width), BF16),
+            jax.ShapeDtypeStruct((heads, 1, span), F32),
+        ],
+        compiler_params=pltpu.CompilerParams(vmem_limit_bytes=48 * 2**20),
+        cost_estimate=pl.CostEstimate(
+            flops=16 * heads * span * span * HD,
+            bytes_accessed=10 * span * local_width * 2,
+            transcendentals=4 * heads * span * span,
+        ),
+        name="attend",
+    )(live, queries, *kvs, *marks)
+
+
+def attend_back(live, queries, kvs, marks, attended, grad_att, log_total):
+    span, local_width = queries.shape
+    heads = local_width // HD
+    head, stat, both, ins = attend_specs(span)
+    return pl.pallas_call(
+        bwd_kernel,
+        grid_spec=pltpu.PrefetchScalarGridSpec(
+            num_scalar_prefetch=1,
+            grid=(heads,),
+            in_specs=ins + [head, head, stat],
+            out_specs=[head, both, both],
+            scratch_shapes=[pltpu.VMEM((HD, span), F32)],
+        ),
+        out_shape=[
+            jax.ShapeDtypeStruct((span, local_width), BF16),
+            jax.ShapeDtypeStruct((2, 2, span, local_width), BF16),
+            jax.ShapeDtypeStruct((2, 2, span, local_width), BF16),
+        ],
+        compiler_params=pltpu.CompilerParams(vmem_limit_bytes=48 * 2**20),
+        cost_estimate=pl.CostEstimate(
+            flops=40 * heads * span * span * HD,
+            bytes_accessed=20 * span * local_width * 2,
+            transcendentals=4 * heads * span * span,
+        ),
+        name="attend_back",
+    )(live, queries, *kvs, *marks, attended, grad_att, log_total)
 
 
 def sum_pairs(values, tp_too):
@@ -232,7 +359,6 @@
     blocks = lax.axis_size("ctx")
     part = span // n
     local_width = w_qkv.shape[2]
-    heads = local_width // HD
     each = range(seqs)
 
     wk = gather_weight(w_qkv[:, 1], 0)
@@ -251,48 +377,37 @@
     bias_q, bias_v = b_qv[0].astype(F32), b_qv[1].astype(F32)
     bias_up = b_up.astype(F32)
 
-    spot = lax.rem(lax.axis_index("tp") * part + jnp.arange(span), span)
-
-    x_rows, n1, queries, kv_all, allowed, cot = [], [], [], [], [], []
-    for s in each:
-        rows = to_relative(roll_rows(block_in[s]))
+    spot = mix_rows(jnp.arange(span, dtype=jnp.int32))
+    live = jnp.stack([((cx ^ b) <= cx).astype(jnp.int32) for b in range(blocks)])
+
+    x_rows, n1, queries, kv_all, marks, cot = [], [], [], [], [], []
+    for s in each:
+        rows = to_relative(mix_rows(block_in[s]))
         x_rows.append(rows)
         normed, unused = norm_parts(rows.astype(F32))
         n1.append((normed * gain_one + shift_one).astype(BF16))
     for s in each:
         keys_here = dot(n1[s], wk).astype(BF16)
         values_here = (dot(n1[s], wv) + bias_v).astype(BF16)
-        kv = jnp.concatenate([keys_here, values_here], axis=1)
+        kv = jnp.stack([keys_here, values_here])
         kv1 = core_swap(kv)
         kv2 = y_swap(kv)
         kv3 = core_swap(kv2)
-        kv_all.append(jnp.concatenate([kv, kv1, kv2, kv3], axis=0))
+        kv_all.append((kv, kv1, kv2, kv3))
     for s in each:
         queries.append((dot(n1[s], wq) + bias_q).astype(BF16))
-        query_seg = roll_rows(piece(segments[s], cx * span, span, 0))
-        key_seg = jnp.concatenate(
-            [roll_rows(piece(segments[s], (cx ^ b) * span, span, 0)) for b in range(blocks)]
+        key_seg = jnp.stack(
+            [mix_rows(piece(segments[s], (cx ^ b) * span, span, 0)) for b in range(blocks)]
         )
-        key_pos = jnp.concatenate([(cx ^ b) * span + spot for b in range(blocks)])
-        allowed.append(
-            (query_seg[:, None] == key_seg[None, :])
-            & (key_pos[None, :] <= (cx * span + spot)[:, None])
-        )
-        valid = (query_seg != 0).astype(BF16)[:, None]
-        cot.append(to_relative(roll_rows(out_grad[s])) * valid)
-
-    def heads_of(values):
-        return values.reshape(values.shape[0], heads, HD)
-
-    def halves(s):
-        return heads_of(kv_all[s][:, :local_width]), heads_of(kv_all[s][:, local_width:])
+        marks.append((key_seg[:, :, None], key_seg[0][None, :], spot[:, None], spot[None, :]))
+        valid = (key_seg[0] != 0).astype(BF16)[:, None]
+        cot.append(to_relative(mix_rows(out_grad[s])) * valid)
 
     attended, log_total, middle = [], [], []
     n2 = []
     for s in each:
-        keys, values = halves(s)
-        out, total = attend(heads_of(queries[s]), keys, values, allowed[s])
-        attended.append(out.reshape(span, local_width))
+        out, total = attend(live, queries[s], kv_all[s], marks[s])
+        attended.append(out)
         log_total.append(total)
         summed = line_reduce(dot(attended[s], wo).astype(BF16))
         mid = x_rows[s][:part].astype(F32) + summed + bias_out
@@ -322,19 +437,14 @@
     grads, kept_one, in_rows = [], [], []
     for s in each:
         grad_att = dot_t(gm[s], wo).astype(BF16)
-        keys, values = halves(s)
-        gq, gk, gv = attend_back(
-            heads_of(queries[s]), keys, values, allowed[s], log_total[s], heads_of(grad_att)
+        gq, near, away = attend_back(
+            live, queries[s], kv_all[s], marks[s], attended[s], grad_att, log_total[s]
         )
-        gq = gq.reshape(span, local_width)
-        gkv = jnp.concatenate(
-            [gk.reshape(blocks, span, local_width), gv.reshape(blocks, span, local_width)], axis=2
-        )
-        got = core_swap(jnp.stack([gkv[1], gkv[3]]))
-        far = (gkv[2].astype(F32) + got[1].astype(F32)).astype(BF16)
-        near = gkv[0].astype(F32) + got[0].astype(F32)
-        total = (near + y_swap(far).astype(F32)).astype(BF16)
-        gk, gv = total[:, :local_width], total[:, local_width:]
+        got = core_swap(away)
+        far = (near[1].astype(F32) + got[1].astype(F32)).astype(BF16)
+        total = near[0].astype(F32) + got[0].astype(F32)
+        total = (total + y_swap(far).astype(F32)).astype(BF16)
+        gk, gv = total[0], total[1]
         grads.append((gq, gk, gv))
         summed = line_reduce((dot_t(gq, wq) + dot_t(gk, wk) + dot_t(gv, wv)).astype(BF16))
         normed, norm_scale = norm_parts(x_rows[s][:part].astype(F32))

time: 1270 us -> 1010 us (0.80)
  starting transfers between devices: 231 us -> 116 us
  other arithmetic: 208 us -> 107 us
  matrix products: 251 us -> 163 us
  waiting for transfers between devices: 472 us -> 514 us
  Pallas kernels: 0 us -> 29.4 us
  local copies, waits for them, and re-layouts: 93.6 us -> 66.8 us
    ppermute x96 -> x48, starting transfers between devices: 186 us -> 44 us  [tp_swap(): return lax.ppermute(values, 'tp', xor_pairs(lax.axis_size('tp'), bit))]
    ppermute x96 -> x48, waiting for transfers between devices: 261 us -> 357 us  [tp_swap(): return lax.ppermute(values, 'tp', xor_pairs(lax.axis_size('tp'), bit))]
    dot_general x12 -> x0, matrix products: 84 us -> none  [the longest x2 24.2 us: attend_back(): jnp.einsum('qhe,khe->hqk', grad_att, values, preferred_element_type=F32)]
    ppermute x12, waiting for transfers between devices: 132 us -> 76.4 us  [y_swap(): return lax.ppermute(values, 'ctx', xor_pairs(lax.axis_size('ctx'), 2))]
    convert_element_type x23 -> x13, other arithmetic: 42 us -> 10.1 us  [the longest x8 3.9 us: line_reduce(): passed = (blocks[2].astype(F32) + got.astype(F32)).astype(BF16)]
    reshape x8 -> x0, local copies, waits for them, and re-layouts: 29.9 us -> none  [the longest x4 17.9 us: local(): gk.reshape(blocks, span, local_width)]
    pallas_call x0 -> x4, Pallas kernels: none -> 29.4 us  [the longest x2 17.3 us: attend_back(): pl.pallas_call(bwd_kernel, grid_spec=pltpu.PrefetchScalarGridSpec(num_sca...]
    reduce_sum x2 -> x0, other arithmetic: 16.2 us -> none  [attend(): row_total = jnp.sum(exp_scores, axis=-1, keepdims=True)]
  transfers between devices with their start and end apart: 150 -> 102, of which waited for: 55 -> 43; matrix products, arithmetic and copies ran while one was open for 40% -> 30% of each run, Pallas kernels for 0% -> 3%
where the time goes in v2:
time: 1010 us; the launch traced here: 1000 us
  waiting for transfers between devices  514 us (51%)
  matrix products  163 us (16%)
  starting transfers between devices  116 us (11%)
  other arithmetic  107 us (11%)
  local copies, waits for them, and re-layouts  66.8 us (7%)
  Pallas kernels  29.4 us (3%)
    ppermute x48, waiting for transfers between devices, tp_swap(): return lax.ppermute(values, 'tp', xor_pairs(lax.axis_size('tp'), bit))  357 us
    ppermute x12, waiting for transfers between devices, y_swap(): return lax.ppermute(values, 'ctx', xor_pairs(lax.axis_size('ctx'), 2))  76.4 us
    ppermute x14, waiting for transfers between devices, x_swap(): return lax.ppermute(values, 'fsdp', X_SWAP)  70.5 us
    dot_general x12, matrix products, dot_t(): lax.dot_general(a, b, (((1,), (1,)), ((), ())), preferred_element_type=F32)  66.4 us
    dot_general x12, matrix products, dot(): return jnp.dot(a, b, preferred_element_type=F32)  61.8 us
    ppermute x48, starting transfers between devices, tp_swap(): return lax.ppermute(values, 'tp', xor_pairs(lax.axis_size('tp'), bit))  44 us
    dot_general x6, matrix products, t_dot(): lax.dot_general(a, b, (((0,), (0,)), ((), ())), preferred_element_type=F32)  34.6 us
    ppermute x12, starting transfers between devices, y_swap(): return lax.ppermute(values, 'ctx', xor_pairs(lax.axis_size('ctx'), 2))  32.1 us
  transfers between devices with their start and end apart: 102, of which 43 were waited for; matrix products, arithmetic and copies ran while one was open for 30% of the time, Pallas kernels for 3%

profile of v2, /device:TPU:0, one launch (start us, length us, event | category | flops | bytes accessed | tf_op | source)
XLA Modules:
  0.0 999.7 jit_solution(1499147927128859846)
XLA Ops:
  32.2 10.1 %collective-permute-done.2 = bf16[512,512]{1,0:T(8,128)(2,1)} collective-permute-done((bf16[512,512]{1,0:T(8,128)(2,1)}, bf16[512,512]{1,0:T(8,128)(2,1)}, u32[]{:S(2)}, u32[]{:S(2)}) %collective-permute-start.2) | collective-permute-done | bytes 524320 | tf_op jit(solution)/shard_map/ppermute | solution.py:31
  62.6 18.5 %collective-permute-done.28.kv2 = bf16[2,512,512]{2,1,0:T(8,128)(2,1)S(1)} collective-permute-done((bf16[2,512,512]{2,1,0:T(8,128)(2,1)S(1)}, bf16[2,512,512]{2,1,0:T(8,128)(2,1)S(1)}, u32[]{:S(2)}, u32[]{:S(2)}) %collective-permute-start.28) | collective-permute-done | bytes 1048608 | tf_op jit(solution)/shard_map/ppermute | solution.py:27
  89.0 14.0 %collective-permute-done.7.kv2 = bf16[2,512,512]{2,1,0:T(8,128)(2,1)S(1)} collective-permute-done((bf16[2,512,512]{2,1,0:T(8,128)(2,1)S(1)}, bf16[2,512,512]{2,1,0:T(8,128)(2,1)S(1)}, u32[]{:S(2)}, u32[]{:S(2)}) %collective-permute-start.7) | collective-permute-done | bytes 1048608 | tf_op jit(solution)/shard_map/ppermute | solution.py:27
  114.0 6.1 attend.2
  128.3 17.8 %collective-permute-done.12 = bf16[128,2048]{1,0:T(8,128)(2,1)S(1)} collective-permute-done((bf16[128,2048]{1,0:T(8,128)(2,1)S(1)}, bf16[128,2048]{1,0:T(8,128)(2,1)S(1)}, u32[]{:S(2)}, u32[]{:S(2)}) %collective-permute-start.12) | collective-permute-done | bytes 524320 | tf_op jit(solution)/shard_map/ppermute | solution.py:126
  150.8 13.1 %collective-permute-done.30 = bf16[128,2048]{1,0:T(8,128)(2,1)S(1)} collective-permute-done((bf16[128,2048]{1,0:T(8,128)(2,1)S(1)}, bf16[128,2048]{1,0:T(8,128)(2,1)S(1)}, u32[]{:S(2)}, u32[]{:S(2)}) %collective-permute-start.30) | collective-permute-done | bytes 524320 | tf_op jit(solution)/shard_map/ppermute | solution.py:126
  163.9 8.4 collective-permute-start.18
  188.2 21.9 %collective-permute-done.15 = bf16[128,2048]{1,0:T(8,128)(2,1)} collective-permute-done((bf16[128,2048]{1,0:T(8,128)(2,1)}, bf16[128,2048]{1,0:T(8,128)(2,1)}, u32[]{:S(2)}, u32[]{:S(2)}) %collective-permute-start.15) | collective-permute-done | bytes 524320 | tf_op jit(solution)/shard_map/ppermute | solution.py:126
  212.7 12.0 %collective-permute-done.16 = bf16[128,2048]{1,0:T(8,128)(2,1)} collective-permute-done((bf16[128,2048]{1,0:T(8,128)(2,1)}, bf16[128,2048]{1,0:T(8,128)(2,1)}, u32[]{:S(2)}, u32[]{:S(2)}) %collective-permute-start.16) | collective-permute-done | bytes 524320 | tf_op jit(solution)/shard_map/ppermute | solution.py:126
  224.8 9.5 multiply_convert_fusion.1
  234.4 10.2 %convert_reduce_fusion.3 = (f32[2048]{0:T(1024)}, bf16[512,2048]{1,0:T(8,128)(2,1)S(1)}) fusion(f32[512,2048]{1,0:T(8,128)S(1)} %get-tuple-element.275, f32[2048]{0:T(1024)S(1)} %convert_element_type.580, bf16[512,2048]{1,0:T(8,128)(2,1)S(1)} %copy-done.38, bf16[2048,512]{1,0:T(8,128)(2,1)S(1)} %collective-permute-done.20, ...), kind=kOutput, calls=%fused_computation.63 | convolution fusion | flops 4352636928 | bytes 16793600 | tf_op jit(solution)/shard_map/dot_general | solution.py:62
  244.6 10.4 %convolution_convert_fusion.7 = bf16[512,2048]{1,0:T(8,128)(2,1)S(1)} fusion(bf16[512,2048]{1,0:T(8,128)(2,1)S(1)} %get-tuple-element.279, bf16[512,2048]{1,0:T(8,128)(2,1)} %collective-permute-done.18, bf16[512,2048]{1,0:T(8,128)(2,1)S(1)} %copy-done.57, bf16[512,2048]{1,0:T(8,128)(2,1)} %collective-permute-done.17, bf16[512,2048]{1,0:T(8,128)(2,1)} %get-tuple-element.81), kind=kOutput, calls=%fused_computation.74 | convolution fusion | flops 4329570304 | bytes 12582912 | tf_op jit(solution)/shard_map/dot_general | solution.py:62
  255.2 8.9 convolution_convert_fusion.10
  270.1 22.3 %collective-permute-done.22 = bf16[128,2048]{1,0:T(8,128)(2,1)S(1)} collective-permute-done((bf16[128,2048]{1,0:T(8,128)(2,1)S(1)}, bf16[128,2048]{1,0:T(8,128)(2,1)S(1)}, u32[]{:S(2)}, u32[]{:S(2)}) %collective-permute-start.22) | collective-permute-done | bytes 524320 | tf_op jit(solution)/shard_map/ppermute | solution.py:126
  298.2 13.4 %collective-permute-done.42 = bf16[128,2048]{1,0:T(8,128)(2,1)S(1)} collective-permute-done((bf16[128,2048]{1,0:T(8,128)(2,1)S(1)}, bf16[128,2048]{1,0:T(8,128)(2,1)S(1)}, u32[]{:S(2)}, u32[]{:S(2)}) %collective-permute-start.42) | collective-permute-done | bytes 524320 | tf_op jit(solution)/shard_map/ppermute | solution.py:126
  311.7 10.6 %collective-permute-done.21 = bf16[128,2048]{1,0:T(8,128)(2,1)S(1)} collective-permute-done((bf16[128,2048]{1,0:T(8,128)(2,1)S(1)}, bf16[128,2048]{1,0:T(8,128)(2,1)S(1)}, u32[]{:S(2)}, u32[]{:S(2)}) %collective-permute-start.21) | collective-permute-done | bytes 524320 | tf_op jit(solution)/shard_map/ppermute | solution.py:126
  322.3 6.4 collective-permute-done.23
  339.7 50.8 %collective-permute-done.34 = bf16[128,2048]{1,0:T(8,128)(2,1)S(1)} collective-permute-done((bf16[128,2048]{1,0:T(8,128)(2,1)S(1)}, bf16[128,2048]{1,0:T(8,128)(2,1)S(1)}, u32[]{:S(2)}, u32[]{:S(2)}) %collective-permute-start.34) | collective-permute-done | bytes 524320 | tf_op jit(solution)/shard_map/ppermute | solution.py:126
  390.5 10.3 %collective-permute-done.25 = bf16[128,2048]{1,0:T(8,128)(2,1)} collective-permute-done((bf16[128,2048]{1,0:T(8,128)(2,1)}, bf16[128,2048]{1,0:T(8,128)(2,1)}, u32[]{:S(2)}, u32[]{:S(2)}) %collective-permute-start.25) | collective-permute-done | bytes 524320 | tf_op jit(solution)/shard_map/ppermute | solution.py:126
  407.1 16.0 %collective-permute-done.35 = bf16[128,2048]{1,0:T(8,128)(2,1)S(1)} collective-permute-done((bf16[128,2048]{1,0:T(8,128)(2,1)S(1)}, bf16[128,2048]{1,0:T(8,128)(2,1)S(1)}, u32[]{:S(2)}, u32[]{:S(2)}) %collective-permute-start.35) | collective-permute-done | bytes 524320 | tf_op jit(solution)/shard_map/ppermute | solution.py:126
  423.2 9.3 multiply_convert_fusion
  432.5 10.4 %convert_reduce_fusion.2 = (f32[2048]{0:T(1024)S(1)}, bf16[512,2048]{1,0:T(8,128)(2,1)}) fusion(f32[512,2048]{1,0:T(8,128)} %get-tuple-element.277, f32[2048]{0:T(1024)S(1)} %convert_element_type.580, bf16[512,2048]{1,0:T(8,128)(2,1)S(1)} %copy-done.36, bf16[2048,512]{1,0:T(8,128)(2,1)S(1)} %copy-done.133, bf16[2048,512]{1,0:T(8,128)(2,1)S(1)} %copy-done.58, ...), kind=kOutput, calls=%fused_computation.62 | convolution fusion | flops 4352636928 | bytes 16793600 | tf_op jit(solution)/shard_map/dot_general | solution.py:62
  442.9 10.3 %convolution_convert_fusion.6 = bf16[512,2048]{1,0:T(8,128)(2,1)S(1)} fusion(bf16[512,2048]{1,0:T(8,128)(2,1)} %get-tuple-element.281, bf16[512,2048]{1,0:T(8,128)(2,1)} %collective-permute-done.18, bf16[512,2048]{1,0:T(8,128)(2,1)S(1)} %copy-done.57, bf16[512,2048]{1,0:T(8,128)(2,1)} %collective-permute-done.17, bf16[512,2048]{1,0:T(8,128)(2,1)} %get-tuple-element.81), kind=kOutput, calls=%fused_computation.73 | convolution fusion | flops 4329570304 | bytes 12582912 | tf_op jit(solution)/shard_map/dot_general | solution.py:62
  457.3 14.0 %convolution_convert_fusion.1 = bf16[2048,2048]{1,0:T(8,128)(2,1)} fusion(bf16[1024,2048]{1,0:T(8,128)(2,1)} %constant_dynamic-update-slice_fusion.8, bf16[512,2048]{1,0:T(8,128)(2,1)S(1)} %copy-done.142, bf16[512,2048]{1,0:T(8,128)(2,1)S(1)} %copy-done.141), kind=kOutput, calls=%fused_computation.5 | convolution fusion | flops 8602517504 | bytes 16777216 | tf_op jit(solution)/shard_map/dot_general | solution.py:66
  471.3 10.8 %convolution_convert_fusion = bf16[2048,2048]{1,0:T(8,128)(2,1)S(1)} fusion(bf16[512,2048]{1,0:T(8,128)(2,1)} %get-tuple-element.276, bf16[512,2048]{1,0:T(8,128)(2,1)S(1)} %copy-done.143, bf16[512,2048]{1,0:T(8,128)(2,1)S(1)} %copy-done.36, bf16[512,2048]{1,0:T(8,128)(2,1)S(1)} %copy-done.38), kind=kOutput, calls=%fused_computation.4 | convolution fusion | flops 8610906112 | bytes 16777216 | tf_op jit(solution)/shard_map/dot_general | solution.py:66
  482.2 12.2 %convolution_convert_fusion.8 = bf16[512,2048]{1,0:T(8,128)(2,1)S(1)} fusion(bf16[512,2048]{1,0:T(8,128)(2,1)} %get-tuple-element.276, bf16[2048,512]{1,0:T(8,128)(2,1)} %copy-done.132, bf16[2048,512]{1,0:T(8,128)(2,1)S(1)} %copy-done.59, bf16[2048,512]{1,0:T(8,128)(2,1)} %collective-permute-done.19, bf16[2048,512]{1,0:T(8,128)(2,1)} %get-tuple-element.79), kind=kOutput, calls=%fused_computation.75 | convolution fusion | flops 4329570304 | bytes 12582912 | tf_op jit(solution)/shard_map/dot_general | solution.py:58
  499.2 8.5 attend_back.2
  533.0 28.4 %collective-permute-done.58 = bf16[128,2048]{1,0:T(8,128)(2,1)S(1)} collective-permute-done((bf16[128,2048]{1,0:T(8,128)(2,1)S(1)}, bf16[128,2048]{1,0:T(8,128)(2,1)S(1)}, u32[]{:S(2)}, u32[]{:S(2)}) %collective-permute-start.58) | collective-permute-done | bytes 524320 | tf_op jit(solution)/shard_map/ppermute | solution.py:126
  561.3 11.1 %collective-permute-done.38 = bf16[128,2048]{1,0:T(8,128)(2,1)S(1)} collective-permute-done((bf16[128,2048]{1,0:T(8,128)(2,1)S(1)}, bf16[128,2048]{1,0:T(8,128)(2,1)S(1)}, u32[]{:S(2)}, u32[]{:S(2)}) %collective-permute-start.38) | collective-permute-done | bytes 524320 | tf_op jit(solution)/shard_map/ppermute | solution.py:126
  583.1 18.6 %collective-permute-done.60 = bf16[128,2048]{1,0:T(8,128)(2,1)S(1)} collective-permute-done((bf16[128,2048]{1,0:T(8,128)(2,1)S(1)}, bf16[128,2048]{1,0:T(8,128)(2,1)S(1)}, u32[]{:S(2)}, u32[]{:S(2)}) %collective-permute-start.60) | collective-permute-done | bytes 524320 | tf_op jit(solution)/shard_map/ppermute | solution.py:126
  604.0 19.6 %collective-permute-done.40 = bf16[128,2048]{1,0:T(8,128)(2,1)} collective-permute-done((bf16[128,2048]{1,0:T(8,128)(2,1)}, bf16[128,2048]{1,0:T(8,128)(2,1)}, u32[]{:S(2)}, u32[]{:S(2)}) %collective-permute-start.40) | collective-permute-done | bytes 524320 | tf_op jit(solution)/shard_map/ppermute | solution.py:126
  627.6 10.6 %collective-permute-start.49 = (bf16[2,512,512]{2,1,0:T(8,128)(2,1)S(1)}, bf16[2,512,512]{2,1,0:T(8,128)(2,1)}, u32[]{:S(2)}, u32[]{:S(2)}) collective-permute-start(bf16[2,512,512]{2,1,0:T(8,128)(2,1)S(1)} %fusion.111), channel_id=1, source_target_pairs={{0,8},{4,12},{8,0},{12,4},{1,9},{5,13},{9,1},{13,5},{2,10},{6,14},... | collective-permute-start | bytes 3145736 | tf_op jit(solution)/shard_map/ppermute | solution.py:27
  640.7 8.9 attend_back.3
  683.8 11.5 %collective-permute-done.51 = bf16[128,2048]{1,0:T(8,128)(2,1)S(1)} collective-permute-done((bf16[128,2048]{1,0:T(8,128)(2,1)S(1)}, bf16[128,2048]{1,0:T(8,128)(2,1)S(1)}, u32[]{:S(2)}, u32[]{:S(2)}) %collective-permute-start.51) | collective-permute-done | bytes 524320 | tf_op jit(solution)/shard_map/ppermute | solution.py:126
  698.2 10.1 %collective-permute-done.91 = bf16[512,512]{1,0:T(8,128)(2,1)S(1)} collective-permute-done((bf16[512,512]{1,0:T(8,128)(2,1)S(1)}, bf16[512,512]{1,0:T(8,128)(2,1)S(1)}, u32[]{:S(2)}, u32[]{:S(2)}) %collective-permute-start.91) | collective-permute-done | bytes 524320 | tf_op jit(solution)/shard_map/ppermute | solution.py:31
  708.3 7.0 collective-permute-start.77
  732.1 7.3 collective-permute-done.92
  752.8 6.8 collective-permute-done.63
  780.4 33.5 %collective-permute-done.89 = f32[3072]{0:T(1024)S(1)} collective-permute-done((f32[3072]{0:T(1024)S(1)}, f32[3072]{0:T(1024)S(1)}, u32[]{:S(2)}, u32[]{:S(2)}) %collective-permute-start.89) | collective-permute-done | bytes 12320 | tf_op jit(solution)/shard_map/ppermute | solution.py:31
  828.9 12.3 %collective-permute-done.52 = bf16[128,2048]{1,0:T(8,128)(2,1)} collective-permute-done((bf16[128,2048]{1,0:T(8,128)(2,1)}, bf16[128,2048]{1,0:T(8,128)(2,1)}, u32[]{:S(2)}, u32[]{:S(2)}) %collective-permute-start.52) | collective-permute-done | bytes 524320 | tf_op jit(solution)/shard_map/ppermute | solution.py:126
  843.5 16.4 %collective-permute-done.66 = bf16[128,2048]{1,0:T(8,128)(2,1)S(1)} collective-permute-done((bf16[128,2048]{1,0:T(8,128)(2,1)S(1)}, bf16[128,2048]{1,0:T(8,128)(2,1)S(1)}, u32[]{:S(2)}, u32[]{:S(2)}) %collective-permute-start.66) | collective-permute-done | bytes 524320 | tf_op jit(solution)/shard_map/ppermute | solution.py:126
  874.0 16.7 %collective-permute-done.71 = f32[6,2048]{1,0:T(8,128)S(1)} collective-permute-done((f32[6,2048]{1,0:T(8,128)S(1)}, f32[6,2048]{1,0:T(8,128)S(1)}, u32[]{:S(2)}, u32[]{:S(2)}) %collective-permute-start.71) | collective-permute-done | bytes 49184 | tf_op jit(solution)/shard_map/ppermute | solution.py:27
  894.3 10.9 %collective-permute-done.72 = f32[6,2048]{1,0:T(8,128)S(1)} collective-permute-done((f32[6,2048]{1,0:T(8,128)S(1)}, f32[6,2048]{1,0:T(8,128)S(1)}, u32[]{:S(2)}, u32[]{:S(2)}) %collective-permute-start.72) | collective-permute-done | bytes 49184 | tf_op jit(solution)/shard_map/ppermute | solution.py:31
  931.1 8.7 collective-permute-done.54
  939.8 8.8 collective-permute-done.69
  952.1 7.7 collective-permute-done.53
  959.9 8.2 collective-permute-done.55
  974.8 8.1 collective-permute-done.100
  (705 shorter events, 358.5 us)
Async XLA Ops:
  3.8 44.4 %collective-permute-start = (bf16[512,512]{1,0:T(8,128)(2,1)}, bf16[512,512]{1,0:T(8,128)(2,1)}, u32[]{:S(2)}, u32[]{:S(2)}) collective-permute-start(bf16[512,512]{1,0:T(8,128)(2,1)} %get-tuple-element.174), channel_id=1, source_target_pairs={{0,16},{16,0},{1,17},{17,1},{2,18},{18,2},{3,19},{19,3},{4,20},{20... | collective-permute-start | bytes 1572872 | tf_op jit(solution)/shard_map/ppermute | solution.py:31
  6.8 38.0 %collective-permute-start.4 = (bf16[512,512]{1,0:T(8,128)(2,1)S(1)}, bf16[512,512]{1,0:T(8,128)(2,1)}, u32[]{:S(2)}, u32[]{:S(2)}) collective-permute-start(bf16[512,512]{1,0:T(8,128)(2,1)S(1)} %get-tuple-element.172), channel_id=1, source_target_pairs={{0,16},{16,0},{1,17},{17,1},{2,18},{18,2},{3,19},{19,3},{4,20},{20... | collective-permute-start | bytes 1572872 | tf_op jit(solution)/shard_map/ppermute | solution.py:31
  8.1 34.2 %collective-permute-start.2 = (bf16[512,512]{1,0:T(8,128)(2,1)}, bf16[512,512]{1,0:T(8,128)(2,1)}, u32[]{:S(2)}, u32[]{:S(2)}) collective-permute-start(bf16[512,512]{1,0:T(8,128)(2,1)} %get-tuple-element.170), channel_id=1, source_target_pairs={{0,16},{16,0},{1,17},{17,1},{2,18},{18,2},{3,19},{19,3},{4,20},{20... | collective-permute-start | bytes 1572872 | tf_op jit(solution)/shard_map/ppermute | solution.py:31
  11.1 70.1 %collective-permute-start.9 = (bf16[512,512]{1,0:T(8,128)(2,1)}, bf16[512,512]{1,0:T(8,128)(2,1)}, u32[]{:S(2)}, u32[]{:S(2)}) collective-permute-start(bf16[512,512]{1,0:T(8,128)(2,1)} %get-tuple-element.168), channel_id=1, source_target_pairs={{0,16},{16,0},{1,17},{17,1},{2,18},{18,2},{3,19},{19,3},{4,20},{20... | collective-permute-start | bytes 1572872 | tf_op jit(solution)/shard_map/ppermute | solution.py:31
  48.2 35.1 %collective-permute-start.1 = (bf16[512,512]{1,0:T(8,128)(2,1)}, bf16[512,512]{1,0:T(8,128)(2,1)S(1)}, u32[]{:S(2)}, u32[]{:S(2)}) collective-permute-start(bf16[512,512]{1,0:T(8,128)(2,1)} %collective-permute-done), channel_id=1, source_target_pairs={{0,4},{4,0},{8,12},{12,8},{1,5},{5,1},{9,13},{13,9},{2,6},{6,2},{1... | collective-permute-start | bytes 1572872 | tf_op jit(solution)/shard_map/ppermute | solution.py:23
  54.5 34.2 %collective-permute-start.27 = (bf16[2,512,512]{2,1,0:T(8,128)(2,1)S(1)}, bf16[2,512,512]{2,1,0:T(8,128)(2,1)S(1)}, u32[]{:S(2)}, u32[]{:S(2)}) collective-permute-start(bf16[2,512,512]{2,1,0:T(8,128)(2,1)S(1)} %pad_maximum_fusion.23.kv0), channel_id=1, source_target_pairs={{0,4},{4,0},{8,12},{12,8},{1,5},{5,1},{9,13},{13,9},{2,6},{6,2},{1... | collective-permute-start | bytes 3145736 | tf_op jit(solution)/shard_map/ppermute | solution.py:23
  62.5 40.5 %collective-permute-start.7 = (bf16[2,512,512]{2,1,0:T(8,128)(2,1)S(1)}, bf16[2,512,512]{2,1,0:T(8,128)(2,1)S(1)}, u32[]{:S(2)}, u32[]{:S(2)}) collective-permute-start(bf16[2,512,512]{2,1,0:T(8,128)(2,1)S(1)} %pad_maximum_fusion.22.kv0), channel_id=1, source_target_pairs={{0,8},{4,12},{8,0},{12,4},{1,9},{5,13},{9,1},{13,5},{2,10},{6,14},... | collective-permute-start | bytes 3145736 | tf_op jit(solution)/shard_map/ppermute | solution.py:27
  81.2 67.9 %collective-permute-start.17 = (bf16[512,2048]{1,0:T(8,128)(2,1)}, bf16[512,2048]{1,0:T(8,128)(2,1)}, u32[]{:S(2)}, u32[]{:S(2)}) collective-permute-start(bf16[512,2048]{1,0:T(8,128)(2,1)} %get-tuple-element.81), channel_id=1, source_target_pairs={{0,16},{16,0},{1,17},{17,1},{2,18},{18,2},{3,19},{19,3},{4,20},{20... | collective-permute-start | bytes 6291464 | tf_op jit(solution)/shard_map/ppermute | solution.py:31
  123.3 40.6 %collective-permute-start.30 = (bf16[128,2048]{1,0:T(8,128)(2,1)S(1)}, bf16[128,2048]{1,0:T(8,128)(2,1)S(1)}, u32[]{:S(2)}, u32[]{:S(2)}) collective-permute-start(bf16[128,2048]{1,0:T(8,128)(2,1)S(1)} %get-tuple-element.143), channel_id=1, source_target_pairs={{0,1},{1,0},{2,3},{3,2},{4,5},{5,4},{6,7},{7,6},{8,9},{9,8},{10,11... | collective-permute-start | bytes 1572872 | tf_op jit(solution)/shard_map/ppermute | solution.py:126
  125.1 51.7 %collective-permute-start.11 = (bf16[128,2048]{1,0:T(8,128)(2,1)S(1)}, bf16[128,2048]{1,0:T(8,128)(2,1)S(1)}, u32[]{:S(2)}, u32[]{:S(2)}) collective-permute-start(bf16[128,2048]{1,0:T(8,128)(2,1)S(1)} %get-tuple-element.133), channel_id=1, source_target_pairs={{0,1},{1,0},{2,3},{3,2},{4,5},{5,4},{6,7},{7,6},{8,9},{9,8},{10,11... | collective-permute-start | bytes 1572872 | tf_op jit(solution)/shard_map/ppermute | solution.py:126
  125.4 51.3 %collective-permute-start.32 = (bf16[128,2048]{1,0:T(8,128)(2,1)S(1)}, bf16[128,2048]{1,0:T(8,128)(2,1)S(1)}, u32[]{:S(2)}, u32[]{:S(2)}) collective-permute-start(bf16[128,2048]{1,0:T(8,128)(2,1)S(1)} %add_convert_fusion.17), channel_id=1, source_target_pairs={{0,2},{1,3},{2,0},{3,1},{4,6},{5,7},{6,4},{7,5},{8,10},{9,11},{10,... | collective-permute-start | bytes 1572872 | tf_op jit(solution)/shard_map/ppermute | solution.py:126
  149.2 61.7 %collective-permute-start.19 = (bf16[2048,512]{1,0:T(8,128)(2,1)}, bf16[2048,512]{1,0:T(8,128)(2,1)}, u32[]{:S(2)}, u32[]{:S(2)}) collective-permute-start(bf16[2048,512]{1,0:T(8,128)(2,1)} %get-tuple-element.79), channel_id=1, source_target_pairs={{0,16},{16,0},{1,17},{17,1},{2,18},{18,2},{3,19},{19,3},{4,20},{20... | collective-permute-start | bytes 6291464 | tf_op jit(solution)/shard_map/ppermute | solution.py:31
  163.9 48.9 %collective-permute-start.18 = (bf16[512,2048]{1,0:T(8,128)(2,1)}, bf16[512,2048]{1,0:T(8,128)(2,1)}, u32[]{:S(2)}, u32[]{:S(2)}) collective-permute-start(bf16[512,2048]{1,0:T(8,128)(2,1)} %collective-permute-done.17), channel_id=1, source_target_pairs={{0,4},{4,0},{8,12},{12,8},{1,5},{5,1},{9,13},{13,9},{2,6},{6,2},{1... | collective-permute-start | bytes 6291464 | tf_op jit(solution)/shard_map/ppermute | solution.py:23
  266.2 45.4 %collective-permute-start.42 = (bf16[128,2048]{1,0:T(8,128)(2,1)S(1)}, bf16[128,2048]{1,0:T(8,128)(2,1)S(1)}, u32[]{:S(2)}, u32[]{:S(2)}) collective-permute-start(bf16[128,2048]{1,0:T(8,128)(2,1)S(1)} %get-tuple-element.111), channel_id=1, source_target_pairs={{0,1},{1,0},{2,3},{3,2},{4,5},{5,4},{6,7},{7,6},{8,9},{9,8},{10,11... | collective-permute-start | bytes 1572872 | tf_op jit(solution)/shard_map/ppermute | solution.py:126
  266.3 56.0 %collective-permute-start.21 = (bf16[128,2048]{1,0:T(8,128)(2,1)S(1)}, bf16[128,2048]{1,0:T(8,128)(2,1)S(1)}, u32[]{:S(2)}, u32[]{:S(2)}) collective-permute-start(bf16[128,2048]{1,0:T(8,128)(2,1)S(1)} %get-tuple-element.125), channel_id=1, source_target_pairs={{0,1},{1,0},{2,3},{3,2},{4,5},{5,4},{6,7},{7,6},{8,9},{9,8},{10,11... | collective-permute-start | bytes 1572872 | tf_op jit(solution)/shard_map/ppermute | solution.py:126
  270.0 52.3 %collective-permute-start.44 = (bf16[128,2048]{1,0:T(8,128)(2,1)S(1)}, bf16[128,2048]{1,0:T(8,128)(2,1)S(1)}, u32[]{:S(2)}, u32[]{:S(2)}) collective-permute-start(bf16[128,2048]{1,0:T(8,128)(2,1)S(1)} %add_convert_fusion.13), channel_id=1, source_target_pairs={{0,2},{1,3},{2,0},{3,1},{4,6},{5,7},{6,4},{7,5},{8,10},{9,11},{10,... | collective-permute-start | bytes 1572872 | tf_op jit(solution)/shard_map/ppermute | solution.py:126
  292.5 36.2 %collective-permute-start.23 = (bf16[128,2048]{1,0:T(8,128)(2,1)S(1)}, bf16[128,2048]{1,0:T(8,128)(2,1)S(1)}, u32[]{:S(2)}, u32[]{:S(2)}) collective-permute-start(bf16[128,2048]{1,0:T(8,128)(2,1)S(1)} %add_convert_fusion.19), channel_id=1, source_target_pairs={{0,2},{1,3},{2,0},{3,1},{4,6},{5,7},{6,4},{7,5},{8,10},{9,11},{10,... | collective-permute-start | bytes 1572872 | tf_op jit(solution)/shard_map/ppermute | solution.py:126
  331.6 69.2 %collective-permute-start.46 = (bf16[128,2048]{1,0:T(8,128)(2,1)S(1)}, bf16[128,2048]{1,0:T(8,128)(2,1)}, u32[]{:S(2)}, u32[]{:S(2)}) collective-permute-start(bf16[128,2048]{1,0:T(8,128)(2,1)S(1)} %get-tuple-element.58), channel_id=1, source_target_pairs={{0,2},{1,3},{2,0},{3,1},{4,6},{5,7},{6,4},{7,5},{8,10},{9,11},{10,... | collective-permute-start | bytes 1572872 | tf_op jit(solution)/shard_map/ppermute | solution.py:126
  331.6 71.3 %collective-permute-start.45 = (bf16[128,2048]{1,0:T(8,128)(2,1)S(1)}, bf16[128,2048]{1,0:T(8,128)(2,1)S(1)}, u32[]{:S(2)}, u32[]{:S(2)}) collective-permute-start(bf16[128,2048]{1,0:T(8,128)(2,1)S(1)} %get-tuple-element.58), channel_id=1, source_target_pairs={{0,1},{1,0},{2,3},{3,2},{4,5},{5,4},{6,7},{7,6},{8,9},{9,8},{10,11... | collective-permute-start | bytes 1572872 | tf_op jit(solution)/shard_map/ppermute | solution.py:126
  334.6 55.8 %collective-permute-start.34 = (bf16[128,2048]{1,0:T(8,128)(2,1)S(1)}, bf16[128,2048]{1,0:T(8,128)(2,1)S(1)}, u32[]{:S(2)}, u32[]{:S(2)}) collective-permute-start(bf16[128,2048]{1,0:T(8,128)(2,1)S(1)} %get-tuple-element.215), channel_id=1, source_target_pairs={{0,2},{1,3},{2,0},{3,1},{4,6},{5,7},{6,4},{7,5},{8,10},{9,11},{10,... | collective-permute-start | bytes 1572872 | tf_op jit(solution)/shard_map/ppermute | solution.py:126
  335.6 65.2 %collective-permute-start.25 = (bf16[128,2048]{1,0:T(8,128)(2,1)}, bf16[128,2048]{1,0:T(8,128)(2,1)}, u32[]{:S(2)}, u32[]{:S(2)}) collective-permute-start(bf16[128,2048]{1,0:T(8,128)(2,1)} %pad_maximum_fusion.24), channel_id=1, source_target_pairs={{0,2},{1,3},{2,0},{3,1},{4,6},{5,7},{6,4},{7,5},{8,10},{9,11},{10,... | collective-permute-start | bytes 1572872 | tf_op jit(solution)/shard_map/ppermute | solution.py:126
  339.6 64.5 %collective-permute-start.33 = (bf16[128,2048]{1,0:T(8,128)(2,1)S(1)}, bf16[128,2048]{1,0:T(8,128)(2,1)S(1)}, u32[]{:S(2)}, u32[]{:S(2)}) collective-permute-start(bf16[128,2048]{1,0:T(8,128)(2,1)S(1)} %get-tuple-element.215), channel_id=1, source_target_pairs={{0,1},{1,0},{2,3},{3,2},{4,5},{5,4},{6,7},{7,6},{8,9},{9,8},{10,11... | collective-permute-start | bytes 1572872 | tf_op jit(solution)/shard_map/ppermute | solution.py:126
  390.5 117.3 %collective-permute-start.24 = (bf16[128,2048]{1,0:T(8,128)(2,1)}, bf16[128,2048]{1,0:T(8,128)(2,1)}, u32[]{:S(2)}, u32[]{:S(2)}) collective-permute-start(bf16[128,2048]{1,0:T(8,128)(2,1)} %pad_maximum_fusion.24), channel_id=1, source_target_pairs={{0,1},{1,0},{2,3},{3,2},{4,5},{5,4},{6,7},{7,6},{8,9},{9,8},{10,11... | collective-permute-start | bytes 1572872 | tf_op jit(solution)/shard_map/ppermute | solution.py:126
  400.8 108.8 %collective-permute-start.26 = (bf16[128,2048]{1,0:T(8,128)(2,1)}, bf16[128,2048]{1,0:T(8,128)(2,1)}, u32[]{:S(2)}, u32[]{:S(2)}) collective-permute-start(bf16[128,2048]{1,0:T(8,128)(2,1)} %collective-permute-done.25), channel_id=1, source_target_pairs={{0,1},{1,0},{2,3},{3,2},{4,5},{5,4},{6,7},{7,6},{8,9},{9,8},{10,11... | collective-permute-start | bytes 1572872 | tf_op jit(solution)/shard_map/ppermute | solution.py:126
  402.8 92.8 %collective-permute-start.47 = (bf16[128,2048]{1,0:T(8,128)(2,1)}, bf16[128,2048]{1,0:T(8,128)(2,1)}, u32[]{:S(2)}, u32[]{:S(2)}) collective-permute-start(bf16[128,2048]{1,0:T(8,128)(2,1)} %collective-permute-done.46), channel_id=1, source_target_pairs={{0,1},{1,0},{2,3},{3,2},{4,5},{5,4},{6,7},{7,6},{8,9},{9,8},{10,11... | collective-permute-start | bytes 1572872 | tf_op jit(solution)/shard_map/ppermute | solution.py:126
  454.4 68.5 %collective-permute-start.57 = (bf16[128,2048]{1,0:T(8,128)(2,1)}, bf16[128,2048]{1,0:T(8,128)(2,1)}, u32[]{:S(2)}, u32[]{:S(2)}) collective-permute-start(bf16[128,2048]{1,0:T(8,128)(2,1)} %get-tuple-element.102), channel_id=1, source_target_pairs={{0,1},{1,0},{2,3},{3,2},{4,5},{5,4},{6,7},{7,6},{8,9},{9,8},{10,11... | collective-permute-start | bytes 1572872 | tf_op jit(solution)/shard_map/ppermute | solution.py:126
  454.4 78.5 %collective-permute-start.56 = (bf16[128,2048]{1,0:T(8,128)(2,1)}, bf16[128,2048]{1,0:T(8,128)(2,1)S(1)}, u32[]{:S(2)}, u32[]{:S(2)}) collective-permute-start(bf16[128,2048]{1,0:T(8,128)(2,1)} %get-tuple-element.101), channel_id=1, source_target_pairs={{0,1},{1,0},{2,3},{3,2},{4,5},{5,4},{6,7},{7,6},{8,9},{9,8},{10,11... | collective-permute-start | bytes 1572872 | tf_op jit(solution)/shard_map/ppermute | solution.py:126
  509.6 114.1 %collective-permute-start.48 = (bf16[2,2,512,512]{3,2,1,0:T(8,128)(2,1)}, bf16[2,2,512,512]{3,2,1,0:T(8,128)(2,1)S(1)}, u32[]{:S(2)}, u32[]{:S(2)}) collective-permute-start(bf16[2,2,512,512]{3,2,1,0:T(8,128)(2,1)} %get-tuple-element.29), channel_id=1, source_target_pairs={{0,4},{4,0},{8,12},{12,8},{1,5},{5,1},{9,13},{13,9},{2,6},{6,2},{1... | collective-permute-start | bytes 6291464 | tf_op jit(solution)/shard_map/ppermute | solution.py:23
  524.1 37.3 %collective-permute-start.58 = (bf16[128,2048]{1,0:T(8,128)(2,1)S(1)}, bf16[128,2048]{1,0:T(8,128)(2,1)S(1)}, u32[]{:S(2)}, u32[]{:S(2)}) collective-permute-start(bf16[128,2048]{1,0:T(8,128)(2,1)S(1)} %add_convert_fusion.11), channel_id=1, source_target_pairs={{0,2},{1,3},{2,0},{3,1},{4,6},{5,7},{6,4},{7,5},{8,10},{9,11},{10,... | collective-permute-start | bytes 1572872 | tf_op jit(solution)/shard_map/ppermute | solution.py:126
  525.5 47.0 %collective-permute-start.38 = (bf16[128,2048]{1,0:T(8,128)(2,1)S(1)}, bf16[128,2048]{1,0:T(8,128)(2,1)S(1)}, u32[]{:S(2)}, u32[]{:S(2)}) collective-permute-start(bf16[128,2048]{1,0:T(8,128)(2,1)S(1)} %add_convert_fusion.15), channel_id=1, source_target_pairs={{0,2},{1,3},{2,0},{3,1},{4,6},{5,7},{6,4},{7,5},{8,10},{9,11},{10,... | collective-permute-start | bytes 1572872 | tf_op jit(solution)/shard_map/ppermute | solution.py:126
  532.9 182.5 %collective-permute-start.94 = (bf16[1024,2048]{1,0:T(8,128)(2,1)}, bf16[1024,2048]{1,0:T(8,128)(2,1)}, u32[]{:S(2)}, u32[]{:S(2)}) collective-permute-start(bf16[1024,2048]{1,0:T(8,128)(2,1)} %slice.458), channel_id=1, source_target_pairs={{0,4},{4,0},{8,12},{12,8},{1,5},{5,1},{9,13},{13,9},{2,6},{6,2},{1... | collective-permute-start | bytes 12582920 | tf_op jit(solution)/shard_map/ppermute | solution.py:23
  581.9 41.7 %collective-permute-start.40 = (bf16[128,2048]{1,0:T(8,128)(2,1)}, bf16[128,2048]{1,0:T(8,128)(2,1)}, u32[]{:S(2)}, u32[]{:S(2)}) collective-permute-start(bf16[128,2048]{1,0:T(8,128)(2,1)} %pad_maximum_fusion.25), channel_id=1, source_target_pairs={{0,2},{1,3},{2,0},{3,1},{4,6},{5,7},{6,4},{7,5},{8,10},{9,11},{10,... | collective-permute-start | bytes 1572872 | tf_op jit(solution)/shard_map/ppermute | solution.py:126
  601.7 139.0 %collective-permute-start.98 = (bf16[2048,1024]{1,0:T(8,128)(2,1)}, bf16[2048,1024]{1,0:T(8,128)(2,1)}, u32[]{:S(2)}, u32[]{:S(2)}) collective-permute-start(bf16[2048,1024]{1,0:T(8,128)(2,1)} %slice.463), channel_id=1, source_target_pairs={{0,4},{4,0},{8,12},{12,8},{1,5},{5,1},{9,13},{13,9},{2,6},{6,2},{1... | collective-permute-start | bytes 12582920 | tf_op jit(solution)/shard_map/ppermute | solution.py:23
  627.6 42.5 %collective-permute-start.49 = (bf16[2,512,512]{2,1,0:T(8,128)(2,1)S(1)}, bf16[2,512,512]{2,1,0:T(8,128)(2,1)}, u32[]{:S(2)}, u32[]{:S(2)}) collective-permute-start(bf16[2,512,512]{2,1,0:T(8,128)(2,1)S(1)} %fusion.111), channel_id=1, source_target_pairs={{0,8},{4,12},{8,0},{12,4},{1,9},{5,13},{9,1},{13,5},{2,10},{6,14},... | collective-permute-start | bytes 3145736 | tf_op jit(solution)/shard_map/ppermute | solution.py:27
  656.8 65.9 %collective-permute-start.62 = (bf16[2,2,512,512]{3,2,1,0:T(8,128)(2,1)}, bf16[2,2,512,512]{3,2,1,0:T(8,128)(2,1)}, u32[]{:S(2)}, u32[]{:S(2)}) collective-permute-start(bf16[2,2,512,512]{3,2,1,0:T(8,128)(2,1)} %get-tuple-element.33), channel_id=1, source_target_pairs={{0,4},{4,0},{8,12},{12,8},{1,5},{5,1},{9,13},{13,9},{2,6},{6,2},{1... | collective-permute-start | bytes 6291464 | tf_op jit(solution)/shard_map/ppermute | solution.py:23
  697.7 130.9 %collective-permute-start.50 = (bf16[128,2048]{1,0:T(8,128)(2,1)}, bf16[128,2048]{1,0:T(8,128)(2,1)}, u32[]{:S(2)}, u32[]{:S(2)}) collective-permute-start(bf16[128,2048]{1,0:T(8,128)(2,1)} %get-tuple-element.91), channel_id=1, source_target_pairs={{0,1},{1,0},{2,3},{3,2},{4,5},{5,4},{6,7},{7,6},{8,9},{9,8},{10,11... | collective-permute-start | bytes 1572872 | tf_op jit(solution)/shard_map/ppermute | solution.py:126
  722.8 95.0 %collective-permute-start.95 = (bf16[512,2048]{1,0:T(8,128)(2,1)}, bf16[512,2048]{1,0:T(8,128)(2,1)}, u32[]{:S(2)}, u32[]{:S(2)}) collective-permute-start(bf16[512,2048]{1,0:T(8,128)(2,1)} %slice.596), channel_id=1, source_target_pairs={{0,16},{16,0},{1,17},{17,1},{2,18},{18,2},{3,19},{19,3},{4,20},{20... | collective-permute-start | bytes 6291464 | tf_op jit(solution)/shard_map/ppermute | solution.py:31
  747.5 75.3 %collective-permute-start.99 = (bf16[2048,512]{1,0:T(8,128)(2,1)}, bf16[2048,512]{1,0:T(8,128)(2,1)}, u32[]{:S(2)}, u32[]{:S(2)}) collective-permute-start(bf16[2048,512]{1,0:T(8,128)(2,1)} %slice.595), channel_id=1, source_target_pairs={{0,16},{16,0},{1,17},{17,1},{2,18},{18,2},{3,19},{19,3},{4,20},{20... | collective-permute-start | bytes 6291464 | tf_op jit(solution)/shard_map/ppermute | solution.py:31
  768.1 47.9 %collective-permute-start.65 = (bf16[128,2048]{1,0:T(8,128)(2,1)S(1)}, bf16[128,2048]{1,0:T(8,128)(2,1)S(1)}, u32[]{:S(2)}, u32[]{:S(2)}) collective-permute-start(bf16[128,2048]{1,0:T(8,128)(2,1)S(1)} %get-tuple-element.99), channel_id=1, source_target_pairs={{0,1},{1,0},{2,3},{3,2},{4,5},{5,4},{6,7},{7,6},{8,9},{9,8},{10,11... | collective-permute-start | bytes 1572872 | tf_op jit(solution)/shard_map/ppermute | solution.py:126
  773.5 40.3 %collective-permute-start.89 = (f32[3072]{0:T(1024)S(1)}, f32[3072]{0:T(1024)S(1)}, u32[]{:S(2)}, u32[]{:S(2)}) collective-permute-start(f32[3072]{0:T(1024)S(1)} %add.930), channel_id=1, source_target_pairs={{0,16},{16,0},{1,17},{17,1},{2,18},{18,2},{3,19},{19,3},{4,20},{20... | collective-permute-start | bytes 36872 | tf_op jit(solution)/shard_map/ppermute | solution.py:31
  817.8 52.0 %collective-permute-start.83 = (bf16[1024,512]{1,0:T(8,128)(2,1)}, bf16[1024,512]{1,0:T(8,128)(2,1)}, u32[]{:S(2)}, u32[]{:S(2)}) collective-permute-start(bf16[1024,512]{1,0:T(8,128)(2,1)} %slice.446), channel_id=1, source_target_pairs={{0,4},{4,0},{8,12},{12,8},{1,5},{5,1},{9,13},{13,9},{2,6},{6,2},{1... | collective-permute-start | bytes 3145736 | tf_op jit(solution)/shard_map/ppermute | solution.py:23
  822.8 37.1 %collective-permute-start.66 = (bf16[128,2048]{1,0:T(8,128)(2,1)S(1)}, bf16[128,2048]{1,0:T(8,128)(2,1)S(1)}, u32[]{:S(2)}, u32[]{:S(2)}) collective-permute-start(bf16[128,2048]{1,0:T(8,128)(2,1)S(1)} %add_convert_fusion.10), channel_id=1, source_target_pairs={{0,2},{1,3},{2,0},{3,1},{4,6},{5,7},{6,4},{7,5},{8,10},{9,11},{10,... | collective-permute-start | bytes 1572872 | tf_op jit(solution)/shard_map/ppermute | solution.py:126
  828.6 63.6 %collective-permute-start.79 = (bf16[1024,512]{1,0:T(8,128)(2,1)}, bf16[1024,512]{1,0:T(8,128)(2,1)}, u32[]{:S(2)}, u32[]{:S(2)}) collective-permute-start(bf16[1024,512]{1,0:T(8,128)(2,1)} %slice.442), channel_id=1, source_target_pairs={{0,4},{4,0},{8,12},{12,8},{1,5},{5,1},{9,13},{13,9},{2,6},{6,2},{1... | collective-permute-start | bytes 3145736 | tf_op jit(solution)/shard_map/ppermute | solution.py:23
  841.2 130.3 %collective-permute-start.96 = (bf16[512,2048]{1,0:T(8,128)(2,1)}, bf16[512,2048]{1,0:T(8,128)(2,1)}, u32[]{:S(2)}, u32[]{:S(2)}) collective-permute-start(bf16[512,2048]{1,0:T(8,128)(2,1)} %fusion.27), channel_id=1, source_target_pairs={{0,8},{4,12},{8,0},{12,4},{1,9},{5,13},{9,1},{13,5},{2,10},{6,14},... | collective-permute-start | bytes 6291464 | tf_op jit(solution)/shard_map/ppermute | solution.py:27
  867.1 51.7 %collective-permute-start.68 = (bf16[128,2048]{1,0:T(8,128)(2,1)S(1)}, bf16[128,2048]{1,0:T(8,128)(2,1)S(1)}, u32[]{:S(2)}, u32[]{:S(2)}) collective-permute-start(bf16[128,2048]{1,0:T(8,128)(2,1)S(1)} %pad_maximum_fusion.27), channel_id=1, source_target_pairs={{0,2},{1,3},{2,0},{3,1},{4,6},{5,7},{6,4},{7,5},{8,10},{9,11},{10,... | collective-permute-start | bytes 1572872 | tf_op jit(solution)/shard_map/ppermute | solution.py:126
  868.3 62.1 %collective-permute-start.67 = (bf16[128,2048]{1,0:T(8,128)(2,1)S(1)}, bf16[128,2048]{1,0:T(8,128)(2,1)S(1)}, u32[]{:S(2)}, u32[]{:S(2)}) collective-permute-start(bf16[128,2048]{1,0:T(8,128)(2,1)S(1)} %pad_maximum_fusion.27), channel_id=1, source_target_pairs={{0,1},{1,0},{2,3},{3,2},{4,5},{5,4},{6,7},{7,6},{8,9},{9,8},{10,11... | collective-permute-start | bytes 1572872 | tf_op jit(solution)/shard_map/ppermute | solution.py:126
  930.4 52.4 %collective-permute-start.100 = (bf16[2048,512]{1,0:T(8,128)(2,1)S(1)}, bf16[2048,512]{1,0:T(8,128)(2,1)S(1)}, u32[]{:S(2)}, u32[]{:S(2)}) collective-permute-start(bf16[2048,512]{1,0:T(8,128)(2,1)S(1)} %copy-done.33), channel_id=1, source_target_pairs={{0,8},{4,12},{8,0},{12,4},{1,9},{5,13},{9,1},{13,5},{2,10},{6,14},... | collective-permute-start | bytes 6291464 | tf_op jit(solution)/shard_map/ppermute | solution.py:27
  951.7 34.3 %collective-permute-start.86 = (bf16[512,512]{1,0:T(8,128)(2,1)S(1)}, bf16[512,512]{1,0:T(8,128)(2,1)S(1)}, u32[]{:S(2)}, u32[]{:S(2)}) collective-permute-start(bf16[512,512]{1,0:T(8,128)(2,1)S(1)} %add_convert_fusion.7), channel_id=1, source_target_pairs={{0,4},{4,0},{8,12},{12,8},{1,5},{5,1},{9,13},{13,9},{2,6},{6,2},{1... | collective-permute-start | bytes 1572872 | tf_op jit(solution)/shard_map/ppermute | solution.py:23
  (200 other events, 4107.3 us)

commit v3 on v1

v3 whole, which is shorter than its diff:
```python
import jax
import jax.numpy as jnp
from jax import lax
from jax.experimental import pallas as pl
from jax.experimental.pallas import tpu as pltpu
from jax.sharding import PartitionSpec as P

HD = 128
NORM_EPS = 1e-05
MASKED = -1e30
LOG2E = 1.4426950408889634
F32 = jnp.float32
BF16 = jnp.bfloat16

ROOM = 44 * 2**20
X_SWAP = [(0, 1), (1, 0)]
ANY = pl.BlockSpec(memory_space=pl.ANY)


def xor_pairs(count, bit):
    return [(j, j ^ bit) for j in range(count)]


def core_swap(values):
    return lax.ppermute(values, "ctx", xor_pairs(lax.axis_size("ctx"), 1))


def y_swap(values):
    return lax.ppermute(values, "ctx", xor_pairs(lax.axis_size("ctx"), 2))


def x_swap(values):
    return lax.ppermute(values, "fsdp", X_SWAP)


def tp_swap(values, bit):
    return lax.ppermute(values, "tp", xor_pairs(lax.axis_size("tp"), bit))


def norm_parts(values):
    centred = values - jnp.mean(values, axis=-1, keepdims=True)
    norm_scale = lax.rsqrt(jnp.mean(centred * centred, axis=-1, keepdims=True) + NORM_EPS)
    return (centred * norm_scale, norm_scale)


def norm_back(grad_norm, gain, normed, norm_scale):
    lifted = grad_norm * gain
    return norm_scale * (
        lifted
        - jnp.mean(lifted, axis=-1, keepdims=True)
        - normed * jnp.mean(lifted * normed, axis=-1, keepdims=True)
    )


def dot(a, b):
    return jnp.dot(a, b, preferred_element_type=F32)


def dot_t(a, b):
    return lax.dot_general(a, b, (((1,), (1,)), ((), ())), preferred_element_type=F32)


def t_dot(a, b):
    return lax.dot_general(a, b, (((0,), (0,)), ((), ())), preferred_element_type=F32)


def piece(values, start, count, axis):
    return lax.dynamic_slice_in_dim(values, start, count, axis)


def to_relative(values):
    i, c = lax.axis_index("fsdp"), lax.axis_index("ctx") & 1
    size = values.shape[-1] // 4
    axis = values.ndim - 1
    return jnp.concatenate(
        [piece(values, (((k & 1) ^ i) * 2 + ((k >> 1) ^ c)) * size, size, axis) for k in range(4)],
        axis=axis,
    )


def to_natural(values):
    i, c = lax.axis_index("fsdp"), lax.axis_index("ctx") & 1
    size = values.shape[-1] // 4
    axis = values.ndim - 1
    return jnp.concatenate(
        [piece(values, (((b >> 1) ^ i) + 2 * ((b & 1) ^ c)) * size, size, axis) for b in range(4)],
        axis=axis,
    )


def mix_rows(values):
    n = lax.axis_size("tp")
    z = lax.axis_index("tp")
    size = values.shape[0] // n
    return jnp.concatenate([piece(values, (z ^ k) * size, size, 0) for k in range(n)], axis=0)


class Order:
    def __init__(self, place):
        self.place = place
        self.last = None

    def call(self, body, name, grid, ins, outs, scratch=(), flops=0, after=(), alias=None):
        spare = list(after)
        if self.last is not None and self.last is not alias:
            spare.append(self.last)
        if alias is not None:
            spare.append(alias)
        first = 1 + len(ins)

        def kernel(*refs):
            body(*refs[:first], *refs[first + len(spare) :])

        moved = sum(a.size * a.dtype.itemsize for a, unused in ins)
        moved += sum(2 * jnp.dtype(d).itemsize * len(s) for s, d, unused in outs)
        result = pl.pallas_call(
            kernel,
            grid_spec=pltpu.PrefetchScalarGridSpec(
                num_scalar_prefetch=1,
                grid=grid,
                in_specs=[spec for unused, spec in ins] + [ANY] * len(spare),
                out_specs=[spec for unused, also, spec in outs],
                scratch_shapes=list(scratch),
            ),
            out_shape=[jax.ShapeDtypeStruct(s, d) for s, d, unused in outs],
            input_output_aliases={} if alias is None else {len(ins) + len(spare): 0},
            compiler_params=pltpu.CompilerParams(vmem_limit_bytes=ROOM),
            cost_estimate=pl.CostEstimate(
                flops=int(flops), bytes_accessed=int(moved), transcendentals=0
            ),
            name=name,
        )(self.place, *[a for a, unused in ins], *spare)
        self.last = result[-1]
        return result

    def tie(self, *values):
        count = len(values)

        def kernel(place, *refs):
            del place, refs

        tied = pl.pallas_call(
            kernel,
            grid_spec=pltpu.PrefetchScalarGridSpec(
                num_scalar_prefetch=1,
                grid=(1,),
                in_specs=[ANY] * (count + 1),
                out_specs=[ANY] * count,
            ),
            out_shape=[jax.ShapeDtypeStruct(a.shape, a.dtype) for a in values],
            input_output_aliases={1 + k: k for k in range(count)},
            name="tie",
        )(self.place, *values, self.last)
        self.last = tied[0]
        return tied if count > 1 else tied[0]


def whole(shape):
    return pl.BlockSpec(shape, lambda *_: (0,) * len(shape))


def natural_of(place, k):
    return ((k & 1) ^ place[1]) * 2 + ((k >> 1) ^ place[0])


def own_half(place, which):
    return place[0] if which == 0 else 1 - place[0]


def take_half(order, weight, base, count, axis, after=()):
    unused, rows, cols = weight.shape
    if axis == 0:
        rows = rows // 2
    else:
        cols = cols // 2
    tile = min(rows, 512)

    def body(place, src, dst):
        dst[...] = src[...]

    def spot(g, i, place):
        if axis == 0:
            return (base + g, place[0] * (rows // tile) + i, 0)
        return (base + g, i, place[0])

    block = (1, tile, cols)
    return order.call(
        body,
        "take_half",
        (count, rows // tile),
        [(weight, pl.BlockSpec(block, spot))],
        [((count, rows, cols), BF16, pl.BlockSpec(block, lambda g, i, place: (g, i, 0)))],
        after=after,
    )[0]


def norm_in(order, block_in, gain, shift, n):
    seqs, span, width = block_in.shape
    part = span // n
    size = width // 4

    def body(place, src, gain_ref, shift_ref, normed_ref, own_ref, line):
        for k in range(n):
            rows = pl.ds(pl.multiple_of((place[2] ^ k) * part, part), part)
            for s in range(seqs):
                values = src[s, rows, :].astype(F32)
                normed, unused = norm_parts(values)
                line[...] = (normed * gain_ref[...] + shift_ref[...]).astype(BF16)
                to = (k * seqs + s) * part
                for p in range(4):
                    cols = pl.ds(pl.multiple_of(natural_of(place, p) * size, size), size)
                    normed_ref[to : to + part, p * size : (p + 1) * size] = line[:, cols]
                    if k == 0:
                        own_ref[to : to + part, p * size : (p + 1) * size] = src[s, rows, cols]

    return order.call(
        body,
        "norm_in",
        (1,),
        [
            (block_in, whole(block_in.shape)),
            (gain, whole((1, width))),
            (shift, whole((1, width))),
        ],
        [
            ((seqs * span, width), BF16, whole((seqs * span, width))),
            ((seqs * part, width), BF16, whole((seqs * part, width))),
        ],
        [pltpu.VMEM((part, width), BF16)],
    )


def cot_in(order, out_grad, valid, n):
    seqs, span, width = out_grad.shape
    part = span // n
    size = width // 4

    def body(place, src, valid_ref, cot_ref):
        for k in range(n):
            rows = pl.ds(pl.multiple_of((place[2] ^ k) * part, part), part)
            for s in range(seqs):
                to = (k * seqs + s) * part
                for p in range(4):
                    cols = pl.ds(pl.multiple_of(natural_of(place, p) * size, size), size)
                    values = src[s, rows, cols].astype(F32) * valid_ref[s, rows, :]
                    cot_ref[to : to + part, p * size : (p + 1) * size] = values.astype(BF16)

    shape = (seqs * span, width)
    return order.call(
        body,
        "cot_in",
        (1,),
        [(out_grad, whole(out_grad.shape)), (valid, whole(valid.shape))],
        [(shape, BF16, whole(shape))],
    )[0]


def by_sequence(values, n, seqs):
    rows, width = values.shape
    return values.reshape(n, seqs, rows // n // seqs, width)


def project(order, n1, weights, base, far_c, far_n, bias, name):
    count, size, local = far_c.shape
    one = isinstance(n1, tuple)
    if one:
        values, s = n1
        n, unused, part, width = values.shape
        rows = n * part
        spec = pl.BlockSpec((n, 1, part, width), lambda g, place: (0, s, 0, 0))
    else:
        values = n1
        rows, width = values.shape
        spec = whole((rows, width))

    def body(place, x, a, b, c, d, bias_ref, out):
        total = bias_ref[0].astype(F32)
        for p, ref in enumerate((a, b, c, d)):
            cols = slice(p * size, (p + 1) * size)
            some = x[:, 0, :, cols].reshape(rows, size) if one else x[:, cols]
            total = total + dot(some, ref[0])
        out[0] = total.astype(BF16)

    block = (1, size, local)
    near = [
        pl.BlockSpec(block, lambda g, place, h=h: (base + g, own_half(place, h), 0)) for h in (0, 1)
    ]
    away = pl.BlockSpec(block, lambda g, place: (g, 0, 0))
    return order.call(
        body,
        name,
        (count,),
        [
            (values, spec),
            (weights, near[0]),
            (far_c, away),
            (weights, near[1]),
            (far_n, away),
            (bias, pl.BlockSpec((1, 1, local), lambda g, place: (g, 0, 0))),
        ],
        [((count, rows, local), BF16, pl.BlockSpec((1, rows, local), lambda g, place: (g, 0, 0)))],
        flops=2 * rows * width * local * count,
    )[0]


def row_ins(parts, part, width):
    return [
        (array, pl.BlockSpec((part, width), lambda *_, k=k: (k, 0))) for array, k in parts
    ]


def row_outs(n, block, width):
    counts = (2, 1, 1) if n == 4 else (n // 2, n // 2)
    return [((c * block, width), BF16, whole((c * block, width))) for c in counts]


def put_rows(outs, block, n, cols, rows):
    for k in range(n):
        which, spot = (k % 2, k // 2)
        if n == 4 and which:
            which, spot = 1 + spot, 0
        outs[which][spot * block : (spot + 1) * block, cols] = rows[k * block : (k + 1) * block]


def col_pieces(weight, far_c, far_n, tile):
    unused, units, size = far_c.shape
    steps = size // tile
    block = (1, units, tile)
    near = [
        pl.BlockSpec(block, lambda g, place, h=h: (0, 0, own_half(place, h) * steps + g))
        for h in (0, 1)
    ]
    away = pl.BlockSpec(block, lambda g, place: (0, 0, g))
    return [(weight, near[0]), (far_c, away), (weight, near[1]), (far_n, away)], steps


def row_pieces(weight, far_c, far_n, tile):
    unused, size, units = far_c.shape
    steps = size // tile
    block = (1, tile, units)
    near = [
        pl.BlockSpec(block, lambda g, place, h=h: (0, own_half(place, h) * steps + g, 0))
        for h in (0, 1)
    ]
    away = pl.BlockSpec(block, lambda g, place: (0, g, 0))
    return [(weight, near[0]), (far_c, away), (weight, near[1]), (far_n, away)], steps


def to_features(order, values, pieces, steps, tile, turned, n, width, name, seqs=None):
    rows, units = values.shape
    block = rows // n
    size = width // 4
    times = dot_t if turned else dot

    def body(place, x, a, b, c, d, *outs):
        g = pl.program_id(0)
        for p, ref in enumerate((a, b, c, d)):
            got = times(x[...], ref[0]).astype(BF16)
            cols = pl.ds(pl.multiple_of(p * size + g * tile, tile), tile)
            if not seqs:
                put_rows(outs, block, n, cols, got)
                continue
            part = block // seqs
            for k in range(n):
                spot = pl.ds(pl.multiple_of((place[2] ^ k) * part, part), part)
                for s in range(seqs):
                    start = k * block + s * part
                    outs[0][s, spot, cols] = got[start : start + part]

    outs = row_outs(n, block, width)
    if seqs:
        shape = (seqs, rows // seqs, width)
        outs = [(shape, BF16, whole(shape))]
    return order.call(
        body,
        name,
        (steps,),
        [(values, whole((rows, units)))] + pieces,
        outs,
        flops=2 * rows * units * width,
    )


def add_rows(order, a, b, block):
    width = a[0].shape[1]

    def body(place, x, y, out):
        out[...] = (x[...].astype(F32) + y[...].astype(F32)).astype(BF16)

    return order.call(
        body,
        "add_rows",
        (1,),
        row_ins([a, b], block, width),
        [((block, width), BF16, whole((block, width)))],
    )[0]


def sum_all(refs):
    total = refs[0][...].astype(F32)
    for ref in refs[1:]:
        total = total + ref[...].astype(F32)
    return total


def norm_mid(order, parts, own, bias, gain, shift):
    part, width = own.shape
    count = len(parts)

    def body(place, *refs):
        own_ref, bias_ref, gain_ref, shift_ref, mid_ref, normed_ref = refs[count:]
        mid = own_ref[...].astype(F32) + sum_all(refs[:count]) + bias_ref[...]
        mid_ref[...] = mid
        normed, unused = norm_parts(mid)
        normed_ref[...] = (normed * gain_ref[...] + shift_ref[...]).astype(BF16)

    block, line = whole((part, width)), whole((1, width))
    return order.call(
        body,
        "norm_mid",
        (1,),
        row_ins(parts, part, width) + [(own, block), (bias, line), (gain, line), (shift, line)],
        [((part, width), F32, block), ((part, width), BF16, block)],
    )


def back_mid(order, parts, mid, cot, gain):
    part, width = mid.shape
    count = len(parts)

    def body(place, *refs):
        mid_ref, cot_ref, gain_ref, stats, grad_ref, low_ref = refs[count:]
        g2 = sum_all(refs[:count])
        normed, norm_scale = norm_parts(mid_ref[...])
        cotan = cot_ref[...].astype(F32)
        grad = cotan + norm_back(g2, gain_ref[...], normed, norm_scale)
        low = grad.astype(BF16)
        grad_ref[...] = grad
        low_ref[...] = low
        rows = (low.astype(F32), g2 * normed, g2, cotan)
        for k, values in enumerate(rows):
            stats[k : k + 1, :] = jnp.sum(values, axis=0, keepdims=True)
        stats[4:8, :] = jnp.zeros((4, width), F32)

    block, line = whole((part, width)), whole((1, width))
    return order.call(
        body,
        "back_mid",
        (1,),
        row_ins(parts, part, width) + [(mid, block), (cot, block), (gain, line)],
        [
            ((8, width), F32, whole((8, width))),
            ((part, width), F32, block),
            ((part, width), BF16, block),
        ],
    )


def back_in(order, parts, own, grad_mid, gain):
    part, width = own.shape
    count = len(parts)
    size = width // 4

    def body(place, *refs):
        own_ref, mid_ref, gain_ref, stats, low_ref, line = refs[count:]
        g1 = sum_all(refs[:count])
        normed, norm_scale = norm_parts(own_ref[...].astype(F32))
        grad = mid_ref[...] + norm_back(g1, gain_ref[...], normed, norm_scale)
        line[...] = grad.astype(BF16)
        for p in range(4):
            cols = pl.ds(pl.multiple_of(natural_of(place, p) * size, size), size)
            low_ref[:, cols] = line[:, p * size : (p + 1) * size]
        for k, values in enumerate((g1 * normed, g1)):
            stats[k : k + 1, :] = jnp.sum(values, axis=0, keepdims=True)
        stats[2:8, :] = jnp.zeros((6, width), F32)

    block, line = whole((part, width)), whole((1, width))
    return order.call(
        body,
        "back_in",
        (1,),
        row_ins(parts, part, width) + [(own, block), (grad_mid, block), (gain, line)],
        [((8, width), F32, whole((8, width))), ((part, width), BF16, block)],
        [pltpu.VMEM((part, width), BF16)],
    )


def gather_rows(refs, store):
    part = refs[0].shape[0]
    for k, ref in enumerate(refs):
        store[k * part : (k + 1) * part, :] = ref[...]


def active_grad(order, cot, weight, far_c, far_n):
    span, width = cot.shape
    units = weight.shape[1]
    size = width // 4
    tile = min(units, 512)

    def body(place, x, a, b, c, d, out):
        total = dot_t(x[:, :size], a[0])
        for p, ref in enumerate((b, c, d)):
            total = total + dot_t(x[:, (p + 1) * size : (p + 2) * size], ref[0])
        out[...] = total

    block = (1, tile, size)
    near = [pl.BlockSpec(block, lambda g, place, h=h: (0, g, own_half(place, h))) for h in (0, 1)]
    away = pl.BlockSpec(block, lambda g, place: (0, g, 0))
    return order.call(
        body,
        "active_grad",
        (units // tile,),
        [
            (cot, whole((span, width))),
            (weight, near[0]),
            (far_c, away),
            (weight, near[1]),
            (far_n, away),
        ],
        [((span, units), F32, pl.BlockSpec((span, tile), lambda g, place: (0, g)))],
        flops=2 * span * units * width,
    )[0]


def feed(order, n2_parts, weight, far_c, far_n, bias, grad_active):
    n = len(n2_parts)
    width = n2_parts[0][0].shape[1]
    span = cot_rows = grad_active.shape[0]
    part = cot_rows // n
    units = weight.shape[2]
    size = width // 4
    tile = min(units, 512)

    def body(place, *refs):
        a, b, c, d, bias_ref, ga_ref, sums, act_ref, gh_ref, x = refs[n:]

        @pl.when(pl.program_id(0) == 0)
        def _():
            gather_rows(refs[:n], x)

        rate = 0.7978845608028654
        step = min(tile, 256)
        for start in range(0, tile, step):
            cols = slice(start, start + step)
            hidden = bias_ref[:, cols] + dot(x[:, :size], a[0, :, cols])
            for p, ref in enumerate((b, c, d)):
                hidden = hidden + dot(x[:, (p + 1) * size : (p + 2) * size], ref[0, :, cols])
            square = hidden * hidden
            bend = jnp.tanh(hidden * (rate + rate * 0.044715 * square))
            half = 0.5 + 0.5 * bend
            act_ref[:, cols] = (hidden * half).astype(BF16)
            turn = half - half * bend
            slope = half + hidden * turn * (rate + rate * 0.134145 * square)
            gh = (ga_ref[:, cols] * slope).astype(BF16)
            gh_ref[:, cols] = gh
            sums[:, cols] = jnp.sum(gh.astype(F32), axis=0, keepdims=True)

    block = (1, size, tile)
    near = [pl.BlockSpec(block, lambda g, place, h=h: (0, own_half(place, h), g)) for h in (0, 1)]
    away = pl.BlockSpec(block, lambda g, place: (0, 0, g))
    cols = pl.BlockSpec((span, tile), lambda g, place: (0, g))
    line = pl.BlockSpec((1, tile), lambda g, place: (0, g))
    return order.call(
        body,
        "feed",
        (units // tile,),
        row_ins(n2_parts, part, width)
        + [
            (weight, near[0]),
            (far_c, away),
            (weight, near[1]),
            (far_n, away),
            (bias, line),
            (grad_active, cols),
        ],
        [((1, units), F32, line), ((span, units), BF16, cols), ((span, units), BF16, cols)],
        [pltpu.VMEM((span, width), BF16)],
        flops=2 * span * units * width,
    )


def heads_grad(order, gm_parts, span, weight, far_c, far_n):
    n = len(gm_parts)
    width = gm_parts[0][0].shape[1]
    part = span // n
    local = weight.shape[1]
    size = width // 4

    def body(place, *refs):
        a, b, c, d, out, x = refs[n:]
        gather_rows(refs[:n], x)
        total = dot_t(x[:, :size], a[0])
        for p, ref in enumerate((b, c, d)):
            total = total + dot_t(x[:, (p + 1) * size : (p + 2) * size], ref[0])
        out[...] = total.astype(BF16)

    pieces, unused = col_pieces(weight, far_c, far_n, size)
    return order.call(
        body,
        "heads_grad",
        (1,),
        row_ins(gm_parts, part, width) + pieces,
        [((span, local), BF16, whole((span, local)))],
        [pltpu.VMEM((span, width), BF16)],
        flops=2 * span * local * width,
    )[0]


def head_rows(ref, h):
    n, unused, part, size = ref.shape
    return ref[:, 0, :, h * HD : (h + 1) * HD].reshape(n * part, HD)


def put_head(ref, h, turned):
    n, unused, part, size = ref.shape
    ref[:, 0, :, h * HD : (h + 1) * HD] = turned.T.astype(BF16).reshape(n, part, HD)


def head_of(kv, j, h):
    return kv[j, :, h * HD : (h + 1) * HD]


def fwd_kernel(live, q, kv0, kv1, kv2, kv3, kseg, qseg, kpos, qpos, out, lse, m_s, l_s, acc_s):
    heads = range(q.shape[3] // HD)
    rate = HD ** (-0.5) * LOG2E

    def scores(kv, b, h):
        t = dot_t(head_of(kv, 0, h), head_rows(q, h)) * rate
        allowed = kseg[b] == qseg[...]
        if b == 0:
            allowed = allowed & (kpos[...] <= qpos[...])
        return jnp.where(allowed, t, MASKED)

    for h in heads:
        t = scores(kv0, 0, h)
        top = jnp.max(t, axis=0, keepdims=True)
        p = jnp.exp2(t - top)
        m_s[h] = top
        l_s[h] = jnp.sum(p, axis=0, keepdims=True)
        acc_s[h] = t_dot(head_of(kv0, 1, h), p.astype(BF16))
    for b, kv in ((1, kv1), (2, kv2), (3, kv3)):

        @pl.when(live[4 + b] > 0)
        def _(b=b, kv=kv):
            for h in heads:
                t = scores(kv, b, h)
                old = m_s[h]
                top = jnp.maximum(old, jnp.max(t, axis=0, keepdims=True))
                p = jnp.exp2(t - top)
                fade = jnp.exp2(old - top)
                m_s[h] = top
                l_s[h] = l_s[h] * fade + jnp.sum(p, axis=0, keepdims=True)
                acc_s[h] = acc_s[h] * fade + t_dot(head_of(kv, 1, h), p.astype(BF16))

    for h in heads:
        total = l_s[h]
        put_head(out, h, acc_s[h] / total)
        lse[h] = m_s[h] + jnp.log2(total)


def bwd_kernel(
    live,
    q,
    kv0,
    kv1,
    kv2,
    kv3,
    kseg,
    qseg,
    kpos,
    qpos,
    att,
    grad,
    lse,
    gq,
    near,
    far,
    gq_s,
    delta_s,
):
    heads = range(q.shape[3] // HD)
    rate = HD ** (-0.5) * LOG2E
    factor = HD ** (-0.5)

    def grads(kv, b, h):
        queries, grad_out, keys = head_rows(q, h), head_rows(grad, h), head_of(kv, 0, h)
        t = dot_t(keys, queries) * rate
        allowed = kseg[b] == qseg[...]
        if b == 0:
            allowed = allowed & (kpos[...] <= qpos[...])
        p = jnp.exp2(jnp.where(allowed, t, MASKED) - lse[h])
        gv = dot(p.astype(BF16), grad_out)
        gp = dot_t(head_of(kv, 1, h), grad_out)
        gs = (p * (gp - delta_s[h])).astype(BF16)
        gk = dot(gs, queries) * factor
        return gk.astype(BF16), gv.astype(BF16), t_dot(keys, gs)

    def put(place, slot, h, gk, gv):
        cols = slice(h * HD, (h + 1) * HD)
        place[slot, 0, :, cols] = gk
        place[slot, 1, :, cols] = gv

    for h in heads:
        product = head_rows(grad, h).astype(F32) * head_rows(att, h).astype(F32)
        delta_s[h] = jnp.sum(product.T, axis=0, keepdims=True)
    for h in heads:
        gk, gv, turned = grads(kv0, 0, h)
        put(near, 0, h, gk, gv)
        gq_s[h] = turned
    for b, kv, place, slot in ((1, kv1, far, 0), (2, kv2, near, 1), (3, kv3, far, 1)):

        @pl.when(live[4 + b] > 0)
        def _(b=b, kv=kv, place=place, slot=slot):
            for h in heads:
                gk, gv, turned = grads(kv, b, h)
                put(place, slot, h, gk, gv)
                gq_s[h] += turned

        @pl.when(live[4 + b] == 0)
        def _(place=place, slot=slot):
            place[slot] = jnp.zeros(place.shape[1:], BF16)

    for h in heads:
        put_head(gq, h, gq_s[h] * factor)


def attend_ins(queries, s, kvs, marks):
    n, unused, part, local = queries.shape
    span = n * part
    heads = local // HD
    some = min(heads, 2)
    cols = some * HD
    head = pl.BlockSpec((n, 1, part, cols), lambda h, *_: (0, s, 0, h))
    pair = pl.BlockSpec((2, span, cols), lambda h, *_: (0, 0, h))
    stat = pl.BlockSpec((some, 1, span), lambda h, *_: (h, 0, 0))
    both = pl.BlockSpec((2, 2, span, cols), lambda h, *_: (0, 0, 0, h))
    shapes = ((4, span, 1), (1, span), (span, 1), (1, span))
    ins = [(queries, head)] + [(kv, pair) for kv in kvs]
    ins += [(mark, whole(shape)) for mark, shape in zip(marks, shapes)]
    return head, stat, both, ins, span, heads, some


def attend(order, queries, s, kvs, marks, sofar):
    head, stat, both, ins, span, heads, some = attend_ins(queries, s, kvs, marks)
    return order.call(
        fwd_kernel,
        "attend",
        (heads // some,),
        ins,
        [(queries.shape, BF16, head), ((heads, 1, span), F32, stat)],
        [
            pltpu.VMEM((some, 1, span), F32),
            pltpu.VMEM((some, 1, span), F32),
            pltpu.VMEM((some, HD, span), F32),
        ],
        flops=16 * heads * span * span * HD,
        alias=sofar,
    )


def attend_back(order, queries, s, kvs, marks, attended, grad_att, log_total, sofar):
    head, stat, both, ins, span, heads, some = attend_ins(queries, s, kvs, marks)
    pairs = (2, 2, span, heads * HD)
    return order.call(
        bwd_kernel,
        "attend_back",
        (heads // some,),
        ins + [(attended, head), (grad_att, head), (log_total, stat)],
        [(queries.shape, BF16, head), (pairs, BF16, both), (pairs, BF16, both)],
        [pltpu.VMEM((some, HD, span), F32), pltpu.VMEM((some, 1, span), F32)],
        flops=40 * heads * span * span * HD,
        alias=sofar,
    )


def add_pair(order, near, got):
    shape = near.shape[1:]

    def body(place, a, b, base, far):
        base[...] = a[0].astype(F32) + b[0].astype(F32)
        far[...] = (a[1].astype(F32) + b[1].astype(F32)).astype(BF16)

    return order.call(
        body,
        "add_pair",
        (1,),
        [(near, whole(near.shape)), (got, whole(near.shape))],
        [(shape, F32, whole(shape)), (shape, BF16, whole(shape))],
    )


def back_project(order, gq, bases, gots, weights, q_c, q_n, kv_c, kv_n, n, width):
    rows, local = gq.shape
    seqs = len(bases)
    block = rows // n
    part = block // seqs
    size = width // 4
    tile = min(size, 256)
    steps = size // tile

    def body(place, gq_ref, *refs):
        base_refs, got_refs = refs[:seqs], refs[seqs : 2 * seqs]
        a, c, qb, qd, kb, kd, gkv, *outs = refs[2 * seqs :]
        g = pl.program_id(0)

        @pl.when(g == 0)
        def _():
            for s in range(seqs):
                for k in range(n):
                    to, at = k * block + s * part, k * part
                    gkv[:, to : to + part, :] = (
                        base_refs[s][:, at : at + part, :]
                        + got_refs[s][:, at : at + part, :].astype(F32)
                    ).astype(BF16)

        grads = (gq_ref[...], gkv[0], gkv[1])
        mine = ((a, 0), (a, 1), (a, 2))
        mine_n = ((c, 0), (c, 1), (c, 2))
        far = ((qb, 0), (kb, 0), (kb, 1))
        far_n = ((qd, 0), (kd, 0), (kd, 1))
        for p, sources in enumerate((mine, far, mine_n, far_n)):
            total = None
            for grad, (ref, j) in zip(grads, sources):
                more = dot_t(grad, ref[j])
                total = more if total is None else total + more
            cols = pl.ds(pl.multiple_of(p * size + g * tile, tile), tile)
            put_rows(outs, block, n, cols, total.astype(BF16))

    near = [
        pl.BlockSpec(
            (3, tile, local), lambda g, place, h=h: (0, own_half(place, h) * steps + g, 0)
        )
        for h in (0, 1)
    ]
    one = pl.BlockSpec((1, tile, local), lambda g, place: (0, g, 0))
    two = pl.BlockSpec((2, tile, local), lambda g, place: (0, g, 0))
    shape = (2, rows, local)
    return order.call(
        body,
        "back_project",
        (steps,),
        [(gq, whole((rows, local)))]
        + [(a, whole(a.shape)) for a in (*bases, *gots)]
        + [(weights, near[0]), (weights, near[1])]
        + [(q_c, one), (q_n, one), (kv_c, two), (kv_n, two)],
        [(shape, BF16, whole(shape))] + row_outs(n, block, width),
        flops=6 * rows * local * width,
    )


def weight_grad_rows(order, lefts, rights, name, more=None):
    span, units = rights[0].shape
    count = 1 if more is None else 1 + more[0].shape[0]
    width = lefts[0][0][0].shape[1]
    part = span // len(lefts[0])
    size = width // 4
    total_lefts = sum(len(parts) for parts in lefts)
    pairs = len(lefts)
    given = list(rights) + list(more or [])

    def body(place, *refs):
        right_refs = refs[total_lefts : total_lefts + pairs]
        more_refs = refs[total_lefts + pairs : -3]
        keep, send, x = refs[-3:]
        gather_rows(refs[:total_lefts], x)
        q = pl.program_id(0)
        for j in range(count):
            total = None
            for s in range(pairs):
                right = more_refs[s][j - 1] if j else right_refs[s][...]
                product = t_dot(x[s * span : (s + 1) * span, :], right)
                total = product if total is None else total + product
            low = total.astype(BF16)

            @pl.when(q < 2)
            def _(j=j, low=low):
                keep[0, j] = low

            @pl.when(q >= 2)
            def _(j=j, low=low):
                send[0, j] = low

    shape = (2, count, size, units)
    block = (1, count, size, units)
    return order.call(
        body,
        name,
        (4,),
        [
            (a, pl.BlockSpec((part, size), lambda q, place, k=k: (k, q)))
            for parts in lefts
            for a, k in parts
        ]
        + [(a, whole(a.shape)) for a in given],
        [
            (shape, BF16, pl.BlockSpec(block, lambda q, place: (jnp.minimum(q, 1), 0, 0, 0))),
            (shape, BF16, pl.BlockSpec(block, lambda q, place: (jnp.maximum(q - 2, 0), 0, 0, 0))),
        ],
        [pltpu.VMEM((pairs * span, size), BF16)],
        flops=2 * count * pairs * span * units * width,
    )


def weight_grad_cols(order, lefts, rights, name):
    span, units = lefts[0].shape
    width = rights[0][0][0].shape[1]
    part = span // len(rights[0])
    size = width // 4
    tile = min(units, 256)
    pairs = len(lefts)

    def body(place, *refs):
        left_refs, right_refs = refs[:pairs], refs[pairs:-3]
        keep, send, y = refs[-3:]

        @pl.when(pl.program_id(0) == 0)
        def _():
            gather_rows(right_refs, y)

        total = None
        for s, ref in enumerate(left_refs):
            more = t_dot(ref[...], y[s * span : (s + 1) * span, :])
            total = more if total is None else total + more
        for q in range(4):
            (keep, send)[q // 2][q % 2, 0] = total[:, q * size : (q + 1) * size].astype(BF16)

    shape = (2, 1, units, size)
    out = pl.BlockSpec((2, 1, tile, size), lambda g, place: (0, 0, g, 0))
    return order.call(
        body,
        name,
        (units // tile,),
        [(a, pl.BlockSpec((span, tile), lambda g, place: (0, g))) for a in lefts]
        + [item for parts in rights for item in row_ins(parts, part, width)],
        [(shape, BF16, out), (shape, BF16, out)],
        [pltpu.VMEM((pairs * span, width), BF16)],
        flops=2 * pairs * span * units * width,
    )


class WeightSum:
    def __init__(self, order, keep, send):
        self.order = order
        self.keep = keep
        self.got = core_swap(send)
        self.shape = keep.shape[1:]

    def add(self, items, name):
        count, rows, cols = self.shape
        tile = min(rows, 512)

        def body(place, *refs):
            total = refs[0][...].astype(F32)
            for ref in refs[1:-1]:
                total = total + ref[...].astype(F32)
            refs[-1][...] = total.astype(BF16).reshape(refs[-1].shape)

        def quarter(k):
            return pl.BlockSpec((1, 1, tile, cols), lambda j, i, place: (k, j, i, 0))

        plain = pl.BlockSpec((1, tile, cols), lambda j, i, place: (j, i, 0))
        ins = []
        for array, k in items:
            if k is None:
                ins.append((array[None], pl.BlockSpec((1, 1, tile, cols), lambda j, i, place: (0, j, i, 0))))
            else:
                ins.append((array, quarter(k)))
        return self.order.call(
            body, name, (count, rows // tile), ins, [(self.shape, BF16, plain)]
        )[0]

    def to_x(self):
        self.got_x = x_swap(self.add([(self.keep, 1), (self.got, 1)], "sum_core"))

    def to_y(self):
        self.four = self.add([(self.keep, 0), (self.got, 0), (self.got_x, None)], "sum_x")
        self.got_y = y_swap(self.four)

    def to_core(self):
        self.total = self.add([(self.four, None), (self.got_y, None)], "sum_y")
        self.other = core_swap(self.total)

    def finish(self, axis, base=0, full=None, sofar=None):
        count, rows, cols = self.shape
        tile = min(rows, 512)
        steps = rows // tile

        def body(place, a, b, out):
            mine = jnp.full(a.shape, (pl.program_id(0) == place[0]).astype(jnp.int32)) > 0
            out[...] = jnp.where(mine, a[...].astype(F32), b[...].astype(F32))

        block = (1, tile, cols)
        source = pl.BlockSpec(block, lambda h, j, i, place: (j, i, 0))
        if axis == 0:
            shape = (full or count, 2 * rows, cols)
            spec = pl.BlockSpec(block, lambda h, j, i, place: (base + j, h * steps + i, 0))
        else:
            shape = (full or count, rows, 2 * cols)
            spec = pl.BlockSpec(block, lambda h, j, i, place: (base + j, i, h))
        return self.order.call(
            body,
            "finish",
            (2, count, steps),
            [(self.total, source), (self.other, source)],
            [(shape, F32, spec)],
            alias=sofar,
        )[0]


def out_rows(order, mid, summed, bias):
    seqs, part, width = summed.shape
    size = width // 4

    def body(place, mid_ref, sum_ref, bias_ref, out, line):
        for s in range(seqs):
            rows = slice(s * part, (s + 1) * part)
            line[...] = (mid_ref[rows] + sum_ref[s].astype(F32) + bias_ref[...]).astype(BF16)
            for p in range(4):
                cols = pl.ds(pl.multiple_of(natural_of(place, p) * size, size), size)
                out[s, :, cols] = line[:, p * size : (p + 1) * size]

    shape = (seqs, part, width)
    return order.call(
        body,
        "out_rows",
        (1,),
        [(mid, whole(mid.shape)), (summed, whole(shape)), (bias, whole((1, width)))],
        [(shape, BF16, whole(shape))],
        [pltpu.VMEM((part, width), BF16)],
    )[0]


def assemble(order, blocks, seqs, block):
    n = len(blocks)
    width = blocks[0][0].shape[1]
    part = block // seqs

    def body(place, *refs):
        out = refs[-1]
        for k in range(n):
            rows = pl.ds(pl.multiple_of((place[2] ^ k) * part, part), part)
            for s in range(seqs):
                out[s, rows, :] = refs[k][s * part : (s + 1) * part]

    shape = (seqs, n * part, width)
    return order.call(
        body,
        "assemble",
        (1,),
        row_ins(blocks, block, width),
        [(shape, BF16, whole(shape))],
    )[0]


def sum_first(parts):
    return tp_swap(parts[-1], 1)


def sum_second(order, parts, got, n, block):
    keep = parts[0]
    if n == 2:
        return [(keep, 0), (got, 0)]
    if n == 4:
        passed = add_rows(order, (keep, 1), (got, 0), block)
        return [(keep, 0), (tp_swap(passed, 2), 0), (tp_swap(parts[1], 1), 0)]
    total = (keep.astype(F32) + got.astype(F32)).astype(BF16)
    held = [total[k * block : (k + 1) * block] for k in range(n // 2)]
    bit = 2
    while bit < n:
        got = tp_swap(jnp.concatenate(held[1::2], axis=0), bit)
        held = [
            (a.astype(F32) + got[j * block : (j + 1) * block].astype(F32)).astype(BF16)
            for j, a in enumerate(held[::2])
        ]
        bit *= 2
    return [(held[0], 0)]


class Gather:
    def __init__(self, order, own):
        self.order = order
        self.own = own
        self.n = lax.axis_size("tp")
        if self.n == 4:
            self.far = tp_swap(own, 2)
            self.near = tp_swap(own, 1)

    def pass_on(self):
        if self.n == 4:
            self.far, self.near = self.order.tie(self.far, self.near)
            self.last = tp_swap(self.far, 1)

    def blocks(self):
        if self.n == 4:
            return [(a, 0) for a in (self.own, self.near, self.far, self.last)]
        blocks = [self.own]
        size = self.own.shape[0]
        bit = 1
        while bit < self.n:
            got = tp_swap(jnp.concatenate(blocks, axis=0), bit)
            blocks = blocks + [got[k * size : (k + 1) * size] for k in range(bit)]
            bit *= 2
        return [(block, 0) for block in blocks]


def sum_pairs(values):
    values = values + core_swap(values)
    values = values + y_swap(values)
    return values + x_swap(values)


def local(
    block_in,
    segments,
    out_grad,
    ln1_gain,
    ln1_bias,
    w_qkv,
    b_qv,
    w_attn_out,
    b_attn_out,
    ln2_gain,
    ln2_bias,
    w_up,
    b_up,
    w_down,
    b_down,
):
    seqs, span, width = block_in.shape
    n = lax.axis_size("tp")
    cx = lax.axis_index("ctx")
    blocks = lax.axis_size("ctx")
    z = lax.axis_index("tp")
    part = span // n
    local_width = w_qkv.shape[2]
    each = range(seqs)

    place = jnp.stack(
        [cx & 1, lax.axis_index("fsdp"), z, cx] + [(cx ^ b) <= cx for b in range(blocks)]
    ).astype(jnp.int32)
    order = Order(place)

    w3 = jnp.transpose(w_qkv, (1, 0, 2))
    wo, wu, wd = w_attn_out[None], w_up[None], w_down[None]

    def vector(values):
        return values.astype(F32)[None]

    gain_one = to_relative(vector(ln1_gain))
    gain_two = to_relative(vector(ln2_gain))
    shift_two = to_relative(vector(ln2_bias))
    bias_out = to_relative(vector(b_attn_out))
    bias_down = to_relative(vector(b_down))
    bias_kv = jnp.stack([jnp.zeros_like(b_qv[1:]), b_qv[1:]])
    bias_q = b_qv[None, :1]

    block = seqs * part
    kv_c = x_swap(take_half(order, w3, 1, 2, 0))
    n1, own_x = norm_in(order, block_in, vector(ln1_gain), vector(ln1_bias), n)
    n1_split = by_sequence(n1, n, seqs)
    kv_c = order.tie(kv_c)
    kv_n = core_swap(kv_c)
    q_c = x_swap(take_half(order, w3, 0, 1, 0))

    spot = mix_rows(jnp.arange(span, dtype=jnp.int32))
    marks, valid = [], []
    for s in each:
        valid.append((piece(segments[s], cx * span, span, 0) != 0).astype(F32)[:, None])
        key_seg = jnp.stack(
            [mix_rows(piece(segments[s], (cx ^ b) * span, span, 0)) for b in range(blocks)]
        )
        marks.append((key_seg[:, :, None], key_seg[0][None, :], spot[:, None], spot[None, :]))

    kvs = [
        project(order, (n1_split, s), w3, 1, kv_c, kv_n, bias_kv, "project_kv") for s in each
    ]
    kv_y = [y_swap(kvs[0])]
    o_c = x_swap(take_half(order, wo, 0, 1, 1))
    cot = cot_in(order, out_grad, jnp.stack(valid), n)
    q_c = order.tie(q_c)
    q_n = core_swap(q_c)
    d_c = x_swap(take_half(order, wd, 0, 1, 1))
    queries = by_sequence(
        project(order, n1, w3, 0, q_c, q_n, bias_q, "project_q")[0], n, seqs
    )
    o_c = order.tie(o_c)
    o_n = core_swap(o_c)
    kv_all, log_total = [], []
    attended = None
    for s in each:
        kv2 = order.tie(kv_y[s])
        kv_all.append((kvs[s], core_swap(kvs[s]), kv2, core_swap(kv2)))
        if s + 1 < seqs:
            kvs[s + 1] = order.tie(kvs[s + 1])
            kv_y.append(y_swap(kvs[s + 1]))
        attended, total = attend(order, queries, s, kv_all[s], marks[s], attended)
        log_total.append(total)
    flat_attended = attended.reshape(seqs * span, local_width)

    pieces, steps = col_pieces(wo, o_c, o_n, 256)
    parts = to_features(
        order, flat_attended, pieces, steps, 256, False, n, width, "attn_out"
    )
    got = sum_first(parts)
    d_c = order.tie(d_c)
    d_n = core_swap(d_c)
    u_c = x_swap(take_half(order, wu, 0, 1, 0))
    grad_active = active_grad(order, cot, wd, d_c, d_n)
    parts = sum_second(order, parts, got, n, block)
    middle, own = norm_mid(order, parts, own_x, bias_out, gain_two, shift_two)
    n2 = Gather(order, own)
    n2.pass_on()
    u_c = order.tie(u_c)
    u_n = core_swap(u_c)

    n2 = n2.blocks()
    up_sums, active, grad_hidden = feed(
        order, n2, wu, u_c, u_n, vector(b_up), grad_active
    )
    pieces, steps = row_pieces(wu, u_c, u_n, 256)
    parts = to_features(order, grad_hidden, pieces, steps, 256, True, n, width, "grad_n2")
    got = sum_first(parts)
    pieces, steps = col_pieces(wd, d_c, d_n, 256)
    (out_part,) = to_features(
        order, active, pieces, steps, 256, False, n, width, "feed_out", seqs
    )
    parts = sum_second(order, parts, got, n, block)
    w_down_sum = WeightSum(
        order, *weight_grad_cols(order, [active], [[(cot, 0)]], "grad_w_down")
    )
    stats_two, grad_mid, own = back_mid(order, parts, middle, cot, gain_two)
    gm = Gather(order, own)
    w_up_sum = WeightSum(order, *weight_grad_rows(order, [n2], [grad_hidden], "grad_w_up"))
    gm.pass_on()
    out_part = order.tie(out_part)
    out_sum = lax.psum_scatter(out_part, "tp", scatter_dimension=1, tiled=True)

    gm = gm.blocks()
    grad_att = by_sequence(heads_grad(order, gm, seqs * span, wo, o_c, o_n), n, seqs)
    near, got, bases, fars = [], [], [], []
    g_q = None

    def pair_back(s):
        base, far = add_pair(order, near[s], got[s])
        bases.append(base)
        fars.append(y_swap(far))

    for s in each:
        g_q, close, away = attend_back(
            order, queries, s, kv_all[s], marks[s], attended, grad_att, log_total[s], g_q
        )
        near.append(close)
        got.append(core_swap(away))
        if s == 0:
            w_down_sum.to_x()
        if s + 1 < seqs:
            pair_back(s)
    w_out_sum = WeightSum(order, *weight_grad_cols(order, [flat_attended], [gm], "grad_w_attn"))
    w_up_sum.to_x()
    pair_back(seqs - 1)
    g_q = g_q.reshape(seqs * span, local_width)
    g_kv, *parts = back_project(
        order, g_q, bases, fars, w3, q_c, q_n, kv_c, kv_n, n, width
    )
    got = sum_first(parts)
    w_qkv_sum = WeightSum(
        order, *weight_grad_rows(order, [[(n1, 0)]], [g_q], "grad_w_qkv", [g_kv])
    )
    w_down_sum.to_y()
    parts = sum_second(order, parts, got, n, block)
    w_up_sum.to_y()
    w_qkv_sum.to_x()
    w_down_sum.to_core()
    stats_one, own = back_in(order, parts, own_x, grad_mid, gain_one)
    in_rows = Gather(order, own)

    def over_rows(values):
        return jnp.sum(values.astype(F32), axis=0)

    tall = to_natural(jnp.concatenate([stats_two[:4], stats_one[:2]])).reshape(-1)
    narrow = jnp.concatenate([over_rows(g_q), over_rows(g_kv[1]), up_sums[0]])
    packed = jnp.concatenate([tall, narrow])
    w_qkv_sum.to_y()
    w_up_sum.to_core()
    in_rows.pass_on()
    out_own = out_rows(order, middle, out_sum, bias_down)
    block_out = lax.all_gather(out_own, "tp", axis=1, tiled=True)
    g_down = w_down_sum.finish(1)[0]
    w_out_sum.to_x()
    packed = packed + order.tie(core_swap(packed))
    g_up = w_up_sum.finish(0)[0]
    w_qkv_sum.to_core()
    w_out_sum.to_y()
    packed = packed + order.tie(x_swap(packed))
    g_qkv = jnp.transpose(w_qkv_sum.finish(0), (1, 0, 2))
    packed = packed + order.tie(y_swap(packed))
    w_out_sum.to_core()
    in_grad = assemble(order, in_rows.blocks(), seqs, block)
    g_out = w_out_sum.finish(1)[0]
    tall = packed[: 6 * width]
    bit = 1
    while bit < n:
        tall = tall + tp_swap(tall, bit)
        bit *= 2
    early = tall.reshape(6, width)
    late = early[4:]
    narrow = packed[6 * width :]
    g_bqv = narrow[: 2 * local_width].reshape(2, local_width)
    g_bup = narrow[2 * local_width :]
    return (
        block_out,
        in_grad,
        late[0],
        late[1],
        g_qkv,
        g_bqv,
        g_out,
        early[0],
        early[1],
        early[2],
        g_up,
        g_bup,
        g_down,
        early[3],
    )


def solution(mesh):
    in_specs = (
        P("fsdp", "ctx", None),
        P("fsdp", None),
        P("fsdp", "ctx", None),
        P(),
        P(),
        P("fsdp", None, "tp"),
        P(None, "tp"),
        P("tp", "fsdp"),
        P(),
        P(),
        P(),
        P("fsdp", "tp"),
        P("tp"),
        P("tp", "fsdp"),
        P(),
    )
    out_specs = (
        P("fsdp", "ctx", None),
        P("fsdp", "ctx", None),
        P(),
        P(),
        P("fsdp", None, "tp"),
        P(None, "tp"),
        P("tp", "fsdp"),
        P(),
        P(),
        P(),
        P("fsdp", "tp"),
        P("tp"),
        P("tp", "fsdp"),
        P(),
    )
    return jax.shard_map(local, mesh=mesh, in_specs=in_specs, out_specs=out_specs, check_vma=False)
```

time: 1270 us -> 873 us (0.69)
  Pallas kernels: 0 us -> 278 us
  matrix products: 251 us -> 0 us
  other arithmetic: 208 us -> 4.94 us
  starting transfers between devices: 231 us -> 70.9 us
  waiting for transfers between devices: 472 us -> 402 us
    pallas_call x0 -> x66, Pallas kernels: none -> 278 us  [the longest x51 267 us: call(): pl.pallas_call(kernel, grid_spec=pltpu.PrefetchScalarGridSpec(num_scalar_...]
    dot_general x42 -> x0, matrix products: 251 us -> none  [the longest x12 66.7 us: dot_t(): lax.dot_general(a, b, (((1,), (1,)), ((), ())), preferred_element_type=F32)]
    ppermute x98 -> x20, starting transfers between devices: 192 us -> 18.1 us  [tp_swap(): return lax.ppermute(values, 'tp', xor_pairs(lax.axis_size('tp'), bit))]
    convert_element_type x41 -> x2, other arithmetic: 75.2 us -> 0.02 us  [the longest x1 0.02 us: local(): (piece(segments[s], cx * span, span, 0) != 0).astype(F32)[:, None]]
    ppermute x12 -> x9, waiting for transfers between devices: 132 us -> 61 us  [y_swap(): return lax.ppermute(values, 'ctx', xor_pairs(lax.axis_size('ctx'), 2))]
    unnamed x459 -> x295, local copies, waits for them, and re-layouts: 18 us -> 87.7 us
    concatenate x21 -> x11, other arithmetic: 32.2 us -> 0.2 us  [the longest x1 0.1 us: local(): jnp.concatenate([stats_two[:4], stats_one[:2]])]
    reduce_sum x20 -> x2, other arithmetic: 32.8 us -> 2.87 us  [over_rows(): return jnp.sum(values.astype(F32), axis=0)]
  transfers between devices with their start and end apart: 150 -> 61, of which waited for: 55 -> 32; matrix products, arithmetic and copies ran while one was open for 40% -> 1% of each run, Pallas kernels for 0% -> 27%
where the time goes in v3:
time: 873 us; the launch traced here: 864 us
  waiting for transfers between devices  402 us (46%)
  Pallas kernels  278 us (32%)
  local copies, waits for them, and re-layouts  92.7 us (11%)
  starting transfers between devices  70.9 us (8%)
  between operations  16.1 us (2%)
    ppermute x20, waiting for transfers between devices, tp_swap(): return lax.ppermute(values, 'tp', xor_pairs(lax.axis_size('tp'), bit))  279 us
    pallas_call x51, Pallas kernels, call(): pl.pallas_call(kernel, grid_spec=pltpu.PrefetchScalarGridSpec(num_scalar_...  267 us
    unnamed x295, local copies, waits for them, and re-layouts  87.7 us
    ppermute x9, waiting for transfers between devices, y_swap(): return lax.ppermute(values, 'ctx', xor_pairs(lax.axis_size('ctx'), 2))  61 us
    ppermute x10, waiting for transfers between devices, x_swap(): return lax.ppermute(values, 'fsdp', X_SWAP)  58.7 us
    ppermute x9, starting transfers between devices, y_swap(): return lax.ppermute(values, 'ctx', xor_pairs(lax.axis_size('ctx'), 2))  28 us
    ppermute x20, starting transfers between devices, tp_swap(): return lax.ppermute(values, 'tp', xor_pairs(lax.axis_size('tp'), bit))  18.1 us
  transfers between devices with their start and end apart: 61, of which 32 were waited for; matrix products, arithmetic and copies ran while one was open for 1% of the time, Pallas kernels for 27%

profile of v3, /device:TPU:0, one launch (start us, length us, event | category | flops | bytes accessed | tf_op | source)
XLA Modules:
  0.0 864.1 jit_solution(16274172535172805459)
XLA Ops:
  12.9 6.1 norm_in.1
  22.1 14.1 %collective-permute-done.refs_0_ = bf16[2,512,512]{2,1,0:T(8,128)(2,1)} collective-permute-done((bf16[2,512,512]{2,1,0:T(8,128)(2,1)S(1)}, bf16[2,512,512]{2,1,0:T(8,128)(2,1)}, u32[]{:S(2)}, u32[]{:S(2)}) %collective-permute-start) | collective-permute-done | bytes 1048608 | tf_op jit(solution)/shard_map/ppermute | solution.py:33
  39.9 5.8 project_kv.2.refs_7_.refs_2_
  47.6 5.3 project_kv.3.refs_2_.refs_0_
  63.6 5.5 project_q.1.refs_1_
  80.2 5.3 attend.2
  88.1 13.3 %collective-permute-done.7.refs_0_ = bf16[2,512,512]{2,1,0:T(8,128)(2,1)S(1)} collective-permute-done((bf16[2,512,512]{2,1,0:T(8,128)(2,1)}, bf16[2,512,512]{2,1,0:T(8,128)(2,1)S(1)}, u32[]{:S(2)}, u32[]{:S(2)}) %collective-permute-start.7) | collective-permute-done | bytes 1048608 | tf_op jit(solution)/shard_map/ppermute | solution.py:29
  119.1 5.3 attn_out.1
  136.3 14.8 %active_grad.1.refs_3_.refs_10_ = f32[1024,2048]{1,0:T(8,128)} custom-call(s32[8]{0:T(128)S(1)} %copy-done.83, bf16[1024,2048]{1,0:T(8,128)(2,1)} %copy-done.4, bf16[1,2048,1024]{2,1,0:T(8,128)(2,1)} %bitcast.172, bf16[1,2048,512]{2,1,0:T(8,128)(2,1)} %tie.21.refs_2_.refs_3_, bf16[1,2048,1024]{2,1,0:T(8,128)(2,1)} %bitcast.173, ...), custom_call_target="tpu_custom_call" | custom-call | flops 8589934592 | bytes 16777232 | tf_op jit(solution)/shard_map/active_grad/pallas_call | solution.py:116
  151.1 4.9 collective-permute-done.12.refs_2_
  162.1 35.5 %collective-permute-done.16.refs_3_ = bf16[256,2048]{1,0:T(8,128)(2,1)} collective-permute-done((bf16[256,2048]{1,0:T(8,128)(2,1)}, bf16[256,2048]{1,0:T(8,128)(2,1)}, u32[]{:S(2)}, u32[]{:S(2)}) %collective-permute-start.16) | collective-permute-done | bytes 1048608 | tf_op jit(solution)/shard_map/ppermute | solution.py:37
  197.5 8.0 collective-permute-done.15.refs_2_
  216.1 42.5 %collective-permute-done.17.refs_0_ = bf16[256,2048]{1,0:T(8,128)(2,1)S(1)} collective-permute-done((bf16[256,2048]{1,0:T(8,128)(2,1)S(1)}, bf16[256,2048]{1,0:T(8,128)(2,1)S(1)}, u32[]{:S(2)}, u32[]{:S(2)}) %collective-permute-start.17) | collective-permute-done | bytes 1048608 | tf_op jit(solution)/shard_map/ppermute | solution.py:37
  261.5 25.2 %collective-permute-done.19.refs_4_ = bf16[256,2048]{1,0:T(8,128)(2,1)S(1)} collective-permute-done((bf16[256,2048]{1,0:T(8,128)(2,1)S(1)}, bf16[256,2048]{1,0:T(8,128)(2,1)S(1)}, u32[]{:S(2)}, u32[]{:S(2)}) %collective-permute-start.19) | collective-permute-done | bytes 1048608 | tf_op jit(solution)/shard_map/ppermute | solution.py:37
  289.6 18.7 %feed.1 = (f32[1,2048]{1,0:T(1,128)S(1)}, bf16[1024,2048]{1,0:T(8,128)(2,1)}, bf16[1024,2048]{1,0:T(8,128)(2,1)}) custom-call(s32[8]{0:T(128)S(1)} %copy-done.84, bf16[256,2048]{1,0:T(8,128)(2,1)S(1)} %copy-done.97, bf16[256,2048]{1,0:T(8,128)(2,1)} %get-tuple-element.75.refs_2_, bf16[256,2048]{1,0:T(8,128)(2,1)S(1)} %copy-done.55, ...), custom_call_target="tpu_custom_call" | custom-call | flops 8589934592 | bytes 25174048 | tf_op jit(solution)/shard_map/feed/pallas_call | solution.py:116
  308.3 14.3 %grad_n2.1 = (bf16[512,2048]{1,0:T(8,128)(2,1)S(1)}, bf16[256,2048]{1,0:T(8,128)(2,1)}, bf16[256,2048]{1,0:T(8,128)(2,1)S(1)}) custom-call(s32[8]{0:T(128)S(1)} %copy-done.84, bf16[1024,2048]{1,0:T(8,128)(2,1)} %get-tuple-element.78.refs_1_.refs_6_.refs_5_, bf16[1,1024,2048]{2,1,0:T(8,128)(2,1)} %bitcast.169, ...), custom_call_target="tpu_custom_call" | custom-call | flops 8589934592 | bytes 16777240 | tf_op jit(solution)/shard_map/grad_n2/pallas_call | solution.py:116
  324.6 13.1 %feed_out.1.refs_3_.refs_0_ = bf16[2,512,2048]{2,1,0:T(8,128)(2,1)S(1)} custom-call(s32[8]{0:T(128)S(1)} %copy-done.84, bf16[1024,2048]{1,0:T(8,128)(2,1)} %get-tuple-element.77.refs_1_, bf16[1,2048,1024]{2,1,0:T(8,128)(2,1)} %bitcast.174, bf16[1,2048,512]{2,1,0:T(8,128)(2,1)} %tie.21.refs_2_.refs_3_, bf16[1,2048,1024]{2,1,0:T(8,128)(2,1)} %bitcast.175, ...), custom_call_target="tpu_custom_call" | custom-call | flops 8589934592 | bytes 16777228 | tf_op jit(solution)/shard_map/feed_out/pallas_call | solution.py:116
  337.8 10.9 %collective-permute-done.22.refs_2_ = bf16[256,2048]{1,0:T(8,128)(2,1)S(1)} collective-permute-done((bf16[256,2048]{1,0:T(8,128)(2,1)S(1)}, bf16[256,2048]{1,0:T(8,128)(2,1)S(1)}, u32[]{:S(2)}, u32[]{:S(2)}) %collective-permute-start.22) | collective-permute-done | bytes 1048608 | tf_op jit(solution)/shard_map/ppermute | solution.py:37
  350.2 14.4 %grad_w_down.1 = (bf16[2,1,2048,512]{3,2,1,0:T(8,128)(2,1)S(1)}, bf16[2,1,2048,512]{3,2,1,0:T(8,128)(2,1)S(1)}) custom-call(s32[8]{0:T(128)S(1)} %copy-done.84, bf16[1024,2048]{1,0:T(8,128)(2,1)} %get-tuple-element.77.refs_1_, bf16[1024,2048]{1,0:T(8,128)(2,1)} %copy-done.4, bf16[256,2048]{1,0:T(8,128)(2,1)S(1)} %add_rows.4.refs_3_), custom_call_target="tpu_custom_call" | custom-call | flops 8589934592 | bytes 8388640 | tf_op jit(solution)/shard_map/grad_w_down/pallas_call | solution.py:116
  366.6 22.7 %collective-permute-done.24.refs_3_ = bf16[256,2048]{1,0:T(8,128)(2,1)S(1)} collective-permute-done((bf16[256,2048]{1,0:T(8,128)(2,1)}, bf16[256,2048]{1,0:T(8,128)(2,1)S(1)}, u32[]{:S(2)}, u32[]{:S(2)}) %collective-permute-start.24) | collective-permute-done | bytes 1048608 | tf_op jit(solution)/shard_map/ppermute | solution.py:37
  389.2 5.6 collective-permute-done.23.refs_2_
  394.9 5.0 back_mid.1
  403.5 14.6 %grad_w_up.1 = (bf16[2,1,512,2048]{3,2,1,0:T(8,128)(2,1)S(1)}, bf16[2,1,512,2048]{3,2,1,0:T(8,128)(2,1)}) custom-call(s32[8]{0:T(128)S(1)} %copy-done.84, bf16[256,2048]{1,0:T(8,128)(2,1)S(1)} %copy-done.98, bf16[256,2048]{1,0:T(8,128)(2,1)} %get-tuple-element.75.refs_2_, bf16[256,2048]{1,0:T(8,128)(2,1)S(1)} %copy-done.56, ...), custom_call_target="tpu_custom_call" | custom-call | flops 8589934592 | bytes 8388640 | tf_op jit(solution)/shard_map/grad_w_up/pallas_call | solution.py:116
  420.2 24.4 %collective-permute-done.25.refs_0_ = bf16[256,2048]{1,0:T(8,128)(2,1)S(1)} collective-permute-done((bf16[256,2048]{1,0:T(8,128)(2,1)S(1)}, bf16[256,2048]{1,0:T(8,128)(2,1)S(1)}, u32[]{:S(2)}, u32[]{:S(2)}) %collective-permute-start.25) | collective-permute-done | bytes 1048608 | tf_op jit(solution)/shard_map/ppermute | solution.py:37
  447.8 23.0 %collective-permute-done.27.refs_4_.refs_5_ = bf16[256,2048]{1,0:T(8,128)(2,1)} collective-permute-done((bf16[256,2048]{1,0:T(8,128)(2,1)}, bf16[256,2048]{1,0:T(8,128)(2,1)}, u32[]{:S(2)}, u32[]{:S(2)}) %collective-permute-start.27) | collective-permute-done | bytes 1048608 | tf_op jit(solution)/shard_map/ppermute | solution.py:37
  472.0 5.0 heads_grad.1.refs_13_
  477.1 7.9 attend_back.2
  495.8 7.1 attend_back.3
  506.3 17.2 %collective-permute-start.32 = (bf16[2,512,512]{2,1,0:T(8,128)(2,1)}, bf16[2,512,512]{2,1,0:T(8,128)(2,1)S(1)}, u32[]{:S(2)}, u32[]{:S(2)}) collective-permute-start(bf16[2,512,512]{2,1,0:T(8,128)(2,1)} %copy-done.134), channel_id=1, source_target_pairs={{0,8},{4,12},{8,0},{12,4},{1,9},{5,13},{9,1},{13,5},{2,10},{6,14},... | collective-permute-start | bytes 3145736 | tf_op jit(solution)/shard_map/ppermute | solution.py:29
  526.9 5.4 grad_w_attn.1
  532.3 4.8 sum_core.5.refs_3_
  542.6 5.0 collective-permute-done.32.refs_4_
  548.6 21.5 %collective-permute-done.33.refs_5_ = bf16[2,512,512]{2,1,0:T(8,128)(2,1)S(1)} collective-permute-done((bf16[2,512,512]{2,1,0:T(8,128)(2,1)S(1)}, bf16[2,512,512]{2,1,0:T(8,128)(2,1)S(1)}, u32[]{:S(2)}, u32[]{:S(2)}) %collective-permute-start.33) | collective-permute-done | bytes 1048608 | tf_op jit(solution)/shard_map/ppermute | solution.py:29
  571.3 13.4 %back_project.1 = (bf16[2,1024,512]{2,1,0:T(8,128)(2,1)}, bf16[512,2048]{1,0:T(8,128)(2,1)}, bf16[256,2048]{1,0:T(8,128)(2,1)S(1)}, bf16[256,2048]{1,0:T(8,128)(2,1)}) custom-call(s32[8]{0:T(128)S(1)} %copy-done.85, bf16[1024,512]{1,0:T(8,128)(2,1)S(1)} %bitcast.180, f32[2,512,512]{2,1,0:T(8,128)} %copy-done.128, f32[2,512,512]{2,1,0:T(8,128)} %copy-done.130, ...), custom_call_target="tpu_custom_call" | custom-call | flops 6442450944 | bytes 16777252 | tf_op jit(solution)/shard_map/back_project/pallas_call | solution.py:116
  587.3 12.4 %grad_w_qkv.1 = (bf16[2,3,512,512]{3,2,1,0:T(8,128)(2,1)S(1)}, bf16[2,3,512,512]{3,2,1,0:T(8,128)(2,1)}) custom-call(s32[8]{0:T(128)S(1)} %copy-done.85, bf16[1024,2048]{1,0:T(8,128)(2,1)} %copy-done.3, bf16[1024,512]{1,0:T(8,128)(2,1)S(1)} %bitcast.181, bf16[2,1024,512]{2,1,0:T(8,128)(2,1)S(1)} %copy-done.123, bf16[256,2048]{1,0:T(8,128)(2,1)} %get-tuple-element.101.refs_4_), custom_call_target="tpu_custom_call" | custom-call | flops 6442450944 | bytes 7340064 | tf_op jit(solution)/shard_map/grad_w_qkv/pallas_call | solution.py:116
  613.5 14.0 %collective-permute-done.34.refs_2_ = bf16[256,2048]{1,0:T(8,128)(2,1)} collective-permute-done((bf16[256,2048]{1,0:T(8,128)(2,1)}, bf16[256,2048]{1,0:T(8,128)(2,1)}, u32[]{:S(2)}, u32[]{:S(2)}) %collective-permute-start.34) | collective-permute-done | bytes 1048608 | tf_op jit(solution)/shard_map/ppermute | solution.py:37
  630.5 17.6 %collective-permute-done.40 = bf16[1,512,2048]{2,1,0:T(8,128)(2,1)} collective-permute-done((bf16[1,512,2048]{2,1,0:T(8,128)(2,1)}, bf16[1,512,2048]{2,1,0:T(8,128)(2,1)}, u32[]{:S(2)}, u32[]{:S(2)}) %collective-permute-start.40) | collective-permute-done | bytes 2097184 | tf_op jit(solution)/shard_map/ppermute | solution.py:33
  662.8 14.5 %collective-permute-done.36.refs_2_ = bf16[256,2048]{1,0:T(8,128)(2,1)} collective-permute-done((bf16[256,2048]{1,0:T(8,128)(2,1)}, bf16[256,2048]{1,0:T(8,128)(2,1)}, u32[]{:S(2)}, u32[]{:S(2)}) %collective-permute-start.36) | collective-permute-done | bytes 1048608 | tf_op jit(solution)/shard_map/ppermute | solution.py:37
  684.1 6.9 collective-permute-done.44
  694.7 7.8 collective-permute-done.43
  706.5 21.1 %collective-permute-done.41.refs_0_ = bf16[256,2048]{1,0:T(8,128)(2,1)S(1)} collective-permute-done((bf16[256,2048]{1,0:T(8,128)(2,1)S(1)}, bf16[256,2048]{1,0:T(8,128)(2,1)S(1)}, u32[]{:S(2)}, u32[]{:S(2)}) %collective-permute-start.41) | collective-permute-done | bytes 1048608 | tf_op jit(solution)/shard_map/ppermute | solution.py:37
  744.9 8.0 finish.4.refs_3_
  756.9 6.0 finish.5.refs_3_
  762.9 11.5 %collective-permute-done.49 = bf16[3,512,512]{2,1,0:T(8,128)(2,1)} collective-permute-done((bf16[3,512,512]{2,1,0:T(8,128)(2,1)}, bf16[3,512,512]{2,1,0:T(8,128)(2,1)}, u32[]{:S(2)}, u32[]{:S(2)}) %collective-permute-start.49) | collective-permute-done | bytes 1572896 | tf_op jit(solution)/shard_map/ppermute | solution.py:29
  778.7 13.4 %collective-permute-done.48 = bf16[1,512,512]{2,1,0:T(8,128)(2,1)S(1)} collective-permute-done((bf16[1,512,512]{2,1,0:T(8,128)(2,1)S(1)}, bf16[1,512,512]{2,1,0:T(8,128)(2,1)S(1)}, u32[]{:S(2)}, u32[]{:S(2)}) %collective-permute-start.48) | collective-permute-done | bytes 524320 | tf_op jit(solution)/shard_map/ppermute | solution.py:33
  802.2 6.4 finish.6.refs_1_
  813.5 25.5 %collective-permute-done.56 = f32[12288]{0:T(1024)S(1)} collective-permute-done((f32[12288]{0:T(1024)S(1)}, f32[12288]{0:T(1024)S(1)}, u32[]{:S(2)}, u32[]{:S(2)}) %collective-permute-start.56) | collective-permute-done | bytes 49184 | tf_op jit(solution)/shard_map/ppermute | solution.py:37
  852.0 4.8 copy.105
  (497 shorter events, 232.4 us)
Async XLA Ops:
  7.2 723.0 %reduce-scatter.2.cloned.1.call-start = ((), (), s32[]{:S(2)}) async-start(), calls=%async_computation.1 | async-start | bytes 5242880 | tf_op jit(solution)/shard_map/reduce_scatter | solution.py:1236
  9.9 26.3 %collective-permute-start = (bf16[2,512,512]{2,1,0:T(8,128)(2,1)S(1)}, bf16[2,512,512]{2,1,0:T(8,128)(2,1)}, u32[]{:S(2)}, u32[]{:S(2)}) collective-permute-start(bf16[2,512,512]{2,1,0:T(8,128)(2,1)S(1)} %take_half.5.refs_4_), channel_id=1, source_target_pairs={{0,16},{16,0},{1,17},{17,1},{2,18},{18,2},{3,19},{19,3},{4,20},{20... | collective-permute-start | bytes 3145736 | tf_op jit(solution)/shard_map/ppermute | solution.py:33
  38.0 19.8 %collective-permute-start.1 = (bf16[1,512,512]{2,1,0:T(8,128)(2,1)S(1)}, bf16[1,512,512]{2,1,0:T(8,128)(2,1)}, u32[]{:S(2)}, u32[]{:S(2)}) collective-permute-start(bf16[1,512,512]{2,1,0:T(8,128)(2,1)S(1)} %take_half.6.refs_7_), channel_id=1, source_target_pairs={{0,16},{16,0},{1,17},{17,1},{2,18},{18,2},{3,19},{19,3},{4,20},{20... | collective-permute-start | bytes 1572872 | tf_op jit(solution)/shard_map/ppermute | solution.py:33
  45.7 28.3 %collective-permute-start.4 = (bf16[2,512,512]{2,1,0:T(8,128)(2,1)}, bf16[2,512,512]{2,1,0:T(8,128)(2,1)}, u32[]{:S(2)}, u32[]{:S(2)}) collective-permute-start(bf16[2,512,512]{2,1,0:T(8,128)(2,1)} %project_kv.2.refs_7_.refs_2_), channel_id=1, source_target_pairs={{0,8},{4,12},{8,0},{12,4},{1,9},{5,13},{9,1},{13,5},{2,10},{6,14},... | collective-permute-start | bytes 3145736 | tf_op jit(solution)/shard_map/ppermute | solution.py:29
  58.7 14.7 %collective-permute-start.5 = (bf16[1,512,512]{2,1,0:T(8,128)(2,1)}, bf16[1,512,512]{2,1,0:T(8,128)(2,1)}, u32[]{:S(2)}, u32[]{:S(2)}) collective-permute-start(bf16[1,512,512]{2,1,0:T(8,128)(2,1)} %copy-done.75), channel_id=1, source_target_pairs={{0,16},{16,0},{1,17},{17,1},{2,18},{18,2},{3,19},{19,3},{4,20},{20... | collective-permute-start | bytes 1572872 | tf_op jit(solution)/shard_map/ppermute | solution.py:33
  60.3 18.7 %collective-permute-start.8 = (bf16[2,512,512]{2,1,0:T(8,128)(2,1)}, bf16[2,512,512]{2,1,0:T(8,128)(2,1)}, u32[]{:S(2)}, u32[]{:S(2)}) collective-permute-start(bf16[2,512,512]{2,1,0:T(8,128)(2,1)} %project_kv.2.refs_7_.refs_2_), channel_id=1, source_target_pairs={{0,4},{4,0},{8,12},{12,8},{1,5},{5,1},{9,13},{13,9},{2,6},{6,2},{1... | collective-permute-start | bytes 3145736 | tf_op jit(solution)/shard_map/ppermute | solution.py:25
  75.6 25.7 %collective-permute-start.7 = (bf16[2,512,512]{2,1,0:T(8,128)(2,1)}, bf16[2,512,512]{2,1,0:T(8,128)(2,1)S(1)}, u32[]{:S(2)}, u32[]{:S(2)}) collective-permute-start(bf16[2,512,512]{2,1,0:T(8,128)(2,1)} %tie.19.refs_10_.refs_2_), channel_id=1, source_target_pairs={{0,8},{4,12},{8,0},{12,4},{1,9},{5,13},{9,1},{13,5},{2,10},{6,14},... | collective-permute-start | bytes 3145736 | tf_op jit(solution)/shard_map/ppermute | solution.py:29
  76.2 50.5 %collective-permute-start.13 = (bf16[1,2048,512]{2,1,0:T(8,128)(2,1)}, bf16[1,2048,512]{2,1,0:T(8,128)(2,1)}, u32[]{:S(2)}, u32[]{:S(2)}) collective-permute-start(bf16[1,2048,512]{2,1,0:T(8,128)(2,1)} %copy-done.38), channel_id=1, source_target_pairs={{0,16},{16,0},{1,17},{17,1},{2,18},{18,2},{3,19},{19,3},{4,20},{20... | collective-permute-start | bytes 6291464 | tf_op jit(solution)/shard_map/ppermute | solution.py:33
  78.9 26.2 %collective-permute-start.6 = (bf16[2,512,512]{2,1,0:T(8,128)(2,1)}, bf16[2,512,512]{2,1,0:T(8,128)(2,1)}, u32[]{:S(2)}, u32[]{:S(2)}) collective-permute-start(bf16[2,512,512]{2,1,0:T(8,128)(2,1)} %tie.19.refs_10_.refs_2_), channel_id=1, source_target_pairs={{0,4},{4,0},{8,12},{12,8},{1,5},{5,1},{9,13},{13,9},{2,6},{6,2},{1... | collective-permute-start | bytes 3145736 | tf_op jit(solution)/shard_map/ppermute | solution.py:25
  103.1 14.8 %collective-permute-start.11 = (bf16[1,512,512]{2,1,0:T(8,128)(2,1)}, bf16[1,512,512]{2,1,0:T(8,128)(2,1)}, u32[]{:S(2)}, u32[]{:S(2)}) collective-permute-start(bf16[1,512,512]{2,1,0:T(8,128)(2,1)} %tie.17.refs_1_.refs_3_.refs_6_), channel_id=1, source_target_pairs={{0,4},{4,0},{8,12},{12,8},{1,5},{5,1},{9,13},{13,9},{2,6},{6,2},{1... | collective-permute-start | bytes 1572872 | tf_op jit(solution)/shard_map/ppermute | solution.py:25
  130.0 26.0 %collective-permute-start.12 = (bf16[256,2048]{1,0:T(8,128)(2,1)S(1)}, bf16[256,2048]{1,0:T(8,128)(2,1)S(1)}, u32[]{:S(2)}, u32[]{:S(2)}) collective-permute-start(bf16[256,2048]{1,0:T(8,128)(2,1)S(1)} %copy-done.103), channel_id=1, source_target_pairs={{0,1},{1,0},{2,3},{3,2},{4,5},{5,4},{6,7},{7,6},{8,9},{9,8},{10,11... | collective-permute-start | bytes 3145736 | tf_op jit(solution)/shard_map/ppermute | solution.py:37
  135.8 61.8 %collective-permute-start.16 = (bf16[256,2048]{1,0:T(8,128)(2,1)}, bf16[256,2048]{1,0:T(8,128)(2,1)}, u32[]{:S(2)}, u32[]{:S(2)}) collective-permute-start(bf16[256,2048]{1,0:T(8,128)(2,1)} %get-tuple-element.72), channel_id=1, source_target_pairs={{0,1},{1,0},{2,3},{3,2},{4,5},{5,4},{6,7},{7,6},{8,9},{9,8},{10,11... | collective-permute-start | bytes 3145736 | tf_op jit(solution)/shard_map/ppermute | solution.py:37
  157.8 47.8 %collective-permute-start.15 = (bf16[256,2048]{1,0:T(8,128)(2,1)}, bf16[256,2048]{1,0:T(8,128)(2,1)}, u32[]{:S(2)}, u32[]{:S(2)}) collective-permute-start(bf16[256,2048]{1,0:T(8,128)(2,1)} %add_rows.3.refs_8_), channel_id=1, source_target_pairs={{0,2},{1,3},{2,0},{3,1},{4,6},{5,7},{6,4},{7,5},{8,10},{9,11},{10,... | collective-permute-start | bytes 3145736 | tf_op jit(solution)/shard_map/ppermute | solution.py:37
  160.4 99.9 %collective-permute-start.20 = (bf16[1,512,2048]{2,1,0:T(8,128)(2,1)}, bf16[1,512,2048]{2,1,0:T(8,128)(2,1)}, u32[]{:S(2)}, u32[]{:S(2)}) collective-permute-start(bf16[1,512,2048]{2,1,0:T(8,128)(2,1)} %take_half.9.refs_6_), channel_id=1, source_target_pairs={{0,16},{16,0},{1,17},{17,1},{2,18},{18,2},{3,19},{19,3},{4,20},{20... | collective-permute-start | bytes 6291464 | tf_op jit(solution)/shard_map/ppermute | solution.py:33
  211.9 46.7 %collective-permute-start.17 = (bf16[256,2048]{1,0:T(8,128)(2,1)S(1)}, bf16[256,2048]{1,0:T(8,128)(2,1)S(1)}, u32[]{:S(2)}, u32[]{:S(2)}) collective-permute-start(bf16[256,2048]{1,0:T(8,128)(2,1)S(1)} %get-tuple-element.74.refs_2_.refs_1_), channel_id=1, source_target_pairs={{0,2},{1,3},{2,0},{3,1},{4,6},{5,7},{6,4},{7,5},{8,10},{9,11},{10,... | collective-permute-start | bytes 3145736 | tf_op jit(solution)/shard_map/ppermute | solution.py:37
  212.0 46.8 %collective-permute-start.18 = (bf16[256,2048]{1,0:T(8,128)(2,1)S(1)}, bf16[256,2048]{1,0:T(8,128)(2,1)}, u32[]{:S(2)}, u32[]{:S(2)}) collective-permute-start(bf16[256,2048]{1,0:T(8,128)(2,1)S(1)} %get-tuple-element.74.refs_2_.refs_1_), channel_id=1, source_target_pairs={{0,1},{1,0},{2,3},{3,2},{4,5},{5,4},{6,7},{7,6},{8,9},{9,8},{10,11... | collective-permute-start | bytes 3145736 | tf_op jit(solution)/shard_map/ppermute | solution.py:37
  261.1 25.6 %collective-permute-start.21 = (bf16[1,512,2048]{2,1,0:T(8,128)(2,1)}, bf16[1,512,2048]{2,1,0:T(8,128)(2,1)S(1)}, u32[]{:S(2)}, u32[]{:S(2)}) collective-permute-start(bf16[1,512,2048]{2,1,0:T(8,128)(2,1)} %tie.23.refs_6_.refs_11_.refs_3_), channel_id=1, source_target_pairs={{0,4},{4,0},{8,12},{12,8},{1,5},{5,1},{9,13},{13,9},{2,6},{6,2},{1... | collective-permute-start | bytes 6291464 | tf_op jit(solution)/shard_map/ppermute | solution.py:25
  261.5 25.3 %collective-permute-start.19 = (bf16[256,2048]{1,0:T(8,128)(2,1)S(1)}, bf16[256,2048]{1,0:T(8,128)(2,1)S(1)}, u32[]{:S(2)}, u32[]{:S(2)}) collective-permute-start(bf16[256,2048]{1,0:T(8,128)(2,1)S(1)} %copy-done.54), channel_id=1, source_target_pairs={{0,1},{1,0},{2,3},{3,2},{4,5},{5,4},{6,7},{7,6},{8,9},{9,8},{10,11... | collective-permute-start | bytes 3145736 | tf_op jit(solution)/shard_map/ppermute | solution.py:37
  322.6 26.1 %collective-permute-start.22 = (bf16[256,2048]{1,0:T(8,128)(2,1)S(1)}, bf16[256,2048]{1,0:T(8,128)(2,1)S(1)}, u32[]{:S(2)}, u32[]{:S(2)}) collective-permute-start(bf16[256,2048]{1,0:T(8,128)(2,1)S(1)} %get-tuple-element.79.refs_6_), channel_id=1, source_target_pairs={{0,1},{1,0},{2,3},{3,2},{4,5},{5,4},{6,7},{7,6},{8,9},{9,8},{10,11... | collective-permute-start | bytes 3145736 | tf_op jit(solution)/shard_map/ppermute | solution.py:37
  322.9 66.3 %collective-permute-start.24 = (bf16[256,2048]{1,0:T(8,128)(2,1)}, bf16[256,2048]{1,0:T(8,128)(2,1)S(1)}, u32[]{:S(2)}, u32[]{:S(2)}) collective-permute-start(bf16[256,2048]{1,0:T(8,128)(2,1)} %get-tuple-element.81), channel_id=1, source_target_pairs={{0,1},{1,0},{2,3},{3,2},{4,5},{5,4},{6,7},{7,6},{8,9},{9,8},{10,11... | collective-permute-start | bytes 3145736 | tf_op jit(solution)/shard_map/ppermute | solution.py:37
  349.5 45.3 %collective-permute-start.23 = (bf16[256,2048]{1,0:T(8,128)(2,1)S(1)}, bf16[256,2048]{1,0:T(8,128)(2,1)S(1)}, u32[]{:S(2)}, u32[]{:S(2)}) collective-permute-start(bf16[256,2048]{1,0:T(8,128)(2,1)S(1)} %add_rows.4.refs_3_), channel_id=1, source_target_pairs={{0,2},{1,3},{2,0},{3,1},{4,6},{5,7},{6,4},{7,5},{8,10},{9,11},{10,... | collective-permute-start | bytes 3145736 | tf_op jit(solution)/shard_map/ppermute | solution.py:37
  401.2 43.4 %collective-permute-start.25 = (bf16[256,2048]{1,0:T(8,128)(2,1)S(1)}, bf16[256,2048]{1,0:T(8,128)(2,1)S(1)}, u32[]{:S(2)}, u32[]{:S(2)}) collective-permute-start(bf16[256,2048]{1,0:T(8,128)(2,1)S(1)} %get-tuple-element.83.refs_6_.refs_1_.refs_2_), channel_id=1, source_target_pairs={{0,2},{1,3},{2,0},{3,1},{4,6},{5,7},{6,4},{7,5},{8,10},{9,11},{10,... | collective-permute-start | bytes 3145736 | tf_op jit(solution)/shard_map/ppermute | solution.py:37
  401.2 43.9 %collective-permute-start.26 = (bf16[256,2048]{1,0:T(8,128)(2,1)S(1)}, bf16[256,2048]{1,0:T(8,128)(2,1)}, u32[]{:S(2)}, u32[]{:S(2)}) collective-permute-start(bf16[256,2048]{1,0:T(8,128)(2,1)S(1)} %get-tuple-element.83.refs_6_.refs_1_.refs_2_), channel_id=1, source_target_pairs={{0,1},{1,0},{2,3},{3,2},{4,5},{5,4},{6,7},{7,6},{8,9},{9,8},{10,11... | collective-permute-start | bytes 3145736 | tf_op jit(solution)/shard_map/ppermute | solution.py:37
  403.5 82.6 %collective-permute-start.29 = (bf16[2,1,2048,512]{3,2,1,0:T(8,128)(2,1)}, bf16[2,1,2048,512]{3,2,1,0:T(8,128)(2,1)}, u32[]{:S(2)}, u32[]{:S(2)}) collective-permute-start(bf16[2,1,2048,512]{3,2,1,0:T(8,128)(2,1)} %copy-done.57), channel_id=1, source_target_pairs={{0,4},{4,0},{8,12},{12,8},{1,5},{5,1},{9,13},{13,9},{2,6},{6,2},{1... | collective-permute-start | bytes 12582920 | tf_op jit(solution)/shard_map/ppermute | solution.py:25
  446.2 24.5 %collective-permute-start.27 = (bf16[256,2048]{1,0:T(8,128)(2,1)}, bf16[256,2048]{1,0:T(8,128)(2,1)}, u32[]{:S(2)}, u32[]{:S(2)}) collective-permute-start(bf16[256,2048]{1,0:T(8,128)(2,1)} %get-tuple-element.85.refs_1_.refs_3_.refs_4_), channel_id=1, source_target_pairs={{0,1},{1,0},{2,3},{3,2},{4,5},{5,4},{6,7},{7,6},{8,9},{9,8},{10,11... | collective-permute-start | bytes 3145736 | tf_op jit(solution)/shard_map/ppermute | solution.py:37
  486.1 46.2 %collective-permute-start.31 = (bf16[2,1,512,2048]{3,2,1,0:T(8,128)(2,1)}, bf16[2,1,512,2048]{3,2,1,0:T(8,128)(2,1)}, u32[]{:S(2)}, u32[]{:S(2)}) collective-permute-start(bf16[2,1,512,2048]{3,2,1,0:T(8,128)(2,1)} %get-tuple-element.84.refs_2_), channel_id=1, source_target_pairs={{0,4},{4,0},{8,12},{12,8},{1,5},{5,1},{9,13},{13,9},{2,6},{6,2},{1... | collective-permute-start | bytes 12582920 | tf_op jit(solution)/shard_map/ppermute | solution.py:25
  502.9 34.2 %collective-permute-start.30 = (bf16[2,2,512,512]{3,2,1,0:T(8,128)(2,1)}, bf16[2,2,512,512]{3,2,1,0:T(8,128)(2,1)}, u32[]{:S(2)}, u32[]{:S(2)}) collective-permute-start(bf16[2,2,512,512]{3,2,1,0:T(8,128)(2,1)} %get-tuple-element.95.refs_6_), channel_id=1, source_target_pairs={{0,4},{4,0},{8,12},{12,8},{1,5},{5,1},{9,13},{13,9},{2,6},{6,2},{1... | collective-permute-start | bytes 6291464 | tf_op jit(solution)/shard_map/ppermute | solution.py:25
  506.2 345.8 %all-gather.2.cloned.1.call-start = ((), (), s32[]{:S(2)}) async-start(), calls=%async_computation.2 | async-start | bytes 5242880 | tf_op jit(solution)/shard_map/all_gather | solution.py:1287
  506.3 41.3 %collective-permute-start.32 = (bf16[2,512,512]{2,1,0:T(8,128)(2,1)}, bf16[2,512,512]{2,1,0:T(8,128)(2,1)S(1)}, u32[]{:S(2)}, u32[]{:S(2)}) collective-permute-start(bf16[2,512,512]{2,1,0:T(8,128)(2,1)} %copy-done.134), channel_id=1, source_target_pairs={{0,8},{4,12},{8,0},{12,4},{1,9},{5,13},{9,1},{13,5},{2,10},{6,14},... | collective-permute-start | bytes 3145736 | tf_op jit(solution)/shard_map/ppermute | solution.py:29
  541.3 28.8 %collective-permute-start.33 = (bf16[2,512,512]{2,1,0:T(8,128)(2,1)S(1)}, bf16[2,512,512]{2,1,0:T(8,128)(2,1)S(1)}, u32[]{:S(2)}, u32[]{:S(2)}) collective-permute-start(bf16[2,512,512]{2,1,0:T(8,128)(2,1)S(1)} %get-tuple-element.99.refs_12_), channel_id=1, source_target_pairs={{0,8},{4,12},{8,0},{12,4},{1,9},{5,13},{9,1},{13,5},{2,10},{6,14},... | collective-permute-start | bytes 3145736 | tf_op jit(solution)/shard_map/ppermute | solution.py:29
  541.4 59.8 %collective-permute-start.35 = (bf16[1,2048,512]{2,1,0:T(8,128)(2,1)S(1)}, bf16[1,2048,512]{2,1,0:T(8,128)(2,1)S(1)}, u32[]{:S(2)}, u32[]{:S(2)}) collective-permute-start(bf16[1,2048,512]{2,1,0:T(8,128)(2,1)S(1)} %copy-done.37), channel_id=1, source_target_pairs={{0,16},{16,0},{1,17},{17,1},{2,18},{18,2},{3,19},{19,3},{4,20},{20... | collective-permute-start | bytes 6291464 | tf_op jit(solution)/shard_map/ppermute | solution.py:33
  599.7 53.9 %collective-permute-start.39 = (bf16[2,3,512,512]{3,2,1,0:T(8,128)(2,1)}, bf16[2,3,512,512]{3,2,1,0:T(8,128)(2,1)S(1)}, u32[]{:S(2)}, u32[]{:S(2)}) collective-permute-start(bf16[2,3,512,512]{3,2,1,0:T(8,128)(2,1)} %get-tuple-element.103.refs_4_), channel_id=1, source_target_pairs={{0,4},{4,0},{8,12},{12,8},{1,5},{5,1},{9,13},{13,9},{2,6},{6,2},{1... | collective-permute-start | bytes 9437192 | tf_op jit(solution)/shard_map/ppermute | solution.py:25
  600.0 48.0 %collective-permute-start.40 = (bf16[1,512,2048]{2,1,0:T(8,128)(2,1)}, bf16[1,512,2048]{2,1,0:T(8,128)(2,1)}, u32[]{:S(2)}, u32[]{:S(2)}) collective-permute-start(bf16[1,512,2048]{2,1,0:T(8,128)(2,1)} %sum_core.5.refs_3_), channel_id=1, source_target_pairs={{0,16},{16,0},{1,17},{17,1},{2,18},{18,2},{3,19},{19,3},{4,20},{20... | collective-permute-start | bytes 6291464 | tf_op jit(solution)/shard_map/ppermute | solution.py:33
  601.1 26.3 %collective-permute-start.34 = (bf16[256,2048]{1,0:T(8,128)(2,1)}, bf16[256,2048]{1,0:T(8,128)(2,1)}, u32[]{:S(2)}, u32[]{:S(2)}) collective-permute-start(bf16[256,2048]{1,0:T(8,128)(2,1)} %get-tuple-element.101.refs_4_), channel_id=1, source_target_pairs={{0,1},{1,0},{2,3},{3,2},{4,5},{5,4},{6,7},{7,6},{8,9},{9,8},{10,11... | collective-permute-start | bytes 3145736 | tf_op jit(solution)/shard_map/ppermute | solution.py:37
  609.7 48.6 %collective-permute-start.38 = (bf16[1,2048,512]{2,1,0:T(8,128)(2,1)S(1)}, bf16[1,2048,512]{2,1,0:T(8,128)(2,1)}, u32[]{:S(2)}, u32[]{:S(2)}) collective-permute-start(bf16[1,2048,512]{2,1,0:T(8,128)(2,1)S(1)} %sum_x.4.refs_3_), channel_id=1, source_target_pairs={{0,8},{4,12},{8,0},{12,4},{1,9},{5,13},{9,1},{13,5},{2,10},{6,14},... | collective-permute-start | bytes 6291464 | tf_op jit(solution)/shard_map/ppermute | solution.py:29
  611.5 51.3 %collective-permute-start.37 = (bf16[256,2048]{1,0:T(8,128)(2,1)}, bf16[256,2048]{1,0:T(8,128)(2,1)}, u32[]{:S(2)}, u32[]{:S(2)}) collective-permute-start(bf16[256,2048]{1,0:T(8,128)(2,1)} %copy-done.131), channel_id=1, source_target_pairs={{0,1},{1,0},{2,3},{3,2},{4,5},{5,4},{6,7},{7,6},{8,9},{9,8},{10,11... | collective-permute-start | bytes 3145736 | tf_op jit(solution)/shard_map/ppermute | solution.py:37
  630.5 46.9 %collective-permute-start.36 = (bf16[256,2048]{1,0:T(8,128)(2,1)}, bf16[256,2048]{1,0:T(8,128)(2,1)}, u32[]{:S(2)}, u32[]{:S(2)}) collective-permute-start(bf16[256,2048]{1,0:T(8,128)(2,1)} %add_rows.5.refs_4_), channel_id=1, source_target_pairs={{0,2},{1,3},{2,0},{3,1},{4,6},{5,7},{6,4},{7,5},{8,10},{9,11},{10,... | collective-permute-start | bytes 3145736 | tf_op jit(solution)/shard_map/ppermute | solution.py:37
  651.6 51.0 %collective-permute-start.43 = (bf16[1,512,2048]{2,1,0:T(8,128)(2,1)S(1)}, bf16[1,512,2048]{2,1,0:T(8,128)(2,1)}, u32[]{:S(2)}, u32[]{:S(2)}) collective-permute-start(bf16[1,512,2048]{2,1,0:T(8,128)(2,1)S(1)} %sum_x.5.refs_3_), channel_id=1, source_target_pairs={{0,8},{4,12},{8,0},{12,4},{1,9},{5,13},{9,1},{13,5},{2,10},{6,14},... | collective-permute-start | bytes 6291464 | tf_op jit(solution)/shard_map/ppermute | solution.py:29
  655.2 35.8 %collective-permute-start.44 = (bf16[3,512,512]{2,1,0:T(8,128)(2,1)S(1)}, bf16[3,512,512]{2,1,0:T(8,128)(2,1)}, u32[]{:S(2)}, u32[]{:S(2)}) collective-permute-start(bf16[3,512,512]{2,1,0:T(8,128)(2,1)S(1)} %sum_core.6.refs_3_), channel_id=1, source_target_pairs={{0,16},{16,0},{1,17},{17,1},{2,18},{18,2},{3,19},{19,3},{4,20},{20... | collective-permute-start | bytes 4718600 | tf_op jit(solution)/shard_map/ppermute | solution.py:33
  683.2 44.4 %collective-permute-start.41 = (bf16[256,2048]{1,0:T(8,128)(2,1)S(1)}, bf16[256,2048]{1,0:T(8,128)(2,1)S(1)}, u32[]{:S(2)}, u32[]{:S(2)}) collective-permute-start(bf16[256,2048]{1,0:T(8,128)(2,1)S(1)} %get-tuple-element.107.refs_4_.refs_1_), channel_id=1, source_target_pairs={{0,2},{1,3},{2,0},{3,1},{4,6},{5,7},{6,4},{7,5},{8,10},{9,11},{10,... | collective-permute-start | bytes 3145736 | tf_op jit(solution)/shard_map/ppermute | solution.py:37
  683.2 44.8 %collective-permute-start.42 = (bf16[256,2048]{1,0:T(8,128)(2,1)S(1)}, bf16[256,2048]{1,0:T(8,128)(2,1)S(1)}, u32[]{:S(2)}, u32[]{:S(2)}) collective-permute-start(bf16[256,2048]{1,0:T(8,128)(2,1)S(1)} %get-tuple-element.107.refs_4_.refs_1_), channel_id=1, source_target_pairs={{0,1},{1,0},{2,3},{3,2},{4,5},{5,4},{6,7},{7,6},{8,9},{9,8},{10,11... | collective-permute-start | bytes 3145736 | tf_op jit(solution)/shard_map/ppermute | solution.py:37
  736.2 19.7 %collective-permute-start.50 = (bf16[1,512,2048]{2,1,0:T(8,128)(2,1)S(1)}, bf16[1,512,2048]{2,1,0:T(8,128)(2,1)}, u32[]{:S(2)}, u32[]{:S(2)}) collective-permute-start(bf16[1,512,2048]{2,1,0:T(8,128)(2,1)S(1)} %copy-done.6), channel_id=1, source_target_pairs={{0,4},{4,0},{8,12},{12,8},{1,5},{5,1},{9,13},{13,9},{2,6},{6,2},{1... | collective-permute-start | bytes 6291464 | tf_op jit(solution)/shard_map/ppermute | solution.py:25
  736.7 37.7 %collective-permute-start.49 = (bf16[3,512,512]{2,1,0:T(8,128)(2,1)}, bf16[3,512,512]{2,1,0:T(8,128)(2,1)}, u32[]{:S(2)}, u32[]{:S(2)}) collective-permute-start(bf16[3,512,512]{2,1,0:T(8,128)(2,1)} %copy-done.17), channel_id=1, source_target_pairs={{0,8},{4,12},{8,0},{12,4},{1,9},{5,13},{9,1},{13,5},{2,10},{6,14},... | collective-permute-start | bytes 4718600 | tf_op jit(solution)/shard_map/ppermute | solution.py:29
  777.7 23.7 %collective-permute-start.55 = (bf16[3,512,512]{2,1,0:T(8,128)(2,1)S(1)}, bf16[3,512,512]{2,1,0:T(8,128)(2,1)}, u32[]{:S(2)}, u32[]{:S(2)}) collective-permute-start(bf16[3,512,512]{2,1,0:T(8,128)(2,1)S(1)} %sum_y.6.refs_4_.refs_1_), channel_id=1, source_target_pairs={{0,4},{4,0},{8,12},{12,8},{1,5},{5,1},{9,13},{13,9},{2,6},{6,2},{1... | collective-permute-start | bytes 4718600 | tf_op jit(solution)/shard_map/ppermute | solution.py:25
  778.7 62.0 %collective-permute-start.45 = (bf16[256,2048]{1,0:T(8,128)(2,1)S(1)}, bf16[256,2048]{1,0:T(8,128)(2,1)}, u32[]{:S(2)}, u32[]{:S(2)}) collective-permute-start(bf16[256,2048]{1,0:T(8,128)(2,1)S(1)} %copy-done.26), channel_id=1, source_target_pairs={{0,1},{1,0},{2,3},{3,2},{4,5},{5,4},{6,7},{7,6},{8,9},{9,8},{10,11... | collective-permute-start | bytes 3145736 | tf_op jit(solution)/shard_map/ppermute | solution.py:37
  792.8 18.0 %collective-permute-start.52 = (bf16[1,512,512]{2,1,0:T(8,128)(2,1)S(1)}, bf16[1,512,512]{2,1,0:T(8,128)(2,1)}, u32[]{:S(2)}, u32[]{:S(2)}) collective-permute-start(bf16[1,512,512]{2,1,0:T(8,128)(2,1)S(1)} %sum_x.7.refs_1_), channel_id=1, source_target_pairs={{0,8},{4,12},{8,0},{12,4},{1,9},{5,13},{9,1},{13,5},{2,10},{6,14},... | collective-permute-start | bytes 1572872 | tf_op jit(solution)/shard_map/ppermute | solution.py:29
  810.8 28.2 %collective-permute-start.56 = (f32[12288]{0:T(1024)S(1)}, f32[12288]{0:T(1024)S(1)}, u32[]{:S(2)}, u32[]{:S(2)}) collective-permute-start(f32[12288]{0:T(1024)S(1)} %slice.96), channel_id=1, source_target_pairs={{0,1},{1,0},{2,3},{3,2},{4,5},{5,4},{6,7},{7,6},{8,9},{9,8},{10,11... | collective-permute-start | bytes 147464 | tf_op jit(solution)/shard_map/ppermute | solution.py:37
  813.4 34.4 %collective-permute-start.58 = (bf16[1,512,512]{2,1,0:T(8,128)(2,1)S(1)}, bf16[1,512,512]{2,1,0:T(8,128)(2,1)S(1)}, u32[]{:S(2)}, u32[]{:S(2)}) collective-permute-start(bf16[1,512,512]{2,1,0:T(8,128)(2,1)S(1)} %sum_y.7.refs_5_.refs_1_), channel_id=1, source_target_pairs={{0,4},{4,0},{8,12},{12,8},{1,5},{5,1},{9,13},{13,9},{2,6},{6,2},{1... | collective-permute-start | bytes 1572872 | tf_op jit(solution)/shard_map/ppermute | solution.py:25
  (160 other events, 1121.3 us)
Sparse Core Ops, SparseCore 0:
  506.3 90.1 reduce-scatter.1
  736.2 100.9 all-gather.1

commit v4 on v3

--- a/solution.py
+++ b/solution.py
@@ -12,7 +12,7 @@
 F32 = jnp.float32
 BF16 = jnp.bfloat16
 
-ROOM = 44 * 2**20
+ROOM = 40 * 2**20
 X_SWAP = [(0, 1), (1, 0)]
 ANY = pl.BlockSpec(memory_space=pl.ANY)
 

time: 873 us -> 883 us (1.011)
  local copies, waits for them, and re-layouts: 92.7 us -> 113 us
  Pallas kernels: 278 us -> 264 us
    unnamed x295 -> x315, local copies, waits for them, and re-layouts: 87.7 us -> 108 us
    pallas_call x51, Pallas kernels: 267 us -> 254 us  [call(): pl.pallas_call(kernel, grid_spec=pltpu.PrefetchScalarGridSpec(num_scalar_...]
  transfers between devices with their start and end apart: 61 -> 61, of which waited for: 32 -> 32; matrix products, arithmetic and copies ran while one was open for 1% -> 1% of each run, Pallas kernels for 27% -> 25%
where the time goes in v4:
time: 883 us; the launch traced here: 874 us
  waiting for transfers between devices  403 us (46%)
  Pallas kernels  264 us (30%)
  local copies, waits for them, and re-layouts  113 us (13%)
  starting transfers between devices  71.7 us (8%)
  between operations  16.2 us (2%)
    ppermute x20, waiting for transfers between devices, tp_swap(): return lax.ppermute(values, 'tp', xor_pairs(lax.axis_size('tp'), bit))  284 us
    pallas_call x51, Pallas kernels, call(): pl.pallas_call(kernel, grid_spec=pltpu.PrefetchScalarGridSpec(num_scalar_...  254 us
    unnamed x315, local copies, waits for them, and re-layouts  108 us
    ppermute x10, waiting for transfers between devices, x_swap(): return lax.ppermute(values, 'fsdp', X_SWAP)  60 us
    ppermute x9, waiting for transfers between devices, y_swap(): return lax.ppermute(values, 'ctx', xor_pairs(lax.axis_size('ctx'), 2))  54.5 us
    ppermute x9, starting transfers between devices, y_swap(): return lax.ppermute(values, 'ctx', xor_pairs(lax.axis_size('ctx'), 2))  28.5 us
    ppermute x20, starting transfers between devices, tp_swap(): return lax.ppermute(values, 'tp', xor_pairs(lax.axis_size('tp'), bit))  18.2 us
  transfers between devices with their start and end apart: 61, of which 32 were waited for; matrix products, arithmetic and copies ran while one was open for 1% of the time, Pallas kernels for 25%

profile of v4, /device:TPU:0, one launch (start us, length us, event | category | flops | bytes accessed | tf_op | source)
XLA Modules:
  0.0 873.5 jit_solution(5502065576896110594)
XLA Ops:
  19.9 16.2 %collective-permute-done.refs_0_ = bf16[2,512,512]{2,1,0:T(8,128)(2,1)} collective-permute-done((bf16[2,512,512]{2,1,0:T(8,128)(2,1)S(1)}, bf16[2,512,512]{2,1,0:T(8,128)(2,1)}, u32[]{:S(2)}, u32[]{:S(2)}) %collective-permute-start) | collective-permute-done | bytes 1048608 | tf_op jit(solution)/shard_map/ppermute | solution.py:33
  39.9 5.1 project_kv.2.refs_7_.refs_2_
  46.9 4.6 project_kv.3.refs_2_.refs_0_
  78.8 5.3 attend.2
  86.6 13.3 %collective-permute-done.7.refs_0_ = bf16[2,512,512]{2,1,0:T(8,128)(2,1)S(1)} collective-permute-done((bf16[2,512,512]{2,1,0:T(8,128)(2,1)}, bf16[2,512,512]{2,1,0:T(8,128)(2,1)S(1)}, u32[]{:S(2)}, u32[]{:S(2)}) %collective-permute-start.7) | collective-permute-done | bytes 1048608 | tf_op jit(solution)/shard_map/ppermute | solution.py:29
  110.8 4.7 attend.3
  117.7 5.2 attn_out.1
  135.3 13.1 %active_grad.1.refs_3_.refs_10_ = f32[1024,2048]{1,0:T(8,128)} custom-call(s32[8]{0:T(128)S(1)} %copy-done.92, bf16[1024,2048]{1,0:T(8,128)(2,1)S(1)} %copy-done.8, bf16[1,2048,1024]{2,1,0:T(8,128)(2,1)} %bitcast.174, bf16[1,2048,512]{2,1,0:T(8,128)(2,1)} %tie.21.refs_2_.refs_3_, bf16[1,2048,1024]{2,1,0:T(8,128)(2,1)} %bitcast.175, ...), custom_call_target="tpu_custom_call" | custom-call | flops 8589934592 | bytes 16777232 | tf_op jit(solution)/shard_map/active_grad/pallas_call | solution.py:116
  148.5 6.1 collective-permute-done.12.refs_2_
  164.1 28.7 %collective-permute-done.16.refs_3_ = bf16[256,2048]{1,0:T(8,128)(2,1)} collective-permute-done((bf16[256,2048]{1,0:T(8,128)(2,1)}, bf16[256,2048]{1,0:T(8,128)(2,1)}, u32[]{:S(2)}, u32[]{:S(2)}) %collective-permute-start.16) | collective-permute-done | bytes 1048608 | tf_op jit(solution)/shard_map/ppermute | solution.py:37
  192.8 14.8 %collective-permute-done.15.refs_2_ = bf16[256,2048]{1,0:T(8,128)(2,1)} collective-permute-done((bf16[256,2048]{1,0:T(8,128)(2,1)}, bf16[256,2048]{1,0:T(8,128)(2,1)}, u32[]{:S(2)}, u32[]{:S(2)}) %collective-permute-start.15) | collective-permute-done | bytes 1048608 | tf_op jit(solution)/shard_map/ppermute | solution.py:37
  213.9 4.2 collective-permute-start.18
  218.1 42.5 %collective-permute-done.17.refs_0_ = bf16[256,2048]{1,0:T(8,128)(2,1)S(1)} collective-permute-done((bf16[256,2048]{1,0:T(8,128)(2,1)S(1)}, bf16[256,2048]{1,0:T(8,128)(2,1)S(1)}, u32[]{:S(2)}, u32[]{:S(2)}) %collective-permute-start.17) | collective-permute-done | bytes 1048608 | tf_op jit(solution)/shard_map/ppermute | solution.py:37
  263.5 25.2 %collective-permute-done.19.refs_4_ = bf16[256,2048]{1,0:T(8,128)(2,1)S(1)} collective-permute-done((bf16[256,2048]{1,0:T(8,128)(2,1)S(1)}, bf16[256,2048]{1,0:T(8,128)(2,1)S(1)}, u32[]{:S(2)}, u32[]{:S(2)}) %collective-permute-start.19) | collective-permute-done | bytes 1048608 | tf_op jit(solution)/shard_map/ppermute | solution.py:37
  291.6 18.7 %feed.1 = (f32[1,2048]{1,0:T(1,128)S(1)}, bf16[1024,2048]{1,0:T(8,128)(2,1)S(1)}, bf16[1024,2048]{1,0:T(8,128)(2,1)}) custom-call(s32[8]{0:T(128)S(1)} %copy-done.93, bf16[256,2048]{1,0:T(8,128)(2,1)S(1)} %copy-done.106, bf16[256,2048]{1,0:T(8,128)(2,1)} %get-tuple-element.75.refs_2_, bf16[256,2048]{1,0:T(8,128)(2,1)S(1)} %copy-done.65, ...), custom_call_target="tpu_custom_call" | custom-call | flops 8589934592 | bytes 25174048 | tf_op jit(solution)/shard_map/feed/pallas_call | solution.py:116
  314.5 12.7 %grad_n2.1 = (bf16[512,2048]{1,0:T(8,128)(2,1)S(1)}, bf16[256,2048]{1,0:T(8,128)(2,1)}, bf16[256,2048]{1,0:T(8,128)(2,1)S(1)}) custom-call(s32[8]{0:T(128)S(1)} %copy-done.93, bf16[1024,2048]{1,0:T(8,128)(2,1)S(1)} %copy-done.144, bf16[1,1024,2048]{2,1,0:T(8,128)(2,1)} %bitcast.171, bf16[1,512,2048]{2,1,0:T(8,128)(2,1)} %tie.23.refs_6_.refs_11_.refs_3_, ...), custom_call_target="tpu_custom_call" | custom-call | flops 8589934592 | bytes 16777240 | tf_op jit(solution)/shard_map/grad_n2/pallas_call | solution.py:116
  331.4 11.8 %feed_out.1.refs_3_.refs_0_ = bf16[2,512,2048]{2,1,0:T(8,128)(2,1)S(1)} custom-call(s32[8]{0:T(128)S(1)} %copy-done.93, bf16[1024,2048]{1,0:T(8,128)(2,1)S(1)} %copy-done.146, bf16[1,2048,1024]{2,1,0:T(8,128)(2,1)} %bitcast.176, bf16[1,2048,512]{2,1,0:T(8,128)(2,1)} %tie.21.refs_2_.refs_3_, bf16[1,2048,1024]{2,1,0:T(8,128)(2,1)} %bitcast.177, ...), custom_call_target="tpu_custom_call" | custom-call | flops 8589934592 | bytes 16777228 | tf_op jit(solution)/shard_map/feed_out/pallas_call | solution.py:116
  343.2 10.1 %collective-permute-done.22.refs_2_ = bf16[256,2048]{1,0:T(8,128)(2,1)S(1)} collective-permute-done((bf16[256,2048]{1,0:T(8,128)(2,1)S(1)}, bf16[256,2048]{1,0:T(8,128)(2,1)S(1)}, u32[]{:S(2)}, u32[]{:S(2)}) %collective-permute-start.22) | collective-permute-done | bytes 1048608 | tf_op jit(solution)/shard_map/ppermute | solution.py:37
  354.7 15.4 %grad_w_down.1 = (bf16[2,1,2048,512]{3,2,1,0:T(8,128)(2,1)S(1)}, bf16[2,1,2048,512]{3,2,1,0:T(8,128)(2,1)}) custom-call(s32[8]{0:T(128)S(1)} %copy-done.93, bf16[1024,2048]{1,0:T(8,128)(2,1)S(1)} %copy-done.146, bf16[1024,2048]{1,0:T(8,128)(2,1)} %copy-done.7, bf16[256,2048]{1,0:T(8,128)(2,1)S(1)} %add_rows.4.refs_3_), custom_call_target="tpu_custom_call" | custom-call | flops 8589934592 | bytes 8388640 | tf_op jit(solution)/shard_map/grad_w_down/pallas_call | solution.py:116
  372.1 21.8 %collective-permute-done.24.refs_3_ = bf16[256,2048]{1,0:T(8,128)(2,1)} collective-permute-done((bf16[256,2048]{1,0:T(8,128)(2,1)}, bf16[256,2048]{1,0:T(8,128)(2,1)}, u32[]{:S(2)}, u32[]{:S(2)}) %collective-permute-start.24) | collective-permute-done | bytes 1048608 | tf_op jit(solution)/shard_map/ppermute | solution.py:37
  393.9 5.6 collective-permute-done.23.refs_2_
  399.5 5.3 back_mid.1
  407.2 13.3 %grad_w_up.1 = (bf16[2,1,512,2048]{3,2,1,0:T(8,128)(2,1)S(1)}, bf16[2,1,512,2048]{3,2,1,0:T(8,128)(2,1)S(1)}) custom-call(s32[8]{0:T(128)S(1)} %copy-done.93, bf16[256,2048]{1,0:T(8,128)(2,1)S(1)} %copy-done.107, bf16[256,2048]{1,0:T(8,128)(2,1)} %get-tuple-element.75.refs_2_, bf16[256,2048]{1,0:T(8,128)(2,1)S(1)} %copy-done.66, ...), custom_call_target="tpu_custom_call" | custom-call | flops 8589934592 | bytes 8388640 | tf_op jit(solution)/shard_map/grad_w_up/pallas_call | solution.py:116
  424.6 23.7 %collective-permute-done.25.refs_0_ = bf16[256,2048]{1,0:T(8,128)(2,1)S(1)} collective-permute-done((bf16[256,2048]{1,0:T(8,128)(2,1)S(1)}, bf16[256,2048]{1,0:T(8,128)(2,1)S(1)}, u32[]{:S(2)}, u32[]{:S(2)}) %collective-permute-start.25) | collective-permute-done | bytes 1048608 | tf_op jit(solution)/shard_map/ppermute | solution.py:37
  451.6 23.0 %collective-permute-done.27.refs_4_.refs_5_ = bf16[256,2048]{1,0:T(8,128)(2,1)} collective-permute-done((bf16[256,2048]{1,0:T(8,128)(2,1)}, bf16[256,2048]{1,0:T(8,128)(2,1)}, u32[]{:S(2)}, u32[]{:S(2)}) %collective-permute-start.27) | collective-permute-done | bytes 1048608 | tf_op jit(solution)/shard_map/ppermute | solution.py:37
  478.0 5.0 heads_grad.1.refs_13_
  483.0 7.8 attend_back.2
  504.1 7.0 attend_back.3
  515.8 17.2 %collective-permute-start.32 = (bf16[2,512,512]{2,1,0:T(8,128)(2,1)}, bf16[2,512,512]{2,1,0:T(8,128)(2,1)S(1)}, u32[]{:S(2)}, u32[]{:S(2)}) collective-permute-start(bf16[2,512,512]{2,1,0:T(8,128)(2,1)} %copy-done.143), channel_id=1, source_target_pairs={{0,8},{4,12},{8,0},{12,4},{1,9},{5,13},{9,1},{13,5},{2,10},{6,14},... | collective-permute-start | bytes 3145736 | tf_op jit(solution)/shard_map/ppermute | solution.py:29
  536.3 5.4 grad_w_attn.1
  552.3 4.8 collective-permute-done.32.refs_4_
  557.1 22.5 %collective-permute-done.33.refs_5_ = bf16[2,512,512]{2,1,0:T(8,128)(2,1)S(1)} collective-permute-done((bf16[2,512,512]{2,1,0:T(8,128)(2,1)S(1)}, bf16[2,512,512]{2,1,0:T(8,128)(2,1)S(1)}, u32[]{:S(2)}, u32[]{:S(2)}) %collective-permute-start.33) | collective-permute-done | bytes 1048608 | tf_op jit(solution)/shard_map/ppermute | solution.py:29
  579.6 12.2 %back_project.1 = (bf16[2,1024,512]{2,1,0:T(8,128)(2,1)S(1)}, bf16[512,2048]{1,0:T(8,128)(2,1)S(1)}, bf16[256,2048]{1,0:T(8,128)(2,1)S(1)}, bf16[256,2048]{1,0:T(8,128)(2,1)}) custom-call(s32[8]{0:T(128)S(1)} %copy-done.94, bf16[1024,512]{1,0:T(8,128)(2,1)S(1)} %bitcast.181, f32[2,512,512]{2,1,0:T(8,128)} %copy-done.137, f32[2,512,512]{2,1,0:T(8,128)} %copy-done.139, ...), custom_call_target="tpu_custom_call" | custom-call | flops 6442450944 | bytes 16777252 | tf_op jit(solution)/shard_map/back_project/pallas_call | solution.py:116
  595.7 11.5 %grad_w_qkv.1 = (bf16[2,3,512,512]{3,2,1,0:T(8,128)(2,1)S(1)}, bf16[2,3,512,512]{3,2,1,0:T(8,128)(2,1)S(1)}) custom-call(s32[8]{0:T(128)S(1)} %copy-done.94, bf16[1024,2048]{1,0:T(8,128)(2,1)} %copy-done.4, bf16[1024,512]{1,0:T(8,128)(2,1)S(1)} %bitcast.182, bf16[2,1024,512]{2,1,0:T(8,128)(2,1)S(1)} %copy-done.132, bf16[256,2048]{1,0:T(8,128)(2,1)} %get-tuple-element.101.refs_4_), custom_call_target="tpu_custom_call" | custom-call | flops 6442450944 | bytes 7340064 | tf_op jit(solution)/shard_map/grad_w_qkv/pallas_call | solution.py:116
  619.9 16.9 %collective-permute-done.34.refs_2_ = bf16[256,2048]{1,0:T(8,128)(2,1)} collective-permute-done((bf16[256,2048]{1,0:T(8,128)(2,1)}, bf16[256,2048]{1,0:T(8,128)(2,1)}, u32[]{:S(2)}, u32[]{:S(2)}) %collective-permute-start.34) | collective-permute-done | bytes 1048608 | tf_op jit(solution)/shard_map/ppermute | solution.py:37
  639.8 17.6 %collective-permute-done.40 = bf16[1,512,2048]{2,1,0:T(8,128)(2,1)} collective-permute-done((bf16[1,512,2048]{2,1,0:T(8,128)(2,1)}, bf16[1,512,2048]{2,1,0:T(8,128)(2,1)}, u32[]{:S(2)}, u32[]{:S(2)}) %collective-permute-start.40) | collective-permute-done | bytes 2097184 | tf_op jit(solution)/shard_map/ppermute | solution.py:33
  671.5 14.9 %collective-permute-done.36.refs_2_ = bf16[256,2048]{1,0:T(8,128)(2,1)} collective-permute-done((bf16[256,2048]{1,0:T(8,128)(2,1)}, bf16[256,2048]{1,0:T(8,128)(2,1)}, u32[]{:S(2)}, u32[]{:S(2)}) %collective-permute-start.36) | collective-permute-done | bytes 1048608 | tf_op jit(solution)/shard_map/ppermute | solution.py:37
  688.0 4.2 back_in.1
  693.2 6.5 collective-permute-done.44
  703.1 5.8 collective-permute-done.43
  712.8 23.6 %collective-permute-done.41.refs_0_ = bf16[256,2048]{1,0:T(8,128)(2,1)S(1)} collective-permute-done((bf16[256,2048]{1,0:T(8,128)(2,1)S(1)}, bf16[256,2048]{1,0:T(8,128)(2,1)S(1)}, u32[]{:S(2)}, u32[]{:S(2)}) %collective-permute-start.41) | collective-permute-done | bytes 1048608 | tf_op jit(solution)/shard_map/ppermute | solution.py:37
  754.3 8.0 finish.4.refs_3_
  769.8 6.0 finish.5.refs_3_
  775.7 8.1 collective-permute-done.49
  791.5 13.4 %collective-permute-done.48 = bf16[1,512,512]{2,1,0:T(8,128)(2,1)S(1)} collective-permute-done((bf16[1,512,512]{2,1,0:T(8,128)(2,1)S(1)}, bf16[1,512,512]{2,1,0:T(8,128)(2,1)S(1)}, u32[]{:S(2)}, u32[]{:S(2)}) %collective-permute-start.48) | collective-permute-done | bytes 524320 | tf_op jit(solution)/shard_map/ppermute | solution.py:33
  815.0 6.4 finish.6.refs_1_
  826.3 22.1 %collective-permute-done.56 = f32[12288]{0:T(1024)S(1)} collective-permute-done((f32[12288]{0:T(1024)S(1)}, f32[12288]{0:T(1024)S(1)}, u32[]{:S(2)}, u32[]{:S(2)}) %collective-permute-start.56) | collective-permute-done | bytes 49184 | tf_op jit(solution)/shard_map/ppermute | solution.py:37
  861.4 4.8 copy.105
  (517 shorter events, 255.2 us)
Async XLA Ops:
  7.2 731.9 %reduce-scatter.2.cloned.1.call-start = ((), (), s32[]{:S(2)}) async-start(), calls=%async_computation.1 | async-start | bytes 5242880 | tf_op jit(solution)/shard_map/reduce_scatter | solution.py:1236
  9.9 26.3 %collective-permute-start = (bf16[2,512,512]{2,1,0:T(8,128)(2,1)S(1)}, bf16[2,512,512]{2,1,0:T(8,128)(2,1)}, u32[]{:S(2)}, u32[]{:S(2)}) collective-permute-start(bf16[2,512,512]{2,1,0:T(8,128)(2,1)S(1)} %take_half.5.refs_4_), channel_id=1, source_target_pairs={{0,16},{16,0},{1,17},{17,1},{2,18},{18,2},{3,19},{19,3},{4,20},{20... | collective-permute-start | bytes 3145736 | tf_op jit(solution)/shard_map/ppermute | solution.py:33
  38.0 18.4 %collective-permute-start.1 = (bf16[1,512,512]{2,1,0:T(8,128)(2,1)S(1)}, bf16[1,512,512]{2,1,0:T(8,128)(2,1)}, u32[]{:S(2)}, u32[]{:S(2)}) collective-permute-start(bf16[1,512,512]{2,1,0:T(8,128)(2,1)S(1)} %take_half.6.refs_7_), channel_id=1, source_target_pairs={{0,16},{16,0},{1,17},{17,1},{2,18},{18,2},{3,19},{19,3},{4,20},{20... | collective-permute-start | bytes 1572872 | tf_op jit(solution)/shard_map/ppermute | solution.py:33
  45.1 27.6 %collective-permute-start.4 = (bf16[2,512,512]{2,1,0:T(8,128)(2,1)}, bf16[2,512,512]{2,1,0:T(8,128)(2,1)}, u32[]{:S(2)}, u32[]{:S(2)}) collective-permute-start(bf16[2,512,512]{2,1,0:T(8,128)(2,1)} %project_kv.2.refs_7_.refs_2_), channel_id=1, source_target_pairs={{0,8},{4,12},{8,0},{12,4},{1,9},{5,13},{9,1},{13,5},{2,10},{6,14},... | collective-permute-start | bytes 3145736 | tf_op jit(solution)/shard_map/ppermute | solution.py:29
  58.9 18.7 %collective-permute-start.8 = (bf16[2,512,512]{2,1,0:T(8,128)(2,1)}, bf16[2,512,512]{2,1,0:T(8,128)(2,1)}, u32[]{:S(2)}, u32[]{:S(2)}) collective-permute-start(bf16[2,512,512]{2,1,0:T(8,128)(2,1)} %project_kv.2.refs_7_.refs_2_), channel_id=1, source_target_pairs={{0,4},{4,0},{8,12},{12,8},{1,5},{5,1},{9,13},{13,9},{2,6},{6,2},{1... | collective-permute-start | bytes 3145736 | tf_op jit(solution)/shard_map/ppermute | solution.py:25
  74.2 25.7 %collective-permute-start.7 = (bf16[2,512,512]{2,1,0:T(8,128)(2,1)}, bf16[2,512,512]{2,1,0:T(8,128)(2,1)S(1)}, u32[]{:S(2)}, u32[]{:S(2)}) collective-permute-start(bf16[2,512,512]{2,1,0:T(8,128)(2,1)} %tie.19.refs_10_.refs_2_), channel_id=1, source_target_pairs={{0,8},{4,12},{8,0},{12,4},{1,9},{5,13},{9,1},{13,5},{2,10},{6,14},... | collective-permute-start | bytes 3145736 | tf_op jit(solution)/shard_map/ppermute | solution.py:29
  74.8 50.5 %collective-permute-start.13 = (bf16[1,2048,512]{2,1,0:T(8,128)(2,1)}, bf16[1,2048,512]{2,1,0:T(8,128)(2,1)}, u32[]{:S(2)}, u32[]{:S(2)}) collective-permute-start(bf16[1,2048,512]{2,1,0:T(8,128)(2,1)} %copy-done.45), channel_id=1, source_target_pairs={{0,16},{16,0},{1,17},{17,1},{2,18},{18,2},{3,19},{19,3},{4,20},{20... | collective-permute-start | bytes 6291464 | tf_op jit(solution)/shard_map/ppermute | solution.py:33
  77.5 26.2 %collective-permute-start.6 = (bf16[2,512,512]{2,1,0:T(8,128)(2,1)}, bf16[2,512,512]{2,1,0:T(8,128)(2,1)}, u32[]{:S(2)}, u32[]{:S(2)}) collective-permute-start(bf16[2,512,512]{2,1,0:T(8,128)(2,1)} %tie.19.refs_10_.refs_2_), channel_id=1, source_target_pairs={{0,4},{4,0},{8,12},{12,8},{1,5},{5,1},{9,13},{13,9},{2,6},{6,2},{1... | collective-permute-start | bytes 3145736 | tf_op jit(solution)/shard_map/ppermute | solution.py:25
  101.7 14.8 %collective-permute-start.11 = (bf16[1,512,512]{2,1,0:T(8,128)(2,1)}, bf16[1,512,512]{2,1,0:T(8,128)(2,1)}, u32[]{:S(2)}, u32[]{:S(2)}) collective-permute-start(bf16[1,512,512]{2,1,0:T(8,128)(2,1)} %tie.17.refs_1_.refs_3_.refs_6_), channel_id=1, source_target_pairs={{0,4},{4,0},{8,12},{12,8},{1,5},{5,1},{9,13},{13,9},{2,6},{6,2},{1... | collective-permute-start | bytes 1572872 | tf_op jit(solution)/shard_map/ppermute | solution.py:25
  128.6 26.0 %collective-permute-start.12 = (bf16[256,2048]{1,0:T(8,128)(2,1)S(1)}, bf16[256,2048]{1,0:T(8,128)(2,1)S(1)}, u32[]{:S(2)}, u32[]{:S(2)}) collective-permute-start(bf16[256,2048]{1,0:T(8,128)(2,1)S(1)} %copy-done.112), channel_id=1, source_target_pairs={{0,1},{1,0},{2,3},{3,2},{4,5},{5,4},{6,7},{7,6},{8,9},{9,8},{10,11... | collective-permute-start | bytes 3145736 | tf_op jit(solution)/shard_map/ppermute | solution.py:37
  134.4 58.4 %collective-permute-start.16 = (bf16[256,2048]{1,0:T(8,128)(2,1)}, bf16[256,2048]{1,0:T(8,128)(2,1)}, u32[]{:S(2)}, u32[]{:S(2)}) collective-permute-start(bf16[256,2048]{1,0:T(8,128)(2,1)} %get-tuple-element.72), channel_id=1, source_target_pairs={{0,1},{1,0},{2,3},{3,2},{4,5},{5,4},{6,7},{7,6},{8,9},{9,8},{10,11... | collective-permute-start | bytes 3145736 | tf_op jit(solution)/shard_map/ppermute | solution.py:37
  159.8 47.8 %collective-permute-start.15 = (bf16[256,2048]{1,0:T(8,128)(2,1)}, bf16[256,2048]{1,0:T(8,128)(2,1)}, u32[]{:S(2)}, u32[]{:S(2)}) collective-permute-start(bf16[256,2048]{1,0:T(8,128)(2,1)} %add_rows.3.refs_8_), channel_id=1, source_target_pairs={{0,2},{1,3},{2,0},{3,1},{4,6},{5,7},{6,4},{7,5},{8,10},{9,11},{10,... | collective-permute-start | bytes 3145736 | tf_op jit(solution)/shard_map/ppermute | solution.py:37
  162.4 99.9 %collective-permute-start.20 = (bf16[1,512,2048]{2,1,0:T(8,128)(2,1)}, bf16[1,512,2048]{2,1,0:T(8,128)(2,1)}, u32[]{:S(2)}, u32[]{:S(2)}) collective-permute-start(bf16[1,512,2048]{2,1,0:T(8,128)(2,1)} %take_half.9.refs_6_), channel_id=1, source_target_pairs={{0,16},{16,0},{1,17},{17,1},{2,18},{18,2},{3,19},{19,3},{4,20},{20... | collective-permute-start | bytes 6291464 | tf_op jit(solution)/shard_map/ppermute | solution.py:33
  213.9 46.7 %collective-permute-start.17 = (bf16[256,2048]{1,0:T(8,128)(2,1)S(1)}, bf16[256,2048]{1,0:T(8,128)(2,1)S(1)}, u32[]{:S(2)}, u32[]{:S(2)}) collective-permute-start(bf16[256,2048]{1,0:T(8,128)(2,1)S(1)} %get-tuple-element.74.refs_2_.refs_1_), channel_id=1, source_target_pairs={{0,2},{1,3},{2,0},{3,1},{4,6},{5,7},{6,4},{7,5},{8,10},{9,11},{10,... | collective-permute-start | bytes 3145736 | tf_op jit(solution)/shard_map/ppermute | solution.py:37
  213.9 46.8 %collective-permute-start.18 = (bf16[256,2048]{1,0:T(8,128)(2,1)S(1)}, bf16[256,2048]{1,0:T(8,128)(2,1)}, u32[]{:S(2)}, u32[]{:S(2)}) collective-permute-start(bf16[256,2048]{1,0:T(8,128)(2,1)S(1)} %get-tuple-element.74.refs_2_.refs_1_), channel_id=1, source_target_pairs={{0,1},{1,0},{2,3},{3,2},{4,5},{5,4},{6,7},{7,6},{8,9},{9,8},{10,11... | collective-permute-start | bytes 3145736 | tf_op jit(solution)/shard_map/ppermute | solution.py:37
  263.1 25.6 %collective-permute-start.21 = (bf16[1,512,2048]{2,1,0:T(8,128)(2,1)}, bf16[1,512,2048]{2,1,0:T(8,128)(2,1)S(1)}, u32[]{:S(2)}, u32[]{:S(2)}) collective-permute-start(bf16[1,512,2048]{2,1,0:T(8,128)(2,1)} %tie.23.refs_6_.refs_11_.refs_3_), channel_id=1, source_target_pairs={{0,4},{4,0},{8,12},{12,8},{1,5},{5,1},{9,13},{13,9},{2,6},{6,2},{1... | collective-permute-start | bytes 6291464 | tf_op jit(solution)/shard_map/ppermute | solution.py:25
  263.5 25.3 %collective-permute-start.19 = (bf16[256,2048]{1,0:T(8,128)(2,1)S(1)}, bf16[256,2048]{1,0:T(8,128)(2,1)S(1)}, u32[]{:S(2)}, u32[]{:S(2)}) collective-permute-start(bf16[256,2048]{1,0:T(8,128)(2,1)S(1)} %copy-done.64), channel_id=1, source_target_pairs={{0,1},{1,0},{2,3},{3,2},{4,5},{5,4},{6,7},{7,6},{8,9},{9,8},{10,11... | collective-permute-start | bytes 3145736 | tf_op jit(solution)/shard_map/ppermute | solution.py:37
  327.2 26.1 %collective-permute-start.22 = (bf16[256,2048]{1,0:T(8,128)(2,1)S(1)}, bf16[256,2048]{1,0:T(8,128)(2,1)S(1)}, u32[]{:S(2)}, u32[]{:S(2)}) collective-permute-start(bf16[256,2048]{1,0:T(8,128)(2,1)S(1)} %get-tuple-element.79.refs_6_), channel_id=1, source_target_pairs={{0,1},{1,0},{2,3},{3,2},{4,5},{5,4},{6,7},{7,6},{8,9},{9,8},{10,11... | collective-permute-start | bytes 3145736 | tf_op jit(solution)/shard_map/ppermute | solution.py:37
  327.5 66.4 %collective-permute-start.24 = (bf16[256,2048]{1,0:T(8,128)(2,1)}, bf16[256,2048]{1,0:T(8,128)(2,1)}, u32[]{:S(2)}, u32[]{:S(2)}) collective-permute-start(bf16[256,2048]{1,0:T(8,128)(2,1)} %get-tuple-element.81), channel_id=1, source_target_pairs={{0,1},{1,0},{2,3},{3,2},{4,5},{5,4},{6,7},{7,6},{8,9},{9,8},{10,11... | collective-permute-start | bytes 3145736 | tf_op jit(solution)/shard_map/ppermute | solution.py:37
  354.1 45.4 %collective-permute-start.23 = (bf16[256,2048]{1,0:T(8,128)(2,1)S(1)}, bf16[256,2048]{1,0:T(8,128)(2,1)}, u32[]{:S(2)}, u32[]{:S(2)}) collective-permute-start(bf16[256,2048]{1,0:T(8,128)(2,1)S(1)} %add_rows.4.refs_3_), channel_id=1, source_target_pairs={{0,2},{1,3},{2,0},{3,1},{4,6},{5,7},{6,4},{7,5},{8,10},{9,11},{10,... | collective-permute-start | bytes 3145736 | tf_op jit(solution)/shard_map/ppermute | solution.py:37
  404.9 43.4 %collective-permute-start.25 = (bf16[256,2048]{1,0:T(8,128)(2,1)S(1)}, bf16[256,2048]{1,0:T(8,128)(2,1)S(1)}, u32[]{:S(2)}, u32[]{:S(2)}) collective-permute-start(bf16[256,2048]{1,0:T(8,128)(2,1)S(1)} %get-tuple-element.83.refs_6_.refs_1_.refs_2_), channel_id=1, source_target_pairs={{0,2},{1,3},{2,0},{3,1},{4,6},{5,7},{6,4},{7,5},{8,10},{9,11},{10,... | collective-permute-start | bytes 3145736 | tf_op jit(solution)/shard_map/ppermute | solution.py:37
  405.0 43.9 %collective-permute-start.26 = (bf16[256,2048]{1,0:T(8,128)(2,1)S(1)}, bf16[256,2048]{1,0:T(8,128)(2,1)}, u32[]{:S(2)}, u32[]{:S(2)}) collective-permute-start(bf16[256,2048]{1,0:T(8,128)(2,1)S(1)} %get-tuple-element.83.refs_6_.refs_1_.refs_2_), channel_id=1, source_target_pairs={{0,1},{1,0},{2,3},{3,2},{4,5},{5,4},{6,7},{7,6},{8,9},{9,8},{10,11... | collective-permute-start | bytes 3145736 | tf_op jit(solution)/shard_map/ppermute | solution.py:37
  407.2 84.7 %collective-permute-start.29 = (bf16[2,1,2048,512]{3,2,1,0:T(8,128)(2,1)}, bf16[2,1,2048,512]{3,2,1,0:T(8,128)(2,1)}, u32[]{:S(2)}, u32[]{:S(2)}) collective-permute-start(bf16[2,1,2048,512]{3,2,1,0:T(8,128)(2,1)} %get-tuple-element.82.refs_7_), channel_id=1, source_target_pairs={{0,4},{4,0},{8,12},{12,8},{1,5},{5,1},{9,13},{13,9},{2,6},{6,2},{1... | collective-permute-start | bytes 12582920 | tf_op jit(solution)/shard_map/ppermute | solution.py:25
  450.0 24.6 %collective-permute-start.27 = (bf16[256,2048]{1,0:T(8,128)(2,1)}, bf16[256,2048]{1,0:T(8,128)(2,1)}, u32[]{:S(2)}, u32[]{:S(2)}) collective-permute-start(bf16[256,2048]{1,0:T(8,128)(2,1)} %get-tuple-element.85.refs_1_.refs_3_.refs_4_), channel_id=1, source_target_pairs={{0,1},{1,0},{2,3},{3,2},{4,5},{5,4},{6,7},{7,6},{8,9},{9,8},{10,11... | collective-permute-start | bytes 3145736 | tf_op jit(solution)/shard_map/ppermute | solution.py:37
  491.9 50.9 %collective-permute-start.31 = (bf16[2,1,512,2048]{3,2,1,0:T(8,128)(2,1)}, bf16[2,1,512,2048]{3,2,1,0:T(8,128)(2,1)}, u32[]{:S(2)}, u32[]{:S(2)}) collective-permute-start(bf16[2,1,512,2048]{3,2,1,0:T(8,128)(2,1)} %copy-done.59), channel_id=1, source_target_pairs={{0,4},{4,0},{8,12},{12,8},{1,5},{5,1},{9,13},{13,9},{2,6},{6,2},{1... | collective-permute-start | bytes 12582920 | tf_op jit(solution)/shard_map/ppermute | solution.py:25
  512.4 33.6 %collective-permute-start.30 = (bf16[2,2,512,512]{3,2,1,0:T(8,128)(2,1)}, bf16[2,2,512,512]{3,2,1,0:T(8,128)(2,1)}, u32[]{:S(2)}, u32[]{:S(2)}) collective-permute-start(bf16[2,2,512,512]{3,2,1,0:T(8,128)(2,1)} %get-tuple-element.95.refs_6_), channel_id=1, source_target_pairs={{0,4},{4,0},{8,12},{12,8},{1,5},{5,1},{9,13},{13,9},{2,6},{6,2},{1... | collective-permute-start | bytes 6291464 | tf_op jit(solution)/shard_map/ppermute | solution.py:25
  515.7 345.7 %all-gather.2.cloned.1.call-start = ((), (), s32[]{:S(2)}) async-start(), calls=%async_computation.2 | async-start | bytes 5242880 | tf_op jit(solution)/shard_map/all_gather | solution.py:1287
  515.8 41.3 %collective-permute-start.32 = (bf16[2,512,512]{2,1,0:T(8,128)(2,1)}, bf16[2,512,512]{2,1,0:T(8,128)(2,1)S(1)}, u32[]{:S(2)}, u32[]{:S(2)}) collective-permute-start(bf16[2,512,512]{2,1,0:T(8,128)(2,1)} %copy-done.143), channel_id=1, source_target_pairs={{0,8},{4,12},{8,0},{12,4},{1,9},{5,13},{9,1},{13,5},{2,10},{6,14},... | collective-permute-start | bytes 3145736 | tf_op jit(solution)/shard_map/ppermute | solution.py:29
  550.9 28.7 %collective-permute-start.33 = (bf16[2,512,512]{2,1,0:T(8,128)(2,1)S(1)}, bf16[2,512,512]{2,1,0:T(8,128)(2,1)S(1)}, u32[]{:S(2)}, u32[]{:S(2)}) collective-permute-start(bf16[2,512,512]{2,1,0:T(8,128)(2,1)S(1)} %get-tuple-element.99.refs_12_), channel_id=1, source_target_pairs={{0,8},{4,12},{8,0},{12,4},{1,9},{5,13},{9,1},{13,5},{2,10},{6,14},... | collective-permute-start | bytes 3145736 | tf_op jit(solution)/shard_map/ppermute | solution.py:29
  551.0 59.5 %collective-permute-start.35 = (bf16[1,2048,512]{2,1,0:T(8,128)(2,1)S(1)}, bf16[1,2048,512]{2,1,0:T(8,128)(2,1)}, u32[]{:S(2)}, u32[]{:S(2)}) collective-permute-start(bf16[1,2048,512]{2,1,0:T(8,128)(2,1)S(1)} %copy-done.44), channel_id=1, source_target_pairs={{0,16},{16,0},{1,17},{17,1},{2,18},{18,2},{3,19},{19,3},{4,20},{20... | collective-permute-start | bytes 6291464 | tf_op jit(solution)/shard_map/ppermute | solution.py:33
  608.9 53.9 %collective-permute-start.39 = (bf16[2,3,512,512]{3,2,1,0:T(8,128)(2,1)}, bf16[2,3,512,512]{3,2,1,0:T(8,128)(2,1)S(1)}, u32[]{:S(2)}, u32[]{:S(2)}) collective-permute-start(bf16[2,3,512,512]{3,2,1,0:T(8,128)(2,1)} %copy-done.76), channel_id=1, source_target_pairs={{0,4},{4,0},{8,12},{12,8},{1,5},{5,1},{9,13},{13,9},{2,6},{6,2},{1... | collective-permute-start | bytes 9437192 | tf_op jit(solution)/shard_map/ppermute | solution.py:25
  609.2 48.1 %collective-permute-start.40 = (bf16[1,512,2048]{2,1,0:T(8,128)(2,1)}, bf16[1,512,2048]{2,1,0:T(8,128)(2,1)}, u32[]{:S(2)}, u32[]{:S(2)}) collective-permute-start(bf16[1,512,2048]{2,1,0:T(8,128)(2,1)} %copy-done.50), channel_id=1, source_target_pairs={{0,16},{16,0},{1,17},{17,1},{2,18},{18,2},{3,19},{19,3},{4,20},{20... | collective-permute-start | bytes 6291464 | tf_op jit(solution)/shard_map/ppermute | solution.py:33
  610.4 26.4 %collective-permute-start.34 = (bf16[256,2048]{1,0:T(8,128)(2,1)}, bf16[256,2048]{1,0:T(8,128)(2,1)}, u32[]{:S(2)}, u32[]{:S(2)}) collective-permute-start(bf16[256,2048]{1,0:T(8,128)(2,1)} %get-tuple-element.101.refs_4_), channel_id=1, source_target_pairs={{0,1},{1,0},{2,3},{3,2},{4,5},{5,4},{6,7},{7,6},{8,9},{9,8},{10,11... | collective-permute-start | bytes 3145736 | tf_op jit(solution)/shard_map/ppermute | solution.py:37
  616.1 49.1 %collective-permute-start.38 = (bf16[1,2048,512]{2,1,0:T(8,128)(2,1)S(1)}, bf16[1,2048,512]{2,1,0:T(8,128)(2,1)}, u32[]{:S(2)}, u32[]{:S(2)}) collective-permute-start(bf16[1,2048,512]{2,1,0:T(8,128)(2,1)S(1)} %sum_x.4.refs_3_), channel_id=1, source_target_pairs={{0,8},{4,12},{8,0},{12,4},{1,9},{5,13},{9,1},{13,5},{2,10},{6,14},... | collective-permute-start | bytes 6291464 | tf_op jit(solution)/shard_map/ppermute | solution.py:29
  617.8 53.7 %collective-permute-start.37 = (bf16[256,2048]{1,0:T(8,128)(2,1)}, bf16[256,2048]{1,0:T(8,128)(2,1)}, u32[]{:S(2)}, u32[]{:S(2)}) collective-permute-start(bf16[256,2048]{1,0:T(8,128)(2,1)} %copy-done.140), channel_id=1, source_target_pairs={{0,1},{1,0},{2,3},{3,2},{4,5},{5,4},{6,7},{7,6},{8,9},{9,8},{10,11... | collective-permute-start | bytes 3145736 | tf_op jit(solution)/shard_map/ppermute | solution.py:37
  639.8 46.7 %collective-permute-start.36 = (bf16[256,2048]{1,0:T(8,128)(2,1)}, bf16[256,2048]{1,0:T(8,128)(2,1)}, u32[]{:S(2)}, u32[]{:S(2)}) collective-permute-start(bf16[256,2048]{1,0:T(8,128)(2,1)} %add_rows.5.refs_4_), channel_id=1, source_target_pairs={{0,2},{1,3},{2,0},{3,1},{4,6},{5,7},{6,4},{7,5},{8,10},{9,11},{10,... | collective-permute-start | bytes 3145736 | tf_op jit(solution)/shard_map/ppermute | solution.py:37
  660.8 48.1 %collective-permute-start.43 = (bf16[1,512,2048]{2,1,0:T(8,128)(2,1)S(1)}, bf16[1,512,2048]{2,1,0:T(8,128)(2,1)}, u32[]{:S(2)}, u32[]{:S(2)}) collective-permute-start(bf16[1,512,2048]{2,1,0:T(8,128)(2,1)S(1)} %sum_x.5.refs_3_), channel_id=1, source_target_pairs={{0,8},{4,12},{8,0},{12,4},{1,9},{5,13},{9,1},{13,5},{2,10},{6,14},... | collective-permute-start | bytes 6291464 | tf_op jit(solution)/shard_map/ppermute | solution.py:29
  663.8 35.9 %collective-permute-start.44 = (bf16[3,512,512]{2,1,0:T(8,128)(2,1)S(1)}, bf16[3,512,512]{2,1,0:T(8,128)(2,1)}, u32[]{:S(2)}, u32[]{:S(2)}) collective-permute-start(bf16[3,512,512]{2,1,0:T(8,128)(2,1)S(1)} %sum_core.6.refs_3_), channel_id=1, source_target_pairs={{0,16},{16,0},{1,17},{17,1},{2,18},{18,2},{3,19},{19,3},{4,20},{20... | collective-permute-start | bytes 4718600 | tf_op jit(solution)/shard_map/ppermute | solution.py:33
  692.2 44.2 %collective-permute-start.41 = (bf16[256,2048]{1,0:T(8,128)(2,1)S(1)}, bf16[256,2048]{1,0:T(8,128)(2,1)S(1)}, u32[]{:S(2)}, u32[]{:S(2)}) collective-permute-start(bf16[256,2048]{1,0:T(8,128)(2,1)S(1)} %get-tuple-element.107.refs_4_.refs_1_), channel_id=1, source_target_pairs={{0,2},{1,3},{2,0},{3,1},{4,6},{5,7},{6,4},{7,5},{8,10},{9,11},{10,... | collective-permute-start | bytes 3145736 | tf_op jit(solution)/shard_map/ppermute | solution.py:37
  692.3 44.6 %collective-permute-start.42 = (bf16[256,2048]{1,0:T(8,128)(2,1)S(1)}, bf16[256,2048]{1,0:T(8,128)(2,1)S(1)}, u32[]{:S(2)}, u32[]{:S(2)}) collective-permute-start(bf16[256,2048]{1,0:T(8,128)(2,1)S(1)} %get-tuple-element.107.refs_4_.refs_1_), channel_id=1, source_target_pairs={{0,1},{1,0},{2,3},{3,2},{4,5},{5,4},{6,7},{7,6},{8,9},{9,8},{10,11... | collective-permute-start | bytes 3145736 | tf_op jit(solution)/shard_map/ppermute | solution.py:37
  745.1 23.7 %collective-permute-start.50 = (bf16[1,512,2048]{2,1,0:T(8,128)(2,1)S(1)}, bf16[1,512,2048]{2,1,0:T(8,128)(2,1)}, u32[]{:S(2)}, u32[]{:S(2)}) collective-permute-start(bf16[1,512,2048]{2,1,0:T(8,128)(2,1)S(1)} %copy-done.13), channel_id=1, source_target_pairs={{0,4},{4,0},{8,12},{12,8},{1,5},{5,1},{9,13},{13,9},{2,6},{6,2},{1... | collective-permute-start | bytes 6291464 | tf_op jit(solution)/shard_map/ppermute | solution.py:25
  745.6 38.2 %collective-permute-start.49 = (bf16[3,512,512]{2,1,0:T(8,128)(2,1)}, bf16[3,512,512]{2,1,0:T(8,128)(2,1)}, u32[]{:S(2)}, u32[]{:S(2)}) collective-permute-start(bf16[3,512,512]{2,1,0:T(8,128)(2,1)} %copy-done.25), channel_id=1, source_target_pairs={{0,8},{4,12},{8,0},{12,4},{1,9},{5,13},{9,1},{13,5},{2,10},{6,14},... | collective-permute-start | bytes 4718600 | tf_op jit(solution)/shard_map/ppermute | solution.py:29
  751.9 15.6 %collective-permute-start.51 = (f32[15360]{0:T(1024)S(1)}, f32[15360]{0:T(1024)S(1)}, u32[]{:S(2)}, u32[]{:S(2)}) collective-permute-start(f32[15360]{0:T(1024)S(1)} %pad_maximum_fusion.1), channel_id=1, source_target_pairs={{0,4},{4,0},{8,12},{12,8},{1,5},{5,1},{9,13},{13,9},{2,6},{6,2},{1... | collective-permute-start | bytes 184328 | tf_op jit(solution)/shard_map/ppermute | solution.py:25
  790.4 23.7 %collective-permute-start.55 = (bf16[3,512,512]{2,1,0:T(8,128)(2,1)S(1)}, bf16[3,512,512]{2,1,0:T(8,128)(2,1)}, u32[]{:S(2)}, u32[]{:S(2)}) collective-permute-start(bf16[3,512,512]{2,1,0:T(8,128)(2,1)S(1)} %sum_y.6.refs_4_.refs_1_), channel_id=1, source_target_pairs={{0,4},{4,0},{8,12},{12,8},{1,5},{5,1},{9,13},{13,9},{2,6},{6,2},{1... | collective-permute-start | bytes 4718600 | tf_op jit(solution)/shard_map/ppermute | solution.py:25
  791.5 58.6 %collective-permute-start.45 = (bf16[256,2048]{1,0:T(8,128)(2,1)S(1)}, bf16[256,2048]{1,0:T(8,128)(2,1)}, u32[]{:S(2)}, u32[]{:S(2)}) collective-permute-start(bf16[256,2048]{1,0:T(8,128)(2,1)S(1)} %copy-done.33), channel_id=1, source_target_pairs={{0,1},{1,0},{2,3},{3,2},{4,5},{5,4},{6,7},{7,6},{8,9},{9,8},{10,11... | collective-permute-start | bytes 3145736 | tf_op jit(solution)/shard_map/ppermute | solution.py:37
  805.6 18.0 %collective-permute-start.52 = (bf16[1,512,512]{2,1,0:T(8,128)(2,1)S(1)}, bf16[1,512,512]{2,1,0:T(8,128)(2,1)}, u32[]{:S(2)}, u32[]{:S(2)}) collective-permute-start(bf16[1,512,512]{2,1,0:T(8,128)(2,1)S(1)} %sum_x.7.refs_1_), channel_id=1, source_target_pairs={{0,8},{4,12},{8,0},{12,4},{1,9},{5,13},{9,1},{13,5},{2,10},{6,14},... | collective-permute-start | bytes 1572872 | tf_op jit(solution)/shard_map/ppermute | solution.py:29
  823.6 24.9 %collective-permute-start.56 = (f32[12288]{0:T(1024)S(1)}, f32[12288]{0:T(1024)S(1)}, u32[]{:S(2)}, u32[]{:S(2)}) collective-permute-start(f32[12288]{0:T(1024)S(1)} %slice.96), channel_id=1, source_target_pairs={{0,1},{1,0},{2,3},{3,2},{4,5},{5,4},{6,7},{7,6},{8,9},{9,8},{10,11... | collective-permute-start | bytes 147464 | tf_op jit(solution)/shard_map/ppermute | solution.py:37
  826.2 31.0 %collective-permute-start.58 = (bf16[1,512,512]{2,1,0:T(8,128)(2,1)S(1)}, bf16[1,512,512]{2,1,0:T(8,128)(2,1)S(1)}, u32[]{:S(2)}, u32[]{:S(2)}) collective-permute-start(bf16[1,512,512]{2,1,0:T(8,128)(2,1)S(1)} %sum_y.7.refs_5_.refs_1_), channel_id=1, source_target_pairs={{0,4},{4,0},{8,12},{12,8},{1,5},{5,1},{9,13},{13,9},{2,6},{6,2},{1... | collective-permute-start | bytes 1572872 | tf_op jit(solution)/shard_map/ppermute | solution.py:25
  (170 other events, 1203.5 us)
Sparse Core Ops, SparseCore 0:
  515.8 90.2 reduce-scatter.1
  745.1 101.4 all-gather.1
